TPU v7x, 256 devices: a whole 4x4x8 slice. The times are simulated.
256 devices in a mesh: heads: 8 (over x, core), seq: 32 (over y, z).
Axes of the slice: x: 4, y: 4, z: 8, core: 2. Of those that a mesh axis runs over, the one named last changes fastest.
Arguments:
- layer_input: bfloat16 [16384, 3072], P('seq'), may hold values from -6 to 6
- query_preact: bfloat16 [16384, 4096], P('seq', 'heads'), may hold values from -6 to 6
- key_preact: bfloat16 [16384, 4096], P('seq', 'heads'), may hold values from -6 to 6
- value_rows: bfloat16 [16384, 4096], P('seq', 'heads'), may hold values from -6 to 6
- output_grad: bfloat16 [16384, 4096], P('seq', 'heads'), may hold values from -6 to 6
- log_decay: float32 [16384, 32], P('seq', 'heads'), may hold values from -2 to 0, as said below
Outputs:
- qweight_grad: float32 [3072, 4096], P('seq', 'heads')
- kweight_grad: float32 [3072, 4096], P('seq', 'heads')
- value_grad: bfloat16 [16384, 4096], P('seq', 'heads')
Inputs may be any that keep to these rules, and one draw needn't show every extreme that they name: `log_decay`: negative at every position.
All inputs are finite; a program needn't handle non-finite values.
Results may differ from a plain program's by a relative error of at most 0.024.
Values may be sent and summed in bfloat16 or wider, within the bound.
No kernel may reach another device: no remote copies, remote signals or barrier semaphores. Data moves between devices by JAX's collectives and lax.ppermute only.
A program may use at most 128 MiB of HBM per device.

v0:
```python
import jax
import jax.numpy as jnp
from jax import lax
from jax.sharding import PartitionSpec as P

HEAD_DIM = 128
BLOCK = 512


precise = lax.Precision.HIGHEST


def silu_slope(preact):
    sigmoid = jax.nn.sigmoid(preact)
    return sigmoid * (1.0 + preact * (1.0 - sigmoid))


def decay_mask(cumulative):
    length = cumulative.shape[1]
    causal = lax.broadcasted_iota(jnp.int32, (length, length), 0) >= lax.broadcasted_iota(
        jnp.int32, (length, length), 1
    )
    spread = cumulative[:, :, None] - cumulative[:, None, :]
    return jnp.where(causal[None], jnp.exp(jnp.minimum(spread, 0.0)), 0.0)


def block_forward(carried, blocks):
    queries, key_rows, value_rows, grad_rows, decay_rows = blocks
    cumulative = jnp.cumsum(decay_rows, axis=0).T
    weights = decay_mask(cumulative)
    scores_out = (
        jnp.einsum("thd,shd->hts", grad_rows, value_rows, preferred_element_type=jnp.float32)
        * weights
    ).astype(jnp.bfloat16)
    scores_in = (
        jnp.einsum("thd,shd->hts", queries, key_rows, preferred_element_type=jnp.float32) * weights
    ).astype(jnp.bfloat16)
    grad_query = jnp.einsum(
        "hts,shd->thd", scores_out, key_rows, preferred_element_type=jnp.float32
    )
    grad_query = grad_query + jnp.exp(cumulative).T[:, :, None] * jnp.einsum(
        "thj,hij->thi", grad_rows.astype(jnp.float32), carried, precision=precise
    )
    grad_key = jnp.einsum("hts,thd->shd", scores_out, queries, preferred_element_type=jnp.float32)
    grad_value = jnp.einsum(
        "hts,thd->shd", scores_in, grad_rows, preferred_element_type=jnp.float32
    )
    final_log = cumulative[:, -1]
    to_end = jnp.exp(final_log[:, None] - cumulative).T[:, :, None]
    updated = jnp.exp(final_log)[:, None, None] * carried + jnp.einsum(
        "shi,shj->hij",
        key_rows.astype(jnp.float32) * to_end,
        value_rows.astype(jnp.float32),
        precision=precise,
    )
    return (updated, (grad_query, grad_key, grad_value))


def block_backward(carried, blocks):
    queries, key_rows, value_rows, grad_rows, decay_rows, grad_key, grad_value = blocks
    cumulative = jnp.cumsum(decay_rows, axis=0).T
    final_log = cumulative[:, -1]
    to_end = jnp.exp(final_log[:, None] - cumulative).T[:, :, None]
    key_total = grad_key + to_end * jnp.einsum(
        "thj,hij->thi", value_rows.astype(jnp.float32), carried, precision=precise
    )
    value_total = grad_value + to_end * jnp.einsum(
        "thi,hij->thj", key_rows.astype(jnp.float32), carried, precision=precise
    )
    from_start = jnp.exp(cumulative).T[:, :, None]
    updated = jnp.exp(final_log)[:, None, None] * carried + jnp.einsum(
        "thi,thj->hij",
        queries.astype(jnp.float32) * from_start,
        grad_rows.astype(jnp.float32),
        precision=precise,
    )
    return (updated, (key_total, value_total))


def prefix_weights(totals, sources, position, from_later):
    devices = totals.shape[0]
    between = jnp.arange(devices, dtype=jnp.int32)[None, :]
    if from_later:
        inside = (position < between) & (between < sources[:, None])
        valid = sources > position
    else:
        inside = (sources[:, None] < between) & (between < position)
        valid = sources < position
    log_weight = jnp.sum(jnp.where(inside[:, :, None], totals[None, :, :], 0.0), axis=1)
    return jnp.where(valid[:, None], jnp.exp(log_weight), 0.0)


def weighted_sum(pieces, totals, sources, position, from_later):
    weights = prefix_weights(totals, sources, position, from_later)
    return jnp.einsum("eh,ehij->hij", weights, pieces, precision=precise)


def make_projection(layer_input, slopes):
    return lax.dot_general(
        layer_input, slopes, (((0,), (0,)), ((), ())), preferred_element_type=jnp.float32
    )


def per_device(layer_input, query_preact, key_preact, value_rows, output_grad, log_decay):
    tokens = layer_input.shape[0]
    heads = log_decay.shape[1]
    columns = query_preact.shape[1]
    scaling = HEAD_DIM ** (-0.5)
    queries = (jax.nn.silu(query_preact.astype(jnp.float32)) * scaling).astype(jnp.bfloat16)
    key_rows = jax.nn.silu(key_preact.astype(jnp.float32)).astype(jnp.bfloat16)
    block_count = tokens // BLOCK

    def blocked(source_array):
        return source_array.reshape(block_count, BLOCK, heads, HEAD_DIM)

    inputs_all = (
        blocked(queries),
        blocked(key_rows),
        blocked(value_rows),
        blocked(output_grad),
        log_decay.reshape(block_count, BLOCK, heads),
    )
    empty_state = jnp.zeros((heads, HEAD_DIM, HEAD_DIM), jnp.float32)
    own_state, (local_query, local_key, local_value) = lax.scan(
        block_forward, empty_state, inputs_all
    )
    back_state, (local_key, local_value) = lax.scan(
        block_backward, empty_state, inputs_all + (local_key, local_value), reverse=True
    )
    device_cum = jnp.cumsum(log_decay, axis=0)
    own_total = device_cum[-1]
    position = lax.axis_index("seq")
    devices = lax.axis_size("seq")
    every_device = jnp.arange(devices, dtype=jnp.int32)
    states, totals = (
        lax.all_gather(own_state[None], "seq", axis=0, tiled=True),
        lax.all_gather(own_total[None], "seq", axis=0, tiled=True),
    )
    incoming = weighted_sum(states, totals, every_device, position, False)
    grads32 = output_grad.reshape(tokens, heads, HEAD_DIM).astype(jnp.float32)
    grad_query = local_query.reshape(tokens, heads, HEAD_DIM) + jnp.exp(device_cum)[
        :, :, None
    ] * jnp.einsum("thj,hij->thi", grads32, incoming, precision=precise)
    query_slope = (
        grad_query.reshape(tokens, columns) * scaling * silu_slope(query_preact.astype(jnp.float32))
    ).astype(jnp.bfloat16)
    later_states = lax.all_gather(back_state[None], "seq", axis=0, tiled=True)
    outgoing = weighted_sum(later_states, totals, every_device, position, True)
    to_device_end = jnp.exp(own_total[None, :] - device_cum)[:, :, None]
    values32 = value_rows.reshape(tokens, heads, HEAD_DIM).astype(jnp.float32)
    keys32 = key_rows.reshape(tokens, heads, HEAD_DIM).astype(jnp.float32)
    key_total = local_key.reshape(tokens, heads, HEAD_DIM) + to_device_end * jnp.einsum(
        "thj,hij->thi", values32, outgoing, precision=precise
    )
    value_total = local_value.reshape(tokens, heads, HEAD_DIM) + to_device_end * jnp.einsum(
        "thi,hij->thj", keys32, outgoing, precision=precise
    )
    value_grad = value_total.reshape(tokens, columns).astype(jnp.bfloat16)
    key_slope = (
        key_total.reshape(tokens, columns) * silu_slope(key_preact.astype(jnp.float32))
    ).astype(jnp.bfloat16)
    slopes = jnp.concatenate([query_slope, key_slope], axis=1)
    summed = lax.psum_scatter(
        make_projection(layer_input, slopes).astype(jnp.bfloat16),
        "seq",
        scatter_dimension=0,
        tiled=True,
    ).astype(jnp.float32)
    qweight_grad = summed[:, :columns]
    kweight_grad = summed[:, columns:]
    return (qweight_grad, kweight_grad, value_grad)


def solution(mesh):
    placed = (
        P("seq", None),
        P("seq", "heads"),
        P("seq", "heads"),
        P("seq", "heads"),
        P("seq", "heads"),
        P("seq", "heads"),
    )
    return jax.shard_map(
        per_device,
        mesh=mesh,
        in_specs=placed,
        out_specs=(P("seq", "heads"), P("seq", "heads"), P("seq", "heads")),
        check_vma=False,
    )
```

profile of v0, /device:TPU:4, one launch (start us, length us, event | category | flops | bytes accessed | tf_op | source)
XLA Modules:
  0.0 505.3 jit_solution(18152964247846208432)
XLA Ops:
  8.1 1.2 reduce-window.14
  10.0 2.2 fusion.23
  12.1 2.0 copy.144
  14.2 2.6 convolution_add_fusion.1
  17.0 42.0 %all-gather.2 = f32[32,1,4]{2,1,0:T(1,128)S(1)} all-gather(f32[1,1,4]{2,1,0:T(1,128)S(1)} %bitcast.169), channel_id=1, replica_groups=mesh['heads'=8,'seq'=32] {'seq'}, dimensions={0}, use_global_device_ids=true | all-gather | bytes 528 | tf_op jit(solution)/shard_map/all_gather | solution.py:137
  59.1 2.1 copy.185
  61.5 2.7 multiply_convert_fusion.1
  64.3 1.3 copy-done.1
  66.4 1.7 fusion.18
  68.1 50.3 %all-gather.6.cloned.1.call-done = f32[128,128,128]{2,1,0:T(8,128)} async-done(((f32[4,128,128]{2,1,0:T(8,128)}), f32[128,128,128]{2,1,0:T(8,128)}) %all-gather.6.cloned.1.call-update) | async-done | bytes 8388624 | tf_op jit(solution)/shard_map/all_gather | solution.py:136
  118.3 12.1 %fusion.2 = f32[4,1,128,128]{3,1,2,0:T(1,128)S(1)} fusion(f32[32,4,1,1]{0,2,3,1:T(1,128)S(1)} %bitcast.164, f32[32,4,128,128]{3,2,1,0:T(8,128)} %bitcast.139), kind=kOutput, calls=%fused_computation.2 | convolution fusion | flops 25165824 | bytes 8651264 | tf_op jit(solution)/shard_map/eh,ehij->hij/dot_general | solution.py:95
  130.5 1.7 fusion.16
  132.1 2.5 copy.152
  134.7 2.9 fusion.34
  137.5 2.1 copy.153
  139.6 2.6 convolution_add_fusion
  142.3 2.2 convolution_bitcast_fusion
  144.5 2.6 fusion.13
  147.1 90.8 %all-gather.8.cloned.1.call-done = f32[128,128,128]{2,1,0:T(8,128)} async-done(((f32[4,128,128]{2,1,0:T(8,128)}), f32[128,128,128]{2,1,0:T(8,128)}) %all-gather.8.cloned.1.call-update) | async-done | bytes 8388624 | tf_op jit(solution)/shard_map/all_gather | solution.py:147
  237.9 12.1 %fusion = f32[4,1,128,128]{3,1,2,0:T(1,128)S(1)} fusion(f32[32,4,1,1]{0,2,3,1:T(1,128)S(1)} %bitcast.165, f32[32,4,128,128]{3,2,1,0:T(8,128)} %bitcast.140), kind=kOutput, calls=%fused_computation | convolution fusion | flops 25165824 | bytes 8651264 | tf_op jit(solution)/shard_map/eh,ehij->hij/dot_general | solution.py:95
  250.1 1.6 fusion.11
  251.7 2.5 copy.159
  254.3 1.8 fusion.27
  256.1 6.5 %convert_bitcast_fusion = bf16[3072,1024]{0,1:T(8,128)(2,1)} fusion(bf16[512,3072]{1,0:T(8,128)(2,1)S(1)} %copy-done, bf16[512,512]{1,0:T(8,128)(2,1)S(1)} %fusion.27, bf16[512,512]{1,0:T(8,128)(2,1)} %get-tuple-element.86), kind=kOutput, calls=%fused_computation.4 | convolution fusion | flops 3226468352 | bytes 10485760 | tf_op jit(solution)/shard_map/dot_general | solution.py:99
  262.6 8.6 %copy.183 = bf16[3072,1024]{1,0:T(8,128)(2,1)} copy(bf16[3072,1024]{0,1:T(8,128)(2,1)} %convert_bitcast_fusion) | data formatting | bytes 12582912
  271.2 4.3 fusion.5
  275.5 2.0 fusion.9
  277.5 2.5 fusion.19
  280.0 2.1 copy.167
  282.0 211.3 %reduce-scatter.4.cloned.1.call-done = bf16[96,1024]{1,0:T(8,128)(2,1)} async-done(((bf16[3072,1024]{1,0:T(8,128)(2,1)}), bf16[96,1024]{1,0:T(8,128)(2,1)}) %reduce-scatter.4.cloned.1.call-update) | async-done | bytes 196624
  495.3 1.8 copy.166
  497.0 1.8 copy.165
  (45 shorter events, 5.0 us)
Async XLA Ops:
  7.2 248.9 %copy-start = (bf16[512,3072]{1,0:T(8,128)(2,1)S(1)}, bf16[512,3072]{1,0:T(8,128)(2,1)}, u32[]{:S(2)}) copy-start(bf16[512,3072]{1,0:T(8,128)(2,1)} %param.6) | copy-start | bytes 9437188
  7.2 111.1 %all-gather.6.cloned.1.call-start = ((), (), s32[]{:S(2)}) async-start(), calls=%async_computation.1 | async-start | bytes 8650752 | tf_op jit(solution)/shard_map/all_gather | solution.py:136
  16.8 221.2 %all-gather.8.cloned.1.call-start = ((), (), s32[]{:S(2)}) async-start(), calls=%async_computation.2 | async-start | bytes 8650752 | tf_op jit(solution)/shard_map/all_gather | solution.py:147
  61.2 4.4 copy-start.2
  61.4 4.9 copy-start.8
  61.5 4.8 copy-start.3
  64.3 1.3 copy-start.1
  118.3 12.1 %copy-start.4 = (bf16[512,512]{0,1:T(8,128)(2,1)S(1)}, bf16[512,512]{0,1:T(8,128)(2,1)}, u32[]{:S(2)}) copy-start(bf16[512,512]{0,1:T(8,128)(2,1)} %copy.185) | copy-start | bytes 1572868
  118.3 12.2 %copy-start.5 = (f32[512,4,128]{0,2,1:T(8,128)S(1)}, f32[512,4,128]{0,2,1:T(8,128)}, u32[]{:S(2)}) copy-start(f32[512,4,128]{0,2,1:T(8,128)} %fusion.18) | copy-start | bytes 3145732
  142.2 351.1 %reduce-scatter.4.cloned.1.call-start = ((), (), s32[]{:S(2)}) async-start(), calls=%async_computation.3 | async-start | bytes 6488064
  237.9 12.1 %copy-start.6 = (f32[512,4,128]{0,2,1:T(8,128)S(1)}, f32[512,4,128]{0,2,1:T(8,128)}, u32[]{:S(2)}) copy-start(f32[512,4,128]{0,2,1:T(8,128)} %fusion.13) | copy-start | bytes 3145732
  237.9 12.2 %copy-start.7 = (bf16[512,512]{1,0:T(8,128)(2,1)S(1)}, bf16[512,512]{1,0:T(8,128)(2,1)}, u32[]{:S(2)}) copy-start(bf16[512,512]{1,0:T(8,128)(2,1)} %param.9) | copy-start | bytes 1572868
Sparse Core Ops, SparseCore 0:
  16.9 101.3 all-gather.5
  142.3 95.5 all-gather.7
  271.3 221.9 reduce-scatter.3
where the time goes:
time: 506 us; the launch traced here: 505 us
  waiting for transfers between devices  352 us (70%)
  matrix products  58 us (11%)
  blocking collectives  42 us (8%)
  local copies, waits for them, and re-layouts  30.1 us (6%)
  between operations  13.9 us (3%)
  other arithmetic  8.64 us (2%)
    unnamed x4, waiting for transfers between devices  211 us
    all_gather x1, waiting for transfers between devices, per_device(): later_states = lax.all_gather(back_state[None], 'seq', axis=0, tiled=True)  90.8 us
    all_gather x1, waiting for transfers between devices, per_device(): lax.all_gather(own_state[None], 'seq', axis=0, tiled=True)  50.3 us
    all_gather x1, blocking collectives, per_device(): lax.all_gather(own_total[None], 'seq', axis=0, tiled=True)  42 us
    dot_general x2, matrix products, weighted_sum(): return jnp.einsum('eh,ehij->hij', weights, pieces, precision=precise)  24.3 us
    unnamed x24, local copies, waits for them, and re-layouts  16.6 us
  transfers between devices with their start and end apart: 3, of which 3 were waited for; matrix products, arithmetic and copies ran while one was open for 5% of the time, Pallas kernels for 0%

commit v1 on v0

v1 whole, which is shorter than its diff:
```python
import jax
import jax.numpy as jnp
import numpy as np
from jax import lax
from jax.experimental import pallas as pl
from jax.experimental.pallas import tpu as pltpu
from jax.sharding import Mesh, PartitionSpec as P

HEAD = 128
N_Y = 4
N_Z = 8
SEQ = N_Y * N_Z
CORES = 2
RANKS = CORES * SEQ
STEPS = 5
AXES = ("core", "y", "z")
MESSAGE = 48
BF16 = jnp.bfloat16
F32 = jnp.float32
VMEM = pltpu.CompilerParams(vmem_limit_bytes=48 * 2**20)


def exchange_plan(stream):
    by_z = [("z", 1, stream), ("y", 1, stream), ("z", 2, 2 * stream), ("y", 2, 0), ("z", 4, 0)]
    by_y = [("y", 1, stream), ("z", 1, stream), ("y", 2, 0), ("z", 2, 2 * stream), ("z", 4, 0)]
    return by_z, by_y


def rank_of(core, y, z):
    return (core * N_Y + y) * N_Z + z


def partner_of(kind, core, y, z):
    axis, distance, offset = kind
    if axis == "z":
        return rank_of(core, y, (((z - offset) ^ distance) + offset) % N_Z)
    return rank_of(core, (((y - offset) ^ distance) + offset) % N_Y, z)


def exchange_partners(stream):
    plan = exchange_plan(stream)
    steps = []
    for step in range(STEPS):
        partners = {}
        for core in range(CORES):
            for y in range(N_Y):
                for z in range(N_Z):
                    partners[rank_of(core, y, z)] = partner_of(plan[core][step], core, y, z)
        steps.append(partners)
    return steps


def block_order(stream):
    steps = exchange_partners(stream)
    order = {rank: [rank % SEQ] for rank in range(RANKS)}
    for partners in reversed(steps):
        order = {rank: order[rank] + order[partners[rank]] for rank in range(RANKS)}
    for rank in range(RANKS):
        assert sorted(order[rank]) == list(range(SEQ))
    return np.array([order[rank] for rank in range(RANKS)], np.int32)


PARTNERS = [exchange_partners(stream) for stream in range(2)]
ORDERS = np.stack([block_order(stream) for stream in range(2)])


def dot(a, b, contract):
    return lax.dot_general(a, b, ((contract[:1], contract[1:]), ((), ())), preferred_element_type=F32)


def split3(value):
    high = value.astype(BF16)
    rest = value - high.astype(F32)
    middle = rest.astype(BF16)
    low = (rest - middle.astype(F32)).astype(BF16)
    return high, middle, low


def states_kernel(query_ref, key_ref, value_ref, grad_ref, decay_ref, q_ref, k_ref, cum_ref, row_ref, out_ref):
    tokens, heads = decay_ref.shape
    scaling = HEAD ** (-0.5)
    x = query_ref[...].astype(F32)
    q_ref[...] = (x * jax.nn.sigmoid(x) * scaling).astype(BF16)
    x = key_ref[...].astype(F32)
    k_ref[...] = (x * jax.nn.sigmoid(x)).astype(BF16)
    rows = lax.broadcasted_iota(jnp.int32, (tokens, tokens), 0)
    columns = lax.broadcasted_iota(jnp.int32, (tokens, tokens), 1)
    lower = jnp.where(rows >= columns, 1.0, 0.0).astype(BF16)
    pieces = split3(decay_ref[...])
    cumulative = sum(dot(lower, piece, (1, 0)) for piece in pieces)
    across = sum(dot(piece, lower, (0, 1)) for piece in pieces)
    cum_ref[...] = cumulative
    row_ref[...] = across
    total = cumulative[tokens - 1 :, :]
    from_start = jnp.exp(cumulative)
    to_end = jnp.exp(total - cumulative)
    per = SEQ // (2 * heads)
    span = HEAD // per
    for head in range(heads):
        part = slice(head * HEAD, (head + 1) * HEAD)
        weighted_key = (k_ref[:, part].astype(F32) * to_end[:, head : head + 1]).astype(BF16)
        weighted_query = (q_ref[:, part].astype(F32) * from_start[:, head : head + 1]).astype(BF16)
        forward = dot(weighted_key, value_ref[:, part], (0, 0)).astype(BF16)
        backward = dot(weighted_query, grad_ref[:, part], (0, 0)).astype(BF16)
        marks = split3(jnp.broadcast_to(total[:, head : head + 1], (16, HEAD)))
        line = lax.broadcasted_iota(jnp.int32, (16, HEAD), 0)
        tail = jnp.where(line == 0, marks[0].astype(F32), jnp.where(line == 1, marks[1].astype(F32), marks[2].astype(F32)))
        tail = jnp.where(line < 3, tail, 0.0).astype(BF16)
        for direction, state in enumerate((forward, backward)):
            for piece in range(per):
                owner = (direction * heads + head) * per + piece
                out_ref[owner, :span, :] = state[piece * span : (piece + 1) * span, :]
                out_ref[owner, span:, :] = tail


def scan_kernel(place_ref, in_ref, out_ref):
    count = in_ref.shape[0]
    span = out_ref.shape[1]
    backward = place_ref[0] >= count // 2

    def step(at, carried):
        source = jnp.where(backward, count - 1 - at, at)
        out_ref[source] = carried.astype(BF16)
        message = in_ref[source].astype(F32)
        total = message[span : span + 1] + message[span + 1 : span + 2] + message[span + 2 : span + 3]
        return jnp.exp(total) * carried + message[:span]

    lax.fori_loop(0, count, step, jnp.zeros((span, HEAD), F32), unroll=4)


def silu_slope(value):
    sigmoid = jax.nn.sigmoid(value)
    return sigmoid * (1.0 + value * (1.0 - sigmoid))


def decay_weights(cum_ref, row_ref, head):
    tokens = cum_ref.shape[0]
    rows = lax.broadcasted_iota(jnp.int32, (tokens, tokens), 0)
    columns = lax.broadcasted_iota(jnp.int32, (tokens, tokens), 1)
    spread = cum_ref[:, head : head + 1] - row_ref[head : head + 1, :]
    return jnp.where(rows >= columns, jnp.exp(jnp.minimum(spread, 0.0)), 0.0)


def slopes_kernel(query_ref, key_ref, q_ref, k_ref, value_ref, grad_ref, cum_ref, row_ref, states_ref, qs_ref, ks_ref):
    tokens, heads = cum_ref.shape
    scaling = HEAD ** (-0.5)
    for head in range(heads):
        part = slice(head * HEAD, (head + 1) * HEAD)
        forward = states_ref[head * HEAD : (head + 1) * HEAD, :]
        backward = states_ref[(heads + head) * HEAD : (heads + head + 1) * HEAD, :]
        cumulative = cum_ref[:, head : head + 1]
        total = cum_ref[tokens - 1 :, head : head + 1]
        grads = grad_ref[:, part]
        values = value_ref[:, part]
        scores = (dot(grads, values, (1, 1)) * decay_weights(cum_ref, row_ref, head)).astype(BF16)
        grad_query = dot(scores, k_ref[:, part], (1, 0)) + jnp.exp(cumulative) * dot(grads, forward, (1, 1))
        qs_ref[:, part] = (grad_query * scaling * silu_slope(query_ref[:, part].astype(F32))).astype(BF16)
        grad_key = dot(scores, q_ref[:, part], (0, 0)) + jnp.exp(total - cumulative) * dot(values, backward, (1, 1))
        ks_ref[:, part] = (grad_key * silu_slope(key_ref[:, part].astype(F32))).astype(BF16)


def values_kernel(q_ref, k_ref, grad_ref, cum_ref, row_ref, states_ref, out_ref):
    tokens, heads = cum_ref.shape
    for head in range(heads):
        part = slice(head * HEAD, (head + 1) * HEAD)
        backward = states_ref[(heads + head) * HEAD : (heads + head + 1) * HEAD, :]
        cumulative = cum_ref[:, head : head + 1]
        total = cum_ref[tokens - 1 :, head : head + 1]
        keys = k_ref[:, part]
        scores = (dot(q_ref[:, part], keys, (1, 1)) * decay_weights(cum_ref, row_ref, head)).astype(BF16)
        grad_value = dot(scores, grad_ref[:, part], (0, 0)) + jnp.exp(total - cumulative) * dot(keys, backward, (1, 0))
        out_ref[:, part] = grad_value.astype(BF16)


def transpose_kernel(in_ref, out_ref):
    out_ref[...] = in_ref[...].T


def projection_kernel(order_ref, input_ref, slope_ref, out_ref, rows_ref):
    block = input_ref.shape[0] // SEQ
    blocks = out_ref.shape[0] // block
    for at in range(blocks):
        start = pl.multiple_of(order_ref[at] * block, block)
        rows_ref[at * block : (at + 1) * block, :] = input_ref[pl.ds(start, block), :]
    out_ref[...] = dot(rows_ref[...], slope_ref[...], (1, 0)).astype(out_ref.dtype)


def add_kernel(received_ref, kept_ref, keep_ref, send_ref):
    half = keep_ref.shape[0]
    keep_ref[...] = kept_ref[:half] + received_ref[:half].astype(F32)
    send_ref[...] = (kept_ref[half:] + received_ref[half:].astype(F32)).astype(BF16)


def last_add_kernel(received_ref, kept_ref, out_ref):
    out_ref[...] = kept_ref[...] + received_ref[...].astype(F32)


def shaped(shape, dtype):
    return jax.ShapeDtypeStruct(shape, dtype)


def cost(flops, moved):
    return pl.CostEstimate(flops=flops, bytes_accessed=moved, transcendentals=0)


def transposed(array):
    tokens, width = array.shape
    chunk = 384
    return pl.pallas_call(
        transpose_kernel,
        grid=(width // chunk,),
        in_specs=[pl.BlockSpec((tokens, chunk), lambda i: (0, i))],
        out_specs=pl.BlockSpec((chunk, tokens), lambda i: (i, 0)),
        out_shape=shaped((width, tokens), array.dtype),
        compiler_params=VMEM,
    )(array)


def projected(order, rows, slopes, dtype):
    width, tokens = rows.shape
    blocks = order.shape[0]
    taken = width // SEQ * blocks
    columns = slopes.shape[1]
    return pl.pallas_call(
        projection_kernel,
        in_specs=[pl.BlockSpec(memory_space=pltpu.SMEM)] + [pl.BlockSpec(memory_space=pltpu.VMEM)] * 2,
        out_specs=pl.BlockSpec(memory_space=pltpu.VMEM),
        out_shape=shaped((taken, columns), dtype),
        scratch_shapes=[pltpu.VMEM((taken, tokens), BF16)],
        compiler_params=VMEM,
        cost_estimate=cost(2 * taken * columns * tokens, 4 * taken * columns),
    )(order, rows, slopes)


def merged(received, kept):
    rows, columns = kept.shape
    half = rows // 2
    return pl.pallas_call(
        add_kernel,
        out_shape=(shaped((half, columns), F32), shaped((half, columns), BF16)),
        compiler_params=VMEM,
        cost_estimate=cost(rows * columns, 8 * rows * columns),
    )(received, kept)


def last_merged(received, kept):
    return pl.pallas_call(last_add_kernel, out_shape=shaped(kept.shape, F32), compiler_params=VMEM)(received, kept)


def per_device(layer_input, query_preact, key_preact, value_rows, output_grad, log_decay):
    tokens, heads = log_decay.shape
    columns = query_preact.shape[1]
    core, y, z = (lax.axis_index(axis) for axis in AXES)
    place = y * N_Z + z
    orders = jnp.asarray(ORDERS)[:, core * SEQ + place]
    half = SEQ // 2
    turned = transposed(layer_input)
    queries, key_rows, cumulative, across, states = pl.pallas_call(
        states_kernel,
        out_shape=(
            shaped((tokens, columns), BF16),
            shaped((tokens, columns), BF16),
            shaped((tokens, heads), F32),
            shaped((heads, tokens), F32),
            shaped((SEQ, MESSAGE, HEAD), BF16),
        ),
        compiler_params=VMEM,
    )(query_preact, key_preact, value_rows, output_grad, log_decay)
    states = lax.all_to_all(states, ("y", "z"), 0, 0, tiled=True)
    span = 2 * heads * HEAD // SEQ
    incoming = pl.pallas_call(
        scan_kernel,
        in_specs=[pl.BlockSpec(memory_space=pltpu.SMEM), pl.BlockSpec(memory_space=pltpu.VMEM)],
        out_specs=pl.BlockSpec(memory_space=pltpu.VMEM),
        out_shape=shaped((SEQ, span, HEAD), BF16),
        compiler_params=VMEM,
    )(place[None].astype(jnp.int32), states)
    incoming = lax.all_to_all(incoming, ("y", "z"), 0, 0, tiled=True).reshape(2 * heads * HEAD, HEAD)
    slopes = pl.pallas_call(
        slopes_kernel,
        out_shape=(shaped((tokens, columns), BF16), shaped((tokens, columns), BF16)),
        compiler_params=VMEM,
    )(query_preact, key_preact, queries, key_rows, value_rows, output_grad, cumulative, across, incoming)
    sends = [projected(orders[stream, half:], turned, slopes[stream], BF16) for stream in range(2)]
    keeps = [projected(orders[stream, :half], turned, slopes[stream], F32) for stream in range(2)]
    for step in range(STEPS):
        received = [
            lax.ppermute(sends[stream], AXES, sorted(PARTNERS[stream][step].items())) for stream in range(2)
        ]
        if step < STEPS - 1:
            pairs = [merged(received[stream], keeps[stream]) for stream in range(2)]
            keeps, sends = [pair[0] for pair in pairs], [pair[1] for pair in pairs]
        else:
            keeps = [last_merged(received[stream], keeps[stream]) for stream in range(2)]
    value_grad = pl.pallas_call(
        values_kernel,
        out_shape=shaped((tokens, columns), BF16),
        compiler_params=VMEM,
        cost_estimate=cost(2 * 3 * tokens * tokens * columns, 8 * tokens * columns),
    )(queries, key_rows, output_grad, cumulative, across, incoming)
    return keeps[0], keeps[1], value_grad


def solution(mesh):
    chips = mesh.devices.shape[0] // CORES
    split = Mesh(mesh.devices.reshape(chips, CORES, N_Y, N_Z), ("x",) + AXES)
    seq, cores = ("y", "z"), ("x", "core")
    both = P(seq, cores)
    return jax.shard_map(
        per_device,
        mesh=split,
        in_specs=(P(seq, None), both, both, both, both, both),
        out_specs=(both, both, both),
        check_vma=False,
    )
```

time: 506 us -> 155 us (0.31)
  waiting for transfers between devices: 352 us -> 77.5 us
  matrix products: 58 us -> 0 us
  blocking collectives: 42 us -> 0 us
  Pallas kernels: 0 us -> 28.9 us
  starting transfers between devices: 0.12 us -> 28.2 us
  between operations: 13.9 us -> 0.81 us
  local copies, waits for them, and re-layouts: 30.1 us -> 18.6 us
  other arithmetic: 8.64 us -> 0 us
    unnamed x4 -> x0, waiting for transfers between devices: 211 us -> none
    all_gather x2 -> x0, waiting for transfers between devices: 141 us -> none  [the longest x1 90.8 us: per_device(): later_states = lax.all_gather(back_state[None], 'seq', axis=0, tiled=True)]
    dot_general x15 -> x0, matrix products: 58 us -> none  [the longest x2 24.3 us: weighted_sum(): return jnp.einsum('eh,ehij->hij', weights, pieces, precision=precise)]
    ppermute x0 -> x10, waiting for transfers between devices: none -> 56.9 us  [per_device(): lax.ppermute(sends[stream], AXES, sorted(PARTNERS[stream][step].items()))]
    all_gather x1 -> x0, blocking collectives: 42 us -> none  [per_device(): lax.all_gather(own_total[None], 'seq', axis=0, tiled=True)]
    pallas_call x0 -> x19, Pallas kernels: none -> 28.9 us  [the longest x4 8.78 us: projected(): pl.pallas_call(projection_kernel, in_specs=[pl.BlockSpec(memory_space=plt...]
    all_to_all x0 -> x2, waiting for transfers between devices: none -> 20.6 us  [the longest x1 14.5 us: per_device(): states = lax.all_to_all(states, ('y', 'z'), 0, 0, tiled=True)]
    all_to_all x0 -> x2, starting transfers between devices: none -> 16.6 us  [the longest x1 11.5 us: per_device(): states = lax.all_to_all(states, ('y', 'z'), 0, 0, tiled=True)]
  transfers between devices with their start and end apart: 3 -> 12, of which waited for: 3 -> 8; matrix products, arithmetic and copies ran while one was open for 5% -> 1% of each run, Pallas kernels for 0% -> 13%
where the time goes in v1:
time: 155 us; the launch traced here: 154 us
  waiting for transfers between devices  77.5 us (50%)
  Pallas kernels  28.9 us (19%)
  starting transfers between devices  28.2 us (18%)
  local copies, waits for them, and re-layouts  18.6 us (12%)
    ppermute x10, waiting for transfers between devices, per_device(): lax.ppermute(sends[stream], AXES, sorted(PARTNERS[stream][step].items()))  56.9 us
    unnamed x43, local copies, waits for them, and re-layouts  17.8 us
    all_to_all x1, waiting for transfers between devices, per_device(): states = lax.all_to_all(states, ('y', 'z'), 0, 0, tiled=True)  14.5 us
    ppermute x10, starting transfers between devices, per_device(): lax.ppermute(sends[stream], AXES, sorted(PARTNERS[stream][step].items()))  11.6 us
    all_to_all x1, starting transfers between devices, per_device(): states = lax.all_to_all(states, ('y', 'z'), 0, 0, tiled=True)  11.5 us
    pallas_call x4, Pallas kernels, projected(): pl.pallas_call(projection_kernel, in_specs=[pl.BlockSpec(memory_space=plt...  8.78 us
    all_to_all x1, waiting for transfers between devices, per_device(): lax.all_to_all(incoming, ('y', 'z'), 0, 0, tiled=True)  6.05 us
    all_to_all x1, starting transfers between devices, per_device(): lax.all_to_all(incoming, ('y', 'z'), 0, 0, tiled=True)  5.13 us
  transfers between devices with their start and end apart: 12, of which 8 were waited for; matrix products, arithmetic and copies ran while one was open for 1% of the time, Pallas kernels for 13%

profile of v1, /device:TPU:4, one launch (start us, length us, event | category | flops | bytes accessed | tf_op | source)
XLA Modules:
  0.0 154.1 jit_solution(13299919148653173030)
XLA Ops:
  2.5 1.0 copy-done.5
  3.6 1.0 copy-done.7
  5.6 2.9 %shard_map.95 = (bf16[512,512]{1,0:T(8,128)(2,1)S(1)}, bf16[512,512]{1,0:T(8,128)(2,1)S(1)}, f32[512,4]{1,0:T(8,128)S(1)}, f32[4,512]{1,0:T(4,128)S(1)}, bf16[32,48,128]{2,1,0:T(8,128)(2,1)}) custom-call(bf16[512,512]{1,0:T(8,128)(2,1)S(1)} %copy-done.3, bf16[512,512]{1,0:T(8,128)(2,1)S(1)} %copy-done.5, bf16[512,512]{1,0:T(8,128)(2,1)S(1)} %copy-done.7, ...), custom_call_target="tpu_custom_call" | custom-call | tf_op jit(solution)/shard_map/pallas_call | solution.py:258
  10.8 11.5 %all-to-all-start = ((bf16[32,48,128]{2,1,0:T(8,128)(2,1)}), bf16[32,48,128]{2,1,0:T(8,128)(2,1)S(1)}, u32[]{:S(2)}, u32[]{:S(2)}) async-start(bf16[32,48,128]{2,1,0:T(8,128)(2,1)} %get-tuple-element.30), calls=%async_computation | async-start | bytes 786432 | tf_op jit(solution)/shard_map/all_to_all | solution.py:269
  22.3 14.5 %all-to-all-done.in_ref = bf16[32,48,128]{2,1,0:T(8,128)(2,1)S(1)} async-done(((bf16[32,48,128]{2,1,0:T(8,128)(2,1)}), bf16[32,48,128]{2,1,0:T(8,128)(2,1)S(1)}, u32[]{:S(2)}, u32[]{:S(2)}) %all-to-all-start) | async-done | bytes 393248 | tf_op jit(solution)/shard_map/all_to_all | solution.py:269
  37.7 5.1 %all-to-all-start.1 = ((bf16[32,32,128]{2,1,0:T(8,128)(2,1)}), bf16[32,32,128]{2,1,0:T(8,128)(2,1)S(1)}, u32[]{:S(2)}, u32[]{:S(2)}) async-start(bf16[32,32,128]{2,1,0:T(8,128)(2,1)} %shard_map.96), calls=%async_computation.1 | async-start | bytes 524288 | tf_op jit(solution)/shard_map/all_to_all | solution.py:278
  42.9 4.9 %shard_map.94.input_ref = bf16[3072,512]{1,0:T(8,128)(2,1)S(1)} custom-call(bf16[512,3072]{1,0:T(8,128)(2,1)} %in_ref.1), custom_call_target="tpu_custom_call" | custom-call | tf_op jit(solution)/shard_map/pallas_call | solution.py:209
  48.6 6.0 %all-to-all-done.1 = bf16[32,32,128]{2,1,0:T(8,128)(2,1)S(1)} async-done(((bf16[32,32,128]{2,1,0:T(8,128)(2,1)}), bf16[32,32,128]{2,1,0:T(8,128)(2,1)S(1)}, u32[]{:S(2)}, u32[]{:S(2)}) %all-to-all-start.1) | async-done | bytes 262176 | tf_op jit(solution)/shard_map/all_to_all | solution.py:278
  54.7 1.0 copy-done.4
  55.7 1.0 copy-done.6
  61.9 2.5 %shard_map.97 = (bf16[512,512]{1,0:T(8,128)(2,1)S(1)}, bf16[512,512]{1,0:T(8,128)(2,1)S(1)}) custom-call(bf16[512,512]{1,0:T(8,128)(2,1)S(1)} %copy-done.4, bf16[512,512]{1,0:T(8,128)(2,1)S(1)} %copy-done.6, bf16[512,512]{1,0:T(8,128)(2,1)S(1)} %copy-done.13, bf16[512,512]{1,0:T(8,128)(2,1)S(1)} %copy-done.16, bf16[512,512]{1,0:T(8,128)(2,1)S(1)} %copy-done.8, ...), custom_call_target="tpu_custom_call" | custom-call | tf_op jit(solution)/shard_map/pallas_call | solution.py:279
  64.4 1.5 shard_map.105
  66.1 1.5 shard_map.98
  67.7 2.4 %collective-permute-start = (bf16[1536,512]{1,0:T(8,128)(2,1)S(1)}, bf16[1536,512]{1,0:T(8,128)(2,1)S(1)}, u32[]{:S(2)}, u32[]{:S(2)}) collective-permute-start(bf16[1536,512]{1,0:T(8,128)(2,1)S(1)} %shard_map.98), channel_id=1, source_target_pairs={{0,1},{1,0},{2,3},{3,2},{4,5},{5,4},{6,7},{7,6},{8,9},{9,8},{10,11... | collective-permute-start | bytes 4718600 | tf_op jit(solution)/shard_map/ppermute | solution.py:288
  70.1 2.9 %shard_map.106.kept_ref = f32[1536,512]{1,0:T(8,128)S(1)} custom-call(s32[16]{0:T(128)S(1)} %get-tuple-element.49.order_ref, bf16[3072,512]{1,0:T(8,128)(2,1)} %copy-done, bf16[512,512]{1,0:T(8,128)(2,1)S(1)} %get-tuple-element.40.slope_ref), custom_call_target="tpu_custom_call" | custom-call | flops 805306368 | bytes 3145728 | tf_op jit(solution)/shard_map/pallas_call | solution.py:224
  73.0 1.7 %copy-done.2 = f32[1536,512]{1,0:T(8,128)} copy-done((f32[1536,512]{1,0:T(8,128)}, f32[1536,512]{1,0:T(8,128)S(1)}, u32[]{:S(2)}) %copy-start.2) | copy-done | bytes 3145752
  74.7 13.0 %collective-permute-done.5.received_ref = bf16[1536,512]{1,0:T(8,128)(2,1)S(1)} collective-permute-done((bf16[1536,512]{1,0:T(8,128)(2,1)S(1)}, bf16[1536,512]{1,0:T(8,128)(2,1)S(1)}, u32[]{:S(2)}, u32[]{:S(2)}) %collective-permute-start.5) | collective-permute-done | bytes 1572896 | tf_op jit(solution)/shard_map/ppermute | solution.py:288
  87.6 2.3 %shard_map.107 = (f32[768,512]{1,0:T(8,128)S(1)}, bf16[768,512]{1,0:T(8,128)(2,1)S(1)}) custom-call(bf16[1536,512]{1,0:T(8,128)(2,1)S(1)} %collective-permute-done.5.received_ref, f32[1536,512]{1,0:T(8,128)} %copy-done.2), custom_call_target="tpu_custom_call" | custom-call | flops 786432 | bytes 6291456 | tf_op jit(solution)/shard_map/pallas_call | solution.py:238
  89.9 1.3 collective-permute-start.6
  91.2 2.9 %shard_map.99.kept_ref = f32[1536,512]{1,0:T(8,128)S(1)} custom-call(s32[16]{0:T(128)S(1)} %get-tuple-element.51.order_ref, bf16[3072,512]{1,0:T(8,128)(2,1)} %copy-done, bf16[512,512]{1,0:T(8,128)(2,1)S(1)} %get-tuple-element.31.slope_ref), custom_call_target="tpu_custom_call" | custom-call | flops 805306368 | bytes 3145728 | tf_op jit(solution)/shard_map/pallas_call | solution.py:224
  94.1 1.6 %copy-done.1 = f32[1536,512]{1,0:T(8,128)} copy-done((f32[1536,512]{1,0:T(8,128)}, f32[1536,512]{1,0:T(8,128)S(1)}, u32[]{:S(2)}) %copy-start.1) | copy-done | bytes 3145752
  95.8 2.3 %shard_map.100 = (f32[768,512]{1,0:T(8,128)S(1)}, bf16[768,512]{1,0:T(8,128)(2,1)S(1)}) custom-call(bf16[1536,512]{1,0:T(8,128)(2,1)S(1)} %collective-permute-done.received_ref, f32[1536,512]{1,0:T(8,128)} %copy-done.1), custom_call_target="tpu_custom_call" | custom-call | flops 786432 | bytes 6291456 | tf_op jit(solution)/shard_map/pallas_call | solution.py:238
  98.3 5.8 %collective-permute-done.6.received_ref = bf16[768,512]{1,0:T(8,128)(2,1)S(1)} collective-permute-done((bf16[768,512]{1,0:T(8,128)(2,1)S(1)}, bf16[768,512]{1,0:T(8,128)(2,1)S(1)}, u32[]{:S(2)}, u32[]{:S(2)}) %collective-permute-start.6) | collective-permute-done | bytes 786464 | tf_op jit(solution)/shard_map/ppermute | solution.py:288
  104.6 13.5 %collective-permute-done.1.received_ref = bf16[768,512]{1,0:T(8,128)(2,1)S(1)} collective-permute-done((bf16[768,512]{1,0:T(8,128)(2,1)S(1)}, bf16[768,512]{1,0:T(8,128)(2,1)S(1)}, u32[]{:S(2)}, u32[]{:S(2)}) %collective-permute-start.1) | collective-permute-done | bytes 786464 | tf_op jit(solution)/shard_map/ppermute | solution.py:288
  119.1 2.1 %collective-permute-start.8 = (bf16[192,512]{1,0:T(8,128)(2,1)S(1)}, bf16[192,512]{1,0:T(8,128)(2,1)S(1)}, u32[]{:S(2)}, u32[]{:S(2)}) collective-permute-start(bf16[192,512]{1,0:T(8,128)(2,1)S(1)} %get-tuple-element.45), channel_id=1, source_target_pairs={{0,16},{1,17},{2,18},{3,19},{4,20},{5,21},{6,22},{7,23},{8,24},{9,... | collective-permute-start | bytes 589832 | tf_op jit(solution)/shard_map/ppermute | solution.py:288
  121.2 16.2 %collective-permute-done.2.received_ref = bf16[384,512]{1,0:T(8,128)(2,1)S(1)} collective-permute-done((bf16[384,512]{1,0:T(8,128)(2,1)S(1)}, bf16[384,512]{1,0:T(8,128)(2,1)S(1)}, u32[]{:S(2)}, u32[]{:S(2)}) %collective-permute-start.2) | collective-permute-done | bytes 393248 | tf_op jit(solution)/shard_map/ppermute | solution.py:288
  137.5 1.1 collective-permute-start.3
  138.7 1.7 %collective-permute-start.9 = (bf16[96,512]{1,0:T(8,128)(2,1)S(1)}, bf16[96,512]{1,0:T(8,128)(2,1)S(1)}, u32[]{:S(2)}, u32[]{:S(2)}) collective-permute-start(bf16[96,512]{1,0:T(8,128)(2,1)S(1)} %get-tuple-element.47), channel_id=1, source_target_pairs={{0,4},{1,5},{2,6},{3,7},{4,0},{5,1},{6,2},{7,3},{8,12},{9,13},{10,... | collective-permute-start | bytes 294920 | tf_op jit(solution)/shard_map/ppermute | solution.py:288
  140.3 4.4 %collective-permute-done.3.received_ref = bf16[192,512]{1,0:T(8,128)(2,1)S(1)} collective-permute-done((bf16[192,512]{1,0:T(8,128)(2,1)S(1)}, bf16[192,512]{1,0:T(8,128)(2,1)S(1)}, u32[]{:S(2)}, u32[]{:S(2)}) %collective-permute-start.3) | collective-permute-done | bytes 196640 | tf_op jit(solution)/shard_map/ppermute | solution.py:288
  144.8 1.5 collective-permute-start.4
  146.2 2.5 %shard_map.112 = bf16[512,512]{1,0:T(8,128)(2,1)} custom-call(bf16[512,512]{1,0:T(8,128)(2,1)S(1)} %copy-done.14, bf16[512,512]{1,0:T(8,128)(2,1)S(1)} %copy-done.17, bf16[512,512]{1,0:T(8,128)(2,1)S(1)} %copy-done.11, f32[512,4]{1,0:T(8,128)S(1)} %copy-done.20, f32[4,512]{1,0:T(4,128)S(1)} %get-tuple-element.29.row_ref, bf16[1024,128]{1,0:T(8,128)(2,1)S(1)} %bitcast.13), custom_call_target="tpu_custom_call" | custom-call | flops 805306368 | bytes 2097152 | tf_op jit(solution)/shard_map/pallas_call | solution.py:295
  149.4 4.0 %collective-permute-done.4.received_ref = bf16[96,512]{1,0:T(8,128)(2,1)S(1)} collective-permute-done((bf16[96,512]{1,0:T(8,128)(2,1)S(1)}, bf16[96,512]{1,0:T(8,128)(2,1)S(1)}, u32[]{:S(2)}, u32[]{:S(2)}) %collective-permute-start.4) | collective-permute-done | bytes 98336 | tf_op jit(solution)/shard_map/ppermute | solution.py:288
  (56 shorter events, 15.5 us)
Async XLA Ops:
  1.5 1.0 copy-start.3
  2.5 1.0 copy-start.5
  3.6 1.0 copy-start.7
  4.6 1.0 copy-start.9
  8.5 0.8 copy-start.12
  9.3 0.8 copy-start.15
  10.8 26.0 %all-to-all-start = ((bf16[32,48,128]{2,1,0:T(8,128)(2,1)}), bf16[32,48,128]{2,1,0:T(8,128)(2,1)S(1)}, u32[]{:S(2)}, u32[]{:S(2)}) async-start(bf16[32,48,128]{2,1,0:T(8,128)(2,1)} %get-tuple-element.30), calls=%async_computation | async-start | bytes 786432 | tf_op jit(solution)/shard_map/all_to_all | solution.py:269
  37.7 16.9 %all-to-all-start.1 = ((bf16[32,32,128]{2,1,0:T(8,128)(2,1)}), bf16[32,32,128]{2,1,0:T(8,128)(2,1)S(1)}, u32[]{:S(2)}, u32[]{:S(2)}) async-start(bf16[32,32,128]{2,1,0:T(8,128)(2,1)} %shard_map.96), calls=%async_computation.1 | async-start | bytes 524288 | tf_op jit(solution)/shard_map/all_to_all | solution.py:278
  47.8 18.3 %copy-start = (bf16[3072,512]{1,0:T(8,128)(2,1)}, bf16[3072,512]{1,0:T(8,128)(2,1)S(1)}, u32[]{:S(2)}) copy-start(bf16[3072,512]{1,0:T(8,128)(2,1)S(1)} %shard_map.94.input_ref) | copy-start | bytes 9437188
  54.7 1.0 copy-start.4
  55.7 1.0 copy-start.6
  56.7 1.0 copy-start.8
  57.8 1.0 copy-start.10
  58.8 1.0 copy-start.13
  59.9 1.0 copy-start.16
  60.9 0.9 copy-start.19
  65.9 21.7 %collective-permute-start.5 = (bf16[1536,512]{1,0:T(8,128)(2,1)S(1)}, bf16[1536,512]{1,0:T(8,128)(2,1)S(1)}, u32[]{:S(2)}, u32[]{:S(2)}) collective-permute-start(bf16[1536,512]{1,0:T(8,128)(2,1)S(1)} %shard_map.105), channel_id=1, source_target_pairs={{0,7},{1,2},{2,1},{3,4},{4,3},{5,6},{6,5},{7,0},{8,15},{9,10},{10,... | collective-permute-start | bytes 4718600 | tf_op jit(solution)/shard_map/ppermute | solution.py:288
  67.7 28.1 %collective-permute-start = (bf16[1536,512]{1,0:T(8,128)(2,1)S(1)}, bf16[1536,512]{1,0:T(8,128)(2,1)S(1)}, u32[]{:S(2)}, u32[]{:S(2)}) collective-permute-start(bf16[1536,512]{1,0:T(8,128)(2,1)S(1)} %shard_map.98), channel_id=1, source_target_pairs={{0,1},{1,0},{2,3},{3,2},{4,5},{5,4},{6,7},{7,6},{8,9},{9,8},{10,11... | collective-permute-start | bytes 4718600 | tf_op jit(solution)/shard_map/ppermute | solution.py:288
  73.0 1.7 %copy-start.2 = (f32[1536,512]{1,0:T(8,128)}, f32[1536,512]{1,0:T(8,128)S(1)}, u32[]{:S(2)}) copy-start(f32[1536,512]{1,0:T(8,128)S(1)} %shard_map.106.kept_ref) | copy-start | bytes 9437188
  89.9 14.2 %collective-permute-start.6 = (bf16[768,512]{1,0:T(8,128)(2,1)S(1)}, bf16[768,512]{1,0:T(8,128)(2,1)S(1)}, u32[]{:S(2)}, u32[]{:S(2)}) collective-permute-start(bf16[768,512]{1,0:T(8,128)(2,1)S(1)} %get-tuple-element.41), channel_id=1, source_target_pairs={{0,24},{1,25},{2,26},{3,27},{4,28},{5,29},{6,30},{7,31},{8,16},{9,... | collective-permute-start | bytes 2359304 | tf_op jit(solution)/shard_map/ppermute | solution.py:288
  94.1 1.7 %copy-start.1 = (f32[1536,512]{1,0:T(8,128)}, f32[1536,512]{1,0:T(8,128)S(1)}, u32[]{:S(2)}) copy-start(f32[1536,512]{1,0:T(8,128)S(1)} %shard_map.99.kept_ref) | copy-start | bytes 9437188
  98.0 20.1 %collective-permute-start.1 = (bf16[768,512]{1,0:T(8,128)(2,1)S(1)}, bf16[768,512]{1,0:T(8,128)(2,1)S(1)}, u32[]{:S(2)}, u32[]{:S(2)}) collective-permute-start(bf16[768,512]{1,0:T(8,128)(2,1)S(1)} %get-tuple-element.32), channel_id=1, source_target_pairs={{0,8},{1,9},{2,10},{3,11},{4,12},{5,13},{6,14},{7,15},{8,0},{9,1},... | collective-permute-start | bytes 2359304 | tf_op jit(solution)/shard_map/ppermute | solution.py:288
  104.2 14.8 %collective-permute-start.7 = (bf16[384,512]{1,0:T(8,128)(2,1)S(1)}, bf16[384,512]{1,0:T(8,128)(2,1)S(1)}, u32[]{:S(2)}, u32[]{:S(2)}) collective-permute-start(bf16[384,512]{1,0:T(8,128)(2,1)S(1)} %get-tuple-element.43), channel_id=1, source_target_pairs={{0,6},{1,7},{2,4},{3,5},{4,2},{5,3},{6,0},{7,1},{8,14},{9,15},{10,... | collective-permute-start | bytes 1179656 | tf_op jit(solution)/shard_map/ppermute | solution.py:288
  118.3 19.1 %collective-permute-start.2 = (bf16[384,512]{1,0:T(8,128)(2,1)S(1)}, bf16[384,512]{1,0:T(8,128)(2,1)S(1)}, u32[]{:S(2)}, u32[]{:S(2)}) collective-permute-start(bf16[384,512]{1,0:T(8,128)(2,1)S(1)} %get-tuple-element.34), channel_id=1, source_target_pairs={{0,2},{1,3},{2,0},{3,1},{4,6},{5,7},{6,4},{7,5},{8,10},{9,11},{10,... | collective-permute-start | bytes 1179656 | tf_op jit(solution)/shard_map/ppermute | solution.py:288
  119.0 27.2 %copy-start.11 = (bf16[512,512]{1,0:T(8,128)(2,1)S(1)}, bf16[512,512]{1,0:T(8,128)(2,1)}, u32[]{:S(2)}) copy-start(bf16[512,512]{1,0:T(8,128)(2,1)} %grad_ref.5) | copy-start | bytes 1572868
  119.0 27.2 %copy-start.14 = (bf16[512,512]{1,0:T(8,128)(2,1)S(1)}, bf16[512,512]{1,0:T(8,128)(2,1)}, u32[]{:S(2)}) copy-start(bf16[512,512]{1,0:T(8,128)(2,1)} %copy-done.12) | copy-start | bytes 1572868
  119.0 27.2 %copy-start.17 = (bf16[512,512]{1,0:T(8,128)(2,1)S(1)}, bf16[512,512]{1,0:T(8,128)(2,1)}, u32[]{:S(2)}) copy-start(bf16[512,512]{1,0:T(8,128)(2,1)} %copy-done.15) | copy-start | bytes 1572868
  119.0 27.2 %copy-start.20 = (f32[512,4]{1,0:T(8,128)S(1)}, f32[512,4]{1,0:T(8,128)}, u32[]{:S(2)}) copy-start(f32[512,4]{1,0:T(8,128)} %copy-done.18) | copy-start | bytes 24580
  119.1 19.5 %collective-permute-start.8 = (bf16[192,512]{1,0:T(8,128)(2,1)S(1)}, bf16[192,512]{1,0:T(8,128)(2,1)S(1)}, u32[]{:S(2)}, u32[]{:S(2)}) collective-permute-start(bf16[192,512]{1,0:T(8,128)(2,1)S(1)} %get-tuple-element.45), channel_id=1, source_target_pairs={{0,16},{1,17},{2,18},{3,19},{4,20},{5,21},{6,22},{7,23},{8,24},{9,... | collective-permute-start | bytes 589832 | tf_op jit(solution)/shard_map/ppermute | solution.py:288
  137.5 7.3 %collective-permute-start.3 = (bf16[192,512]{1,0:T(8,128)(2,1)S(1)}, bf16[192,512]{1,0:T(8,128)(2,1)S(1)}, u32[]{:S(2)}, u32[]{:S(2)}) collective-permute-start(bf16[192,512]{1,0:T(8,128)(2,1)S(1)} %get-tuple-element.36), channel_id=1, source_target_pairs={{0,16},{1,17},{2,18},{3,19},{4,20},{5,21},{6,22},{7,23},{8,24},{9,... | collective-permute-start | bytes 589832 | tf_op jit(solution)/shard_map/ppermute | solution.py:288
  138.7 10.1 %collective-permute-start.9 = (bf16[96,512]{1,0:T(8,128)(2,1)S(1)}, bf16[96,512]{1,0:T(8,128)(2,1)S(1)}, u32[]{:S(2)}, u32[]{:S(2)}) collective-permute-start(bf16[96,512]{1,0:T(8,128)(2,1)S(1)} %get-tuple-element.47), channel_id=1, source_target_pairs={{0,4},{1,5},{2,6},{3,7},{4,0},{5,1},{6,2},{7,3},{8,12},{9,13},{10,... | collective-permute-start | bytes 294920 | tf_op jit(solution)/shard_map/ppermute | solution.py:288
  144.8 8.6 %collective-permute-start.4 = (bf16[96,512]{1,0:T(8,128)(2,1)S(1)}, bf16[96,512]{1,0:T(8,128)(2,1)S(1)}, u32[]{:S(2)}, u32[]{:S(2)}) collective-permute-start(bf16[96,512]{1,0:T(8,128)(2,1)S(1)} %get-tuple-element.38), channel_id=1, source_target_pairs={{0,4},{1,5},{2,6},{3,7},{4,0},{5,1},{6,2},{7,3},{8,12},{9,13},{10,... | collective-permute-start | bytes 294920 | tf_op jit(solution)/shard_map/ppermute | solution.py:288
  (1 other events, 0.7 us)

commit v2 on v1

v2 whole, which is shorter than its diff:
```python
import functools

import jax
import jax.numpy as jnp
import numpy as np
from jax import lax
from jax.experimental import pallas as pl
from jax.experimental.pallas import tpu as pltpu
from jax.sharding import Mesh, PartitionSpec as P

HEAD = 128
N_Y = 4
N_Z = 8
SEQ = N_Y * N_Z
CORES = 2
RANKS = CORES * SEQ
STEPS = 5
AXES = ("core", "y", "z")
MESSAGE = 48
BF16 = jnp.bfloat16
F32 = jnp.float32
VMEM = pltpu.CompilerParams(vmem_limit_bytes=20 * 2**20)
WIDE = pltpu.CompilerParams(vmem_limit_bytes=56 * 2**20)


def exchange_plan(stream, core):
    if stream == 0:
        return [("z", 1, core), ("y", 1, core), ("z", 2, 2 * core), ("y", 2, 0), ("z", 4, 0)]
    return [("y", 1, core), ("z", 1, core), ("y", 2, 0), ("z", 2, 2 * core), ("z", 4, 0)]


def rank_of(core, y, z):
    return (core * N_Y + y) * N_Z + z


def partner_of(kind, core, y, z):
    axis, distance, offset = kind
    if axis == "z":
        return rank_of(core, y, (((z - offset) ^ distance) + offset) % N_Z)
    return rank_of(core, (((y - offset) ^ distance) + offset) % N_Y, z)


def exchange_partners(stream):
    steps = []
    for step in range(STEPS):
        partners = {}
        for core in range(CORES):
            for y in range(N_Y):
                for z in range(N_Z):
                    partners[rank_of(core, y, z)] = partner_of(exchange_plan(stream, core)[step], core, y, z)
        steps.append(partners)
    return steps


def block_order(stream):
    steps = exchange_partners(stream)
    order = {rank: [rank % SEQ] for rank in range(RANKS)}
    for partners in reversed(steps):
        order = {rank: order[rank] + order[partners[rank]] for rank in range(RANKS)}
    for rank in range(RANKS):
        assert sorted(order[rank]) == list(range(SEQ))
    return np.array([order[rank] for rank in range(RANKS)], np.int32)


PARTNERS = [exchange_partners(stream) for stream in range(2)]
ORDERS = np.stack([block_order(stream) for stream in range(2)])


def dot(a, b, contract):
    return lax.dot_general(a, b, ((contract[:1], contract[1:]), ((), ())), preferred_element_type=F32)


def split3(value):
    high = value.astype(BF16)
    rest = value - high.astype(F32)
    middle = rest.astype(BF16)
    low = (rest - middle.astype(F32)).astype(BF16)
    return high, middle, low


def moves(sources, targets, semaphores, first=0):
    return [
        pltpu.make_async_copy(source, target, semaphores.at[first + at])
        for at, (source, target) in enumerate(zip(sources, targets))
    ]


def start_all(copies):
    for copy in copies:
        copy.start()


def prefix_sums(decay):
    tokens = decay.shape[1]
    rows = lax.broadcasted_iota(jnp.int32, (tokens, tokens), 0)
    columns = lax.broadcasted_iota(jnp.int32, (tokens, tokens), 1)
    lower = jnp.where(rows >= columns, 1.0, 0.0).astype(BF16)
    pieces = split3(decay)
    return sum(dot(lower, piece, (1, 1)) for piece in pieces), sum(dot(piece, lower, (1, 1)) for piece in pieces)


def states_kernel(
    decay_hbm, query_hbm, key_hbm, value_hbm, grad_hbm, out_ref,
    decay_ref, query_ref, key_ref, value_ref, grad_ref, semaphores,
):
    heads, tokens = decay_ref.shape
    scaling = HEAD ** (-0.5)
    copies = moves(
        (decay_hbm, key_hbm, value_hbm, query_hbm, grad_hbm),
        (decay_ref, key_ref, value_ref, query_ref, grad_ref),
        semaphores,
    )
    start_all(copies)
    copies[0].wait()
    cumulative, _ = prefix_sums(decay_ref[...])
    total = cumulative[tokens - 1 :, :]
    from_start = jnp.exp(cumulative)
    to_end = jnp.exp(total - cumulative)
    per = SEQ // (2 * heads)
    span = HEAD // per
    line = lax.broadcasted_iota(jnp.int32, (16, HEAD), 0)
    tails = []
    for head in range(heads):
        marks = split3(jnp.broadcast_to(total[:, head : head + 1], (16, HEAD)))
        tail = jnp.where(
            line == 0, marks[0].astype(F32), jnp.where(line == 1, marks[1].astype(F32), marks[2].astype(F32))
        )
        tails.append(jnp.where(line < 3, tail, 0.0).astype(BF16))

    def emit(direction, head, state):
        state = state.astype(BF16)
        for piece in range(per):
            owner = (direction * heads + head) * per + piece
            out_ref[owner, :span, :] = state[piece * span : (piece + 1) * span, :]
            out_ref[owner, span:, :] = tails[head]

    copies[1].wait()
    copies[2].wait()
    for head in range(heads):
        part = slice(head * HEAD, (head + 1) * HEAD)
        x = key_ref[:, part].astype(F32)
        keys = (x * jax.nn.sigmoid(x)).astype(BF16)
        weighted = (keys.astype(F32) * to_end[:, head : head + 1]).astype(BF16)
        emit(0, head, dot(weighted, value_ref[:, part], (0, 0)))
    copies[3].wait()
    copies[4].wait()
    for head in range(heads):
        part = slice(head * HEAD, (head + 1) * HEAD)
        x = query_ref[:, part].astype(F32)
        queries = (x * jax.nn.sigmoid(x) * scaling).astype(BF16)
        weighted = (queries.astype(F32) * from_start[:, head : head + 1]).astype(BF16)
        emit(1, head, dot(weighted, grad_ref[:, part], (0, 0)))


def scan_kernel(place_ref, in_ref, after_hbm, out_ref):
    count = in_ref.shape[0]
    span = out_ref.shape[1]
    backward = place_ref[0] >= count // 2

    def step(at, carried):
        source = jnp.where(backward, count - 1 - at, at)
        out_ref[source] = carried.astype(BF16)
        message = in_ref[source].astype(F32)
        total = message[span : span + 1] + message[span + 1 : span + 2] + message[span + 2 : span + 3]
        return jnp.exp(total) * carried + message[:span]

    lax.fori_loop(0, count, step, jnp.zeros((span, HEAD), F32), unroll=4)


def local_kernel(
    decay_hbm, query_hbm, key_hbm, value_hbm, grad_hbm,
    gq_hbm, gk_hbm, gv_hbm, sq_hbm, sk_hbm, wo_hbm, wv_hbm, wk_hbm,
    decay_ref, query_ref, key_ref, value_ref, grad_ref,
    q_ref, k_ref, gq_ref, gk_ref, gv_ref, sq_ref, sk_ref, wo_ref, wv_ref, wk_ref, cum_ref, row_ref, semaphores,
):
    heads, tokens = decay_ref.shape
    scaling = HEAD ** (-0.5)
    copies = moves(
        (decay_hbm, query_hbm, key_hbm, value_hbm, grad_hbm),
        (decay_ref, query_ref, key_ref, value_ref, grad_ref),
        semaphores,
    )
    start_all(copies)
    writes = moves(
        (gq_ref, gk_ref, gv_ref, sq_ref, sk_ref, wo_ref, wv_ref, wk_ref),
        (gq_hbm, gk_hbm, gv_hbm, sq_hbm, sk_hbm, wo_hbm, wv_hbm, wk_hbm),
        semaphores,
        len(copies),
    )
    copies[0].wait()
    cum_ref[...], row_ref[...] = prefix_sums(decay_ref[...])
    for copy in copies[1:]:
        copy.wait()
    half = tokens // 2
    rows = lax.broadcasted_iota(jnp.int32, (half, half), 0)
    columns = lax.broadcasted_iota(jnp.int32, (half, half), 1)
    causal = rows >= columns
    for head in range(heads):
        part = slice(head * HEAD, (head + 1) * HEAD)
        line = slice(head, head + 1)
        x = query_ref[:, part].astype(F32)
        sigmoid = jax.nn.sigmoid(x)
        q_ref[:, part] = (x * sigmoid * scaling).astype(BF16)
        sq_ref[:, part] = (sigmoid * (1.0 + x * (1.0 - sigmoid)) * scaling).astype(BF16)
        x = key_ref[:, part].astype(F32)
        sigmoid = jax.nn.sigmoid(x)
        keys = (x * sigmoid).astype(BF16)
        k_ref[:, part] = keys
        sk_ref[:, part] = (sigmoid * (1.0 + x * (1.0 - sigmoid))).astype(BF16)
        cumulative = cum_ref[:, line]
        to_end = jnp.exp(cum_ref[tokens - 1 :, line] - cumulative)
        wo_ref[:, part] = (jnp.exp(cumulative) * grad_ref[:, part].astype(F32)).astype(BF16)
        wv_ref[:, part] = (to_end * value_ref[:, part].astype(F32)).astype(BF16)
        wk_ref[:, part] = (to_end * keys.astype(F32)).astype(BF16)

        def diagonal(block):
            spread = cum_ref[block, line] - row_ref[line, block]
            return jnp.where(causal, jnp.exp(jnp.minimum(spread, 0.0)), 0.0)

        early, late = slice(0, half), slice(half, tokens)
        border = cum_ref[half - 1 : half, line]
        decay_first = diagonal(early)
        decay_last = diagonal(late)
        decay_rows = jnp.exp(jnp.minimum(cum_ref[late, line] - border, 0.0))
        decay_columns = jnp.exp(jnp.minimum(border - row_ref[line, early], 0.0))

        def scores(left, right):
            first = (dot(left[early, part], right[early, part], (1, 1)) * decay_first).astype(BF16)
            across = (dot(left[late, part], right[early, part], (1, 1)) * decay_rows * decay_columns).astype(BF16)
            last = (dot(left[late, part], right[late, part], (1, 1)) * decay_last).astype(BF16)
            return first, across, last

        first, across, last = scores(grad_ref, value_ref)
        gq_ref[early, part] = dot(first, k_ref[early, part], (1, 0)).astype(BF16)
        gq_ref[late, part] = (dot(across, k_ref[early, part], (1, 0)) + dot(last, k_ref[late, part], (1, 0))).astype(BF16)
        gk_ref[early, part] = (dot(first, q_ref[early, part], (0, 0)) + dot(across, q_ref[late, part], (0, 0))).astype(BF16)
        gk_ref[late, part] = dot(last, q_ref[late, part], (0, 0)).astype(BF16)
        first, across, last = scores(q_ref, k_ref)
        gv_ref[early, part] = dot(first, grad_ref[early, part], (0, 0)) + dot(across, grad_ref[late, part], (0, 0))
        gv_ref[late, part] = dot(last, grad_ref[late, part], (0, 0))
    start_all(writes)
    for copy in writes:
        copy.wait()


def heads_kernel(
    states_hbm, wo_hbm, gq_hbm, sq_hbm, wv_hbm, gk_hbm, sk_hbm,
    slopes_q_ref, slopes_k_ref,
    states_ref, wo_ref, gq_ref, sq_ref, wv_ref, gk_ref, sk_ref, semaphores,
):
    heads = wo_ref.shape[1] // HEAD
    copies = moves(
        (states_hbm, wo_hbm, gq_hbm, sq_hbm, wv_hbm, gk_hbm, sk_hbm),
        (states_ref, wo_ref, gq_ref, sq_ref, wv_ref, gk_ref, sk_ref),
        semaphores,
    )
    start_all(copies)
    for stream, (weighted, local, slope, slopes) in enumerate(
        ((wo_ref, gq_ref, sq_ref, slopes_q_ref), (wv_ref, gk_ref, sk_ref, slopes_k_ref))
    ):
        for copy in copies[1 + 3 * stream : 4 + 3 * stream] + copies[: 1 - stream]:
            copy.wait()
        for head in range(heads):
            part = slice(head * HEAD, (head + 1) * HEAD)
            state = slice((stream * heads + head) * HEAD, (stream * heads + head + 1) * HEAD)
            gradient = local[:, part].astype(F32) + dot(weighted[:, part], states_ref[state, :], (1, 1))
            slopes[:, part] = (gradient * slope[:, part].astype(F32)).astype(BF16)


def pair_kernel(
    own0_ref, rows0_ref, slopes0_ref, own1_ref, rows1_ref, slopes1_ref, keep0_ref, send0_ref, keep1_ref, send1_ref
):
    half = keep0_ref.shape[0]
    for own, rows, slopes, keep, send in (
        (own0_ref, rows0_ref, slopes0_ref, keep0_ref, send0_ref),
        (own1_ref, rows1_ref, slopes1_ref, keep1_ref, send1_ref),
    ):
        send[...] = (own[half:] + dot(rows[half:], slopes[...], (1, 0))).astype(BF16)
        keep[...] = own[:half] + dot(rows[:half], slopes[...], (1, 0))


def values_kernel(local_ref, weighted_ref, states_ref, out_ref):
    heads = out_ref.shape[1] // HEAD
    for head in range(heads):
        part = slice(head * HEAD, (head + 1) * HEAD)
        later = slice((heads + head) * HEAD, (heads + head + 1) * HEAD)
        out_ref[:, part] = (local_ref[:, part] + dot(weighted_ref[:, part], states_ref[later, :], (1, 0))).astype(BF16)


def arrange_kernel(place_ref, table_ref, input_hbm, *refs, first):
    out0_hbm, out1_hbm, input_ref, turned_ref, out0_ref, out1_ref, semaphores = refs[-7:]
    tokens, width = input_ref.shape
    block = width // SEQ
    chunk = 384
    reads = moves(
        [input_hbm.at[:, at : at + chunk] for at in range(0, width, chunk)],
        [input_ref.at[:, at : at + chunk] for at in range(0, width, chunk)],
        semaphores,
    )
    start_all(reads)
    writes = moves((out0_ref, out1_ref), (out0_hbm, out1_hbm), semaphores, len(reads))
    for at, copy in enumerate(reads):
        copy.wait()
        turned_ref[at * chunk : (at + 1) * chunk, :] = input_ref[:, at * chunk : (at + 1) * chunk].T
    for stream, target in enumerate((out0_ref, out1_ref)):
        for at in range(SEQ // 2):
            entry = (stream * RANKS + place_ref[0]) * SEQ + first + at
            start = pl.multiple_of(table_ref[entry] * block, block)
            target[at * block : (at + 1) * block, :] = turned_ref[pl.ds(start, block), :]
        writes[stream].start()
    for copy in writes:
        copy.wait()


def projection_kernel(rows_ref, slope_ref, out_ref):
    out_ref[...] = dot(rows_ref[...], slope_ref[...], (1, 0))


def add_kernel(received0_ref, kept0_ref, received1_ref, kept1_ref, keep0_ref, send0_ref, keep1_ref, send1_ref):
    half = keep0_ref.shape[0]
    for received, kept, keep, send in (
        (received0_ref, kept0_ref, keep0_ref, send0_ref),
        (received1_ref, kept1_ref, keep1_ref, send1_ref),
    ):
        keep[...] = kept[:half] + received[:half].astype(F32)
        send[...] = (kept[half:] + received[half:].astype(F32)).astype(BF16)


def join_kernel(received0_ref, kept0_ref, received1_ref, kept1_ref, keep_ref, send_ref):
    half, columns = keep_ref.shape[0], kept0_ref.shape[1]
    for stream, (received, kept) in enumerate(((received0_ref, kept0_ref), (received1_ref, kept1_ref))):
        part = slice(stream * columns, (stream + 1) * columns)
        keep_ref[:, part] = kept[:half] + received[:half].astype(F32)
        send_ref[:, part] = (kept[half:] + received[half:].astype(F32)).astype(BF16)


def last_kernel(received_ref, kept_ref, out0_ref, out1_ref):
    columns = out0_ref.shape[1]
    for stream, out in enumerate((out0_ref, out1_ref)):
        part = slice(stream * columns, (stream + 1) * columns)
        out[...] = kept_ref[:, part] + received_ref[:, part].astype(F32)


def shaped(shape, dtype):
    return jax.ShapeDtypeStruct(shape, dtype)


def cost(flops, moved):
    return pl.CostEstimate(flops=flops, bytes_accessed=moved, transcendentals=0)


IN_HBM = pl.BlockSpec(memory_space=pltpu.HBM)
IN_VMEM = pl.BlockSpec(memory_space=pltpu.VMEM)


def per_device(layer_input, query_preact, key_preact, value_rows, output_grad, log_decay):
    tokens, heads = log_decay.shape
    columns = query_preact.shape[1]
    width = layer_input.shape[1]
    core, y, z = (lax.axis_index(axis) for axis in AXES)
    place = y * N_Z + z
    half = width // 2
    small, large = shaped((tokens, columns), BF16), shaped((tokens, columns), F32)
    partial = shaped((half, columns), BF16)
    turned = shaped((half, tokens), BF16)
    decay = shaped((heads, tokens), F32)
    states_shape = shaped((2 * heads * HEAD, HEAD), BF16)
    arguments = (log_decay.T, query_preact, key_preact, value_rows, output_grad)

    def scratch(*shapes):
        return [pltpu.VMEM(one.shape, one.dtype) for one in shapes]

    def semaphores(count):
        return [pltpu.SemaphoreType.DMA((count,))]

    states = pl.pallas_call(
        states_kernel,
        in_specs=[IN_HBM] * 5,
        out_shape=shaped((SEQ, MESSAGE, HEAD), BF16),
        scratch_shapes=scratch(decay, small, small, small, small) + semaphores(5),
        compiler_params=WIDE,
        cost_estimate=cost(10**9, 4 * 10**6),
    )(*arguments)
    states = lax.all_to_all(states, ("y", "z"), 0, 0, tiled=True)
    local_shapes = (small, small, large, small, small, small, small, small)
    local_q, local_k, local_v, slope_q, slope_k, weighted_o, weighted_v, weighted_k = pl.pallas_call(
        local_kernel,
        in_specs=[IN_HBM] * 5,
        out_specs=(IN_HBM,) * 8,
        out_shape=local_shapes,
        scratch_shapes=scratch(decay, *(small,) * 6, *local_shapes, shaped((tokens, heads), F32), decay)
        + semaphores(13),
        compiler_params=WIDE,
        cost_estimate=cost(4 * 10**9, 10**7),
    )(*arguments)
    rank = (core * SEQ + place)[None].astype(jnp.int32)
    table = jnp.asarray(ORDERS.reshape(-1))
    chunks = width // 384

    def arranged(first, *after):
        return pl.pallas_call(
            functools.partial(arrange_kernel, first=first),
            in_specs=[pl.BlockSpec(memory_space=pltpu.SMEM)] * 2 + [IN_HBM] + [pl.BlockSpec(memory_space=pl.ANY)] * len(after),
            out_specs=(IN_HBM,) * 2,
            out_shape=(turned,) * 2,
            scratch_shapes=scratch(shaped((tokens, width), BF16), shaped((width, tokens), BF16), turned, turned)
            + semaphores(chunks + 2),
            compiler_params=WIDE,
            cost_estimate=cost(10**9, 10**7),
        )(rank, table, layer_input, *after)

    sent0, sent1 = arranged(SEQ // 2)
    span = 2 * heads * HEAD // SEQ
    incoming = pl.pallas_call(
        scan_kernel,
        in_specs=[pl.BlockSpec(memory_space=pltpu.SMEM), IN_VMEM, IN_HBM],
        out_shape=shaped((SEQ, span, HEAD), BF16),
        compiler_params=VMEM,
    )(place[None].astype(jnp.int32), states, sent0)
    incoming = lax.all_to_all(incoming, ("y", "z"), 0, 0, tiled=True).reshape(2 * heads * HEAD, HEAD)
    flops = 2 * half * columns * tokens

    def exchange(stream, step, array):
        return lax.ppermute(array, AXES, sorted(PARTNERS[stream][step].items()))

    other0, other1 = exchange(0, 0, sent0), exchange(1, 0, sent1)
    slopes_q, slopes_k = pl.pallas_call(
        heads_kernel,
        in_specs=[pl.BlockSpec(memory_space=pl.ANY)] + [IN_HBM] * 6,
        out_shape=(small, small),
        scratch_shapes=scratch(states_shape, *(small,) * 6) + semaphores(7),
        compiler_params=WIDE,
        cost_estimate=cost(10**9, 4 * 10**6),
    )(incoming, weighted_o, local_q, slope_q, weighted_v, local_k, slope_k)
    partner_q, partner_k = exchange(0, 0, slopes_q), exchange(1, 0, slopes_k)
    kept0, kept1 = arranged(0, slopes_q)
    keeps = [
        pl.pallas_call(
            projection_kernel,
            out_shape=shaped((half, columns), F32),
            compiler_params=VMEM,
            cost_estimate=cost(flops, 5 * 10**6),
        )(rows, slopes)
        for rows, slopes in ((kept0, slopes_q), (kept1, slopes_k))
    ]
    rows = half // 2
    pair = (shaped((rows, columns), F32), shaped((rows, columns), BF16))
    keep0, send0, keep1, send1 = pl.pallas_call(
        pair_kernel, out_shape=pair + pair, compiler_params=VMEM, cost_estimate=cost(2 * flops, 12 * 10**6)
    )(keeps[0], other0, partner_q, keeps[1], other1, partner_k)
    for step in range(1, STEPS - 1):
        operands = (exchange(0, step, send0), keep0, exchange(1, step, send1), keep1)
        rows //= 2
        if step < STEPS - 2:
            pair = (shaped((rows, columns), F32), shaped((rows, columns), BF16))
            keep0, send0, keep1, send1 = pl.pallas_call(
                add_kernel, out_shape=pair + pair, compiler_params=VMEM
            )(*operands)
        else:
            keep, send = pl.pallas_call(
                join_kernel,
                out_shape=(shaped((rows, 2 * columns), F32), shaped((rows, 2 * columns), BF16)),
                compiler_params=VMEM,
            )(*operands)
    assert PARTNERS[0][STEPS - 1] == PARTNERS[1][STEPS - 1]
    received = exchange(0, STEPS - 1, send)
    qweight_grad, kweight_grad = pl.pallas_call(
        last_kernel, out_shape=(shaped((rows, columns), F32),) * 2, compiler_params=VMEM
    )(received, keep)
    value_grad = pl.pallas_call(
        values_kernel,
        out_shape=small,
        compiler_params=VMEM,
        cost_estimate=cost(10**9, 5 * 10**6),
    )(local_v, weighted_k, incoming)
    return qweight_grad, kweight_grad, value_grad


def solution(mesh):
    chips = mesh.devices.shape[0] // CORES
    split = Mesh(mesh.devices.reshape(chips, CORES, N_Y, N_Z), ("x",) + AXES)
    seq, cores = ("y", "z"), ("x", "core")
    both = P(seq, cores)
    return jax.shard_map(
        per_device,
        mesh=split,
        in_specs=(P(seq, None), both, both, both, both, both),
        out_specs=(both, both, both),
        check_vma=False,
    )
```

time: 155 us -> 122 us (0.79)
  waiting for transfers between devices: 77.5 us -> 51 us
  local copies, waits for them, and re-layouts: 18.6 us -> 4.77 us
  starting transfers between devices: 28.2 us -> 32.4 us
  Pallas kernels: 28.9 us -> 31.3 us
    ppermute x10 -> x11, waiting for transfers between devices: 56.9 us -> 36.8 us  [exchange(): return lax.ppermute(array, AXES, sorted(PARTNERS[stream][step].items()))]
    unnamed x43 -> x20, local copies, waits for them, and re-layouts: 17.8 us -> 4.77 us
    all_to_all x1, waiting for transfers between devices: 14.5 us -> 6.79 us  [per_device(): states = lax.all_to_all(states, ('y', 'z'), 0, 0, tiled=True)]
    ppermute x10 -> x11, starting transfers between devices: 11.6 us -> 15.7 us  [exchange(): return lax.ppermute(array, AXES, sorted(PARTNERS[stream][step].items()))]
    pallas_call x18 -> x13, Pallas kernels: 28 us -> 31.1 us  [the longest x2 10.1 us: arranged(): pl.pallas_call(functools.partial(arrange_kernel, first=first), in_specs=[...]
  transfers between devices with their start and end apart: 12 -> 13, of which waited for: 8 -> 8; matrix products, arithmetic and copies ran while one was open for 1% -> 0% of each run, Pallas kernels for 13% -> 20%
where the time goes in v2:
time: 122 us; the launch traced here: 120 us
  waiting for transfers between devices  51 us (42%)
  starting transfers between devices  32.4 us (27%)
  Pallas kernels  31.3 us (26%)
  local copies, waits for them, and re-layouts  4.77 us (4%)
    ppermute x11, waiting for transfers between devices, exchange(): return lax.ppermute(array, AXES, sorted(PARTNERS[stream][step].items()))  36.8 us
    ppermute x11, starting transfers between devices, exchange(): return lax.ppermute(array, AXES, sorted(PARTNERS[stream][step].items()))  15.7 us
    all_to_all x1, starting transfers between devices, per_device(): states = lax.all_to_all(states, ('y', 'z'), 0, 0, tiled=True)  11.5 us
    pallas_call x2, Pallas kernels, arranged(): pl.pallas_call(functools.partial(arrange_kernel, first=first), in_specs=[...  10.1 us
    pallas_call x1, Pallas kernels, per_device(): pl.pallas_call(local_kernel, in_specs=[IN_HBM] * 5, out_specs=(IN_HBM,) *...  7.67 us
    all_to_all x1, waiting for transfers between devices, per_device(): lax.all_to_all(incoming, ('y', 'z'), 0, 0, tiled=True)  7.46 us
    all_to_all x1, waiting for transfers between devices, per_device(): states = lax.all_to_all(states, ('y', 'z'), 0, 0, tiled=True)  6.79 us
    all_to_all x1, starting transfers between devices, per_device(): lax.all_to_all(incoming, ('y', 'z'), 0, 0, tiled=True)  5.22 us
  transfers between devices with their start and end apart: 13, of which 8 were waited for; matrix products, arithmetic and copies ran while one was open for 0% of the time, Pallas kernels for 20%

profile of v2, /device:TPU:4, one launch (start us, length us, event | category | flops | bytes accessed | tf_op | source)
XLA Modules:
  0.0 120.3 jit_solution(17850749984369897589)
XLA Ops:
  0.6 4.1 %shard_map.94 = bf16[32,48,128]{2,1,0:T(8,128)(2,1)} custom-call(f32[4,512]{1,0:T(4,128)} %bitcast.6, bf16[512,512]{1,0:T(8,128)(2,1)} %query_hbm.3, bf16[512,512]{1,0:T(8,128)(2,1)} %key_hbm.3, bf16[512,512]{1,0:T(8,128)(2,1)} %value_hbm.3, bf16[512,512]{1,0:T(8,128)(2,1)} %grad_hbm.3), custom_call_target="tpu_custom_call" | custom-call | flops 1000000000 | bytes 4000000 | tf_op jit(solution)/shard_map/pallas_call | solution.py:376
  4.8 11.5 %all-to-all-start = ((bf16[32,48,128]{2,1,0:T(8,128)(2,1)}), bf16[32,48,128]{2,1,0:T(8,128)(2,1)S(1)}, u32[]{:S(2)}, u32[]{:S(2)}) async-start(bf16[32,48,128]{2,1,0:T(8,128)(2,1)} %shard_map.94), calls=%async_computation | async-start | bytes 786432 | tf_op jit(solution)/shard_map/all_to_all | solution.py:384
  16.3 5.0 %shard_map.95 = (bf16[1536,512]{1,0:T(8,128)(2,1)}, bf16[1536,512]{1,0:T(8,128)(2,1)}) custom-call(s32[1]{0:T(128)} %bitcast.place_ref, s32[4096]{0:T(1024)} %constant.20.clone.table_ref, bf16[512,3072]{1,0:T(8,128)(2,1)} %input_hbm.3), custom_call_target="tpu_custom_call" | custom-call | flops 1000000000 | bytes 10000000 | tf_op jit(solution)/shard_map/pallas_call | solution.py:401
  21.3 1.9 %collective-permute-start.2 = (bf16[1536,512]{1,0:T(8,128)(2,1)}, bf16[1536,512]{1,0:T(8,128)(2,1)S(1)}, u32[]{:S(2)}, u32[]{:S(2)}) collective-permute-start(bf16[1536,512]{1,0:T(8,128)(2,1)} %get-tuple-element.44), channel_id=1, source_target_pairs={{0,8},{1,9},{2,10},{3,11},{4,12},{5,13},{6,14},{7,15},{8,0},{9,1},... | collective-permute-start | bytes 4718600 | tf_op jit(solution)/shard_map/ppermute | solution.py:424
  23.2 1.5 %collective-permute-start = (bf16[1536,512]{1,0:T(8,128)(2,1)}, bf16[1536,512]{1,0:T(8,128)(2,1)S(1)}, u32[]{:S(2)}, u32[]{:S(2)}) collective-permute-start(bf16[1536,512]{1,0:T(8,128)(2,1)} %get-tuple-element.33.after_hbm), channel_id=1, source_target_pairs={{0,1},{1,0},{2,3},{3,2},{4,5},{5,4},{6,7},{7,6},{8,9},{9,8},{10,11... | collective-permute-start | bytes 4718600 | tf_op jit(solution)/shard_map/ppermute | solution.py:424
  24.7 6.8 %all-to-all-done.in_ref = bf16[32,48,128]{2,1,0:T(8,128)(2,1)S(1)} async-done(((bf16[32,48,128]{2,1,0:T(8,128)(2,1)}), bf16[32,48,128]{2,1,0:T(8,128)(2,1)S(1)}, u32[]{:S(2)}, u32[]{:S(2)}) %all-to-all-start) | async-done | bytes 393248 | tf_op jit(solution)/shard_map/all_to_all | solution.py:384
  31.4 1.4 %copy-done = bf16[1536,512]{1,0:T(8,128)(2,1)S(1)} copy-done((bf16[1536,512]{1,0:T(8,128)(2,1)S(1)}, bf16[1536,512]{1,0:T(8,128)(2,1)}, u32[]{:S(2)}) %copy-start) | copy-done | bytes 1572888
  33.1 0.7 copy-done.3
  33.8 5.2 %all-to-all-start.1 = ((bf16[32,32,128]{2,1,0:T(8,128)(2,1)}), bf16[32,32,128]{2,1,0:T(8,128)(2,1)S(1)}, u32[]{:S(2)}, u32[]{:S(2)}) async-start(bf16[32,32,128]{2,1,0:T(8,128)(2,1)} %copy-done.3), calls=%async_computation.1 | async-start | bytes 524288 | tf_op jit(solution)/shard_map/all_to_all | solution.py:420
  39.0 7.7 %shard_map.97 = (bf16[512,512]{1,0:T(8,128)(2,1)}, bf16[512,512]{1,0:T(8,128)(2,1)}, f32[512,512]{1,0:T(8,128)}, bf16[512,512]{1,0:T(8,128)(2,1)}, bf16[512,512]...) custom-call(f32[4,512]{1,0:T(4,128)} %bitcast.7, ...), custom_call_target="tpu_custom_call" | custom-call | flops 4000000000 | bytes 10000000 | tf_op jit(solution)/shard_map/pallas_call | solution.py:386
  46.7 7.5 %all-to-all-done.1 = bf16[32,32,128]{2,1,0:T(8,128)(2,1)S(1)} async-done(((bf16[32,32,128]{2,1,0:T(8,128)(2,1)}), bf16[32,32,128]{2,1,0:T(8,128)(2,1)S(1)}, u32[]{:S(2)}, u32[]{:S(2)}) %all-to-all-start.1) | async-done | bytes 262176 | tf_op jit(solution)/shard_map/all_to_all | solution.py:420
  54.8 3.2 %shard_map.98 = (bf16[512,512]{1,0:T(8,128)(2,1)}, bf16[512,512]{1,0:T(8,128)(2,1)}) custom-call(bf16[1024,128]{1,0:T(8,128)(2,1)} %bitcast.4, bf16[512,512]{1,0:T(8,128)(2,1)} %get-tuple-element.34.wo_hbm, bf16[512,512]{1,0:T(8,128)(2,1)} %get-tuple-element.35.gq_hbm, bf16[512,512]{1,0:T(8,128)(2,1)} %get-tuple-element.36.sq_hbm, ...), custom_call_target="tpu_custom_call" | custom-call | flops 1000000000 | bytes 4000000 | tf_op jit(solution)/shard_map/pallas_call | solution.py:427
  58.5 1.5 %collective-permute-start.1 = (bf16[512,512]{1,0:T(8,128)(2,1)}, bf16[512,512]{1,0:T(8,128)(2,1)S(1)}, u32[]{:S(2)}, u32[]{:S(2)}) collective-permute-start(bf16[512,512]{1,0:T(8,128)(2,1)} %get-tuple-element.40.refs_0_.slope_ref), channel_id=1, source_target_pairs={{0,1},{1,0},{2,3},{3,2},{4,5},{5,4},{6,7},{7,6},{8,9},{9,8},{10,11... | collective-permute-start | bytes 1572872 | tf_op jit(solution)/shard_map/ppermute | solution.py:424
  59.9 5.1 %shard_map.99 = (bf16[1536,512]{1,0:T(8,128)(2,1)}, bf16[1536,512]{1,0:T(8,128)(2,1)}) custom-call(s32[1]{0:T(128)} %bitcast.place_ref, s32[4096]{0:T(1024)} %constant.20.clone.table_ref, bf16[512,3072]{1,0:T(8,128)(2,1)} %input_hbm.3, bf16[512,512]{1,0:T(8,128)(2,1)} %get-tuple-element.40.refs_0_.slope_ref), custom_call_target="tpu_custom_call" | custom-call | flops 1000000000 | bytes 10000000 | tf_op jit(solution)/shard_map/pallas_call | solution.py:401
  65.0 1.4 %copy-done.2 = bf16[1536,512]{1,0:T(8,128)(2,1)S(1)} copy-done((bf16[1536,512]{1,0:T(8,128)(2,1)S(1)}, bf16[1536,512]{1,0:T(8,128)(2,1)}, u32[]{:S(2)}) %copy-start.2) | copy-done | bytes 1572888
  66.4 1.0 shard_map.100.own0_ref
  67.9 1.0 shard_map.101.own1_ref
  69.0 1.8 %shard_map.102 = (f32[768,512]{1,0:T(8,128)S(1)}, bf16[768,512]{1,0:T(8,128)(2,1)S(1)}, f32[768,512]{1,0:T(8,128)S(1)}, bf16[768,512]{1,0:T(8,128)(2,1)S(1)}) custom-call(f32[1536,512]{1,0:T(8,128)S(1)} %shard_map.100.own0_ref, bf16[1536,512]{1,0:T(8,128)(2,1)S(1)} %collective-permute-done.rows0_ref, ...), custom_call_target="tpu_custom_call" | custom-call | flops 1610612736 | bytes 12000000 | tf_op jit(solution)/shard_map/pallas_call | solution.py:448
  70.8 1.7 %collective-permute-start.4 = (bf16[768,512]{1,0:T(8,128)(2,1)S(1)}, bf16[768,512]{1,0:T(8,128)(2,1)S(1)}, u32[]{:S(2)}, u32[]{:S(2)}) collective-permute-start(bf16[768,512]{1,0:T(8,128)(2,1)S(1)} %get-tuple-element.45), channel_id=1, source_target_pairs={{0,8},{1,9},{2,10},{3,11},{4,12},{5,13},{6,14},{7,15},{8,0},{9,1},... | collective-permute-start | bytes 2359304 | tf_op jit(solution)/shard_map/ppermute | solution.py:424
  73.0 9.8 %collective-permute-done.4.received0_ref = bf16[768,512]{1,0:T(8,128)(2,1)S(1)} collective-permute-done((bf16[768,512]{1,0:T(8,128)(2,1)S(1)}, bf16[768,512]{1,0:T(8,128)(2,1)S(1)}, u32[]{:S(2)}, u32[]{:S(2)}) %collective-permute-start.4) | collective-permute-done | bytes 786464 | tf_op jit(solution)/shard_map/ppermute | solution.py:424
  82.8 1.6 %collective-permute-done.5.received1_ref = bf16[768,512]{1,0:T(8,128)(2,1)S(1)} collective-permute-done((bf16[768,512]{1,0:T(8,128)(2,1)S(1)}, bf16[768,512]{1,0:T(8,128)(2,1)S(1)}, u32[]{:S(2)}, u32[]{:S(2)}) %collective-permute-start.5) | collective-permute-done | bytes 786464 | tf_op jit(solution)/shard_map/ppermute | solution.py:424
  84.7 1.5 %collective-permute-start.6 = (bf16[384,512]{1,0:T(8,128)(2,1)S(1)}, bf16[384,512]{1,0:T(8,128)(2,1)S(1)}, u32[]{:S(2)}, u32[]{:S(2)}) collective-permute-start(bf16[384,512]{1,0:T(8,128)(2,1)S(1)} %get-tuple-element.49), channel_id=1, source_target_pairs={{0,2},{1,3},{2,0},{3,1},{4,6},{5,7},{6,4},{7,5},{8,10},{9,11},{10,... | collective-permute-start | bytes 1179656 | tf_op jit(solution)/shard_map/ppermute | solution.py:424
  86.2 1.1 collective-permute-start.7
  87.3 10.4 %collective-permute-done.6.received0_ref = bf16[384,512]{1,0:T(8,128)(2,1)S(1)} collective-permute-done((bf16[384,512]{1,0:T(8,128)(2,1)S(1)}, bf16[384,512]{1,0:T(8,128)(2,1)S(1)}, u32[]{:S(2)}, u32[]{:S(2)}) %collective-permute-start.6) | collective-permute-done | bytes 393248 | tf_op jit(solution)/shard_map/ppermute | solution.py:424
  97.9 1.3 %collective-permute-start.8 = (bf16[192,512]{1,0:T(8,128)(2,1)S(1)}, bf16[192,512]{1,0:T(8,128)(2,1)S(1)}, u32[]{:S(2)}, u32[]{:S(2)}) collective-permute-start(bf16[192,512]{1,0:T(8,128)(2,1)S(1)} %get-tuple-element.53), channel_id=1, source_target_pairs={{0,16},{1,17},{2,18},{3,19},{4,20},{5,21},{6,22},{7,23},{8,24},{9,... | collective-permute-start | bytes 589832 | tf_op jit(solution)/shard_map/ppermute | solution.py:424
  99.2 1.2 collective-permute-start.9
  100.3 4.8 %collective-permute-done.8.received0_ref = bf16[192,512]{1,0:T(8,128)(2,1)S(1)} collective-permute-done((bf16[192,512]{1,0:T(8,128)(2,1)S(1)}, bf16[192,512]{1,0:T(8,128)(2,1)S(1)}, u32[]{:S(2)}, u32[]{:S(2)}) %collective-permute-start.8) | collective-permute-done | bytes 196640 | tf_op jit(solution)/shard_map/ppermute | solution.py:424
  105.2 1.4 %collective-permute-done.9.received1_ref = bf16[192,512]{1,0:T(8,128)(2,1)S(1)} collective-permute-done((bf16[192,512]{1,0:T(8,128)(2,1)S(1)}, bf16[192,512]{1,0:T(8,128)(2,1)S(1)}, u32[]{:S(2)}, u32[]{:S(2)}) %collective-permute-start.9) | collective-permute-done | bytes 196640 | tf_op jit(solution)/shard_map/ppermute | solution.py:424
  106.7 3.1 %collective-permute-start.10 = (bf16[96,1024]{1,0:T(8,128)(2,1)S(1)}, bf16[96,1024]{1,0:T(8,128)(2,1)S(1)}, u32[]{:S(2)}, u32[]{:S(2)}) collective-permute-start(bf16[96,1024]{1,0:T(8,128)(2,1)S(1)} %get-tuple-element.57), channel_id=1, source_target_pairs={{0,4},{1,5},{2,6},{3,7},{4,0},{5,1},{6,2},{7,3},{8,12},{9,13},{10,... | collective-permute-start | bytes 589832 | tf_op jit(solution)/shard_map/ppermute | solution.py:424
  109.8 1.1 shard_map.107
  110.8 8.7 %collective-permute-done.10.received_ref = bf16[96,1024]{1,0:T(8,128)(2,1)S(1)} collective-permute-done((bf16[96,1024]{1,0:T(8,128)(2,1)S(1)}, bf16[96,1024]{1,0:T(8,128)(2,1)S(1)}, u32[]{:S(2)}, u32[]{:S(2)}) %collective-permute-start.10) | collective-permute-done | bytes 196640 | tf_op jit(solution)/shard_map/ppermute | solution.py:424
  119.5 0.8 shard_map.106
  (28 shorter events, 2.9 us)
Async XLA Ops:
  4.8 26.7 %all-to-all-start = ((bf16[32,48,128]{2,1,0:T(8,128)(2,1)}), bf16[32,48,128]{2,1,0:T(8,128)(2,1)S(1)}, u32[]{:S(2)}, u32[]{:S(2)}) async-start(bf16[32,48,128]{2,1,0:T(8,128)(2,1)} %shard_map.94), calls=%async_computation | async-start | bytes 786432 | tf_op jit(solution)/shard_map/all_to_all | solution.py:384
  21.3 47.6 %collective-permute-start.2 = (bf16[1536,512]{1,0:T(8,128)(2,1)}, bf16[1536,512]{1,0:T(8,128)(2,1)S(1)}, u32[]{:S(2)}, u32[]{:S(2)}) collective-permute-start(bf16[1536,512]{1,0:T(8,128)(2,1)} %get-tuple-element.44), channel_id=1, source_target_pairs={{0,8},{1,9},{2,10},{3,11},{4,12},{5,13},{6,14},{7,15},{8,0},{9,1},... | collective-permute-start | bytes 4718600 | tf_op jit(solution)/shard_map/ppermute | solution.py:424
  23.2 45.7 %collective-permute-start = (bf16[1536,512]{1,0:T(8,128)(2,1)}, bf16[1536,512]{1,0:T(8,128)(2,1)S(1)}, u32[]{:S(2)}, u32[]{:S(2)}) collective-permute-start(bf16[1536,512]{1,0:T(8,128)(2,1)} %get-tuple-element.33.after_hbm), channel_id=1, source_target_pairs={{0,1},{1,0},{2,3},{3,2},{4,5},{5,4},{6,7},{7,6},{8,9},{9,8},{10,11... | collective-permute-start | bytes 4718600 | tf_op jit(solution)/shard_map/ppermute | solution.py:424
  31.4 1.4 %copy-start = (bf16[1536,512]{1,0:T(8,128)(2,1)S(1)}, bf16[1536,512]{1,0:T(8,128)(2,1)}, u32[]{:S(2)}) copy-start(bf16[1536,512]{1,0:T(8,128)(2,1)} %get-tuple-element.33.after_hbm) | copy-start | bytes 4718596
  33.0 0.7 copy-start.3
  33.8 20.4 %all-to-all-start.1 = ((bf16[32,32,128]{2,1,0:T(8,128)(2,1)}), bf16[32,32,128]{2,1,0:T(8,128)(2,1)S(1)}, u32[]{:S(2)}, u32[]{:S(2)}) async-start(bf16[32,32,128]{2,1,0:T(8,128)(2,1)} %copy-done.3), calls=%async_computation.1 | async-start | bytes 524288 | tf_op jit(solution)/shard_map/all_to_all | solution.py:420
  54.1 0.7 copy-start.6
  58.0 11.0 %collective-permute-start.3 = (bf16[512,512]{1,0:T(8,128)(2,1)}, bf16[512,512]{1,0:T(8,128)(2,1)S(1)}, u32[]{:S(2)}, u32[]{:S(2)}) collective-permute-start(bf16[512,512]{1,0:T(8,128)(2,1)} %get-tuple-element.43.slope_ref), channel_id=1, source_target_pairs={{0,8},{1,9},{2,10},{3,11},{4,12},{5,13},{6,14},{7,15},{8,0},{9,1},... | collective-permute-start | bytes 1572872 | tf_op jit(solution)/shard_map/ppermute | solution.py:424
  58.5 6.6 %copy-start.4 = (bf16[512,512]{1,0:T(8,128)(2,1)S(1)}, bf16[512,512]{1,0:T(8,128)(2,1)}, u32[]{:S(2)}) copy-start(bf16[512,512]{1,0:T(8,128)(2,1)} %get-tuple-element.40.refs_0_.slope_ref) | copy-start | bytes 1572868
  58.5 10.5 %collective-permute-start.1 = (bf16[512,512]{1,0:T(8,128)(2,1)}, bf16[512,512]{1,0:T(8,128)(2,1)S(1)}, u32[]{:S(2)}, u32[]{:S(2)}) collective-permute-start(bf16[512,512]{1,0:T(8,128)(2,1)} %get-tuple-element.40.refs_0_.slope_ref), channel_id=1, source_target_pairs={{0,1},{1,0},{2,3},{3,2},{4,5},{5,4},{6,7},{7,6},{8,9},{9,8},{10,11... | collective-permute-start | bytes 1572872 | tf_op jit(solution)/shard_map/ppermute | solution.py:424
  65.0 1.4 %copy-start.2 = (bf16[1536,512]{1,0:T(8,128)(2,1)S(1)}, bf16[1536,512]{1,0:T(8,128)(2,1)}, u32[]{:S(2)}) copy-start(bf16[1536,512]{1,0:T(8,128)(2,1)} %get-tuple-element.41.rows_ref) | copy-start | bytes 4718596
  66.4 1.4 %copy-start.1 = (bf16[1536,512]{1,0:T(8,128)(2,1)S(1)}, bf16[1536,512]{1,0:T(8,128)(2,1)}, u32[]{:S(2)}) copy-start(bf16[1536,512]{1,0:T(8,128)(2,1)} %get-tuple-element.42.rows_ref) | copy-start | bytes 4718596
  66.4 1.5 %copy-start.5 = (bf16[512,512]{1,0:T(8,128)(2,1)S(1)}, bf16[512,512]{1,0:T(8,128)(2,1)}, u32[]{:S(2)}) copy-start(bf16[512,512]{1,0:T(8,128)(2,1)} %get-tuple-element.43.slope_ref) | copy-start | bytes 1572868
  70.8 12.1 %collective-permute-start.4 = (bf16[768,512]{1,0:T(8,128)(2,1)S(1)}, bf16[768,512]{1,0:T(8,128)(2,1)S(1)}, u32[]{:S(2)}, u32[]{:S(2)}) collective-permute-start(bf16[768,512]{1,0:T(8,128)(2,1)S(1)} %get-tuple-element.45), channel_id=1, source_target_pairs={{0,8},{1,9},{2,10},{3,11},{4,12},{5,13},{6,14},{7,15},{8,0},{9,1},... | collective-permute-start | bytes 2359304 | tf_op jit(solution)/shard_map/ppermute | solution.py:424
  72.5 12.0 %collective-permute-start.5 = (bf16[768,512]{1,0:T(8,128)(2,1)S(1)}, bf16[768,512]{1,0:T(8,128)(2,1)S(1)}, u32[]{:S(2)}, u32[]{:S(2)}) collective-permute-start(bf16[768,512]{1,0:T(8,128)(2,1)S(1)} %get-tuple-element.47), channel_id=1, source_target_pairs={{0,1},{1,0},{2,3},{3,2},{4,5},{5,4},{6,7},{7,6},{8,9},{9,8},{10,11... | collective-permute-start | bytes 2359304 | tf_op jit(solution)/shard_map/ppermute | solution.py:424
  84.7 13.0 %collective-permute-start.6 = (bf16[384,512]{1,0:T(8,128)(2,1)S(1)}, bf16[384,512]{1,0:T(8,128)(2,1)S(1)}, u32[]{:S(2)}, u32[]{:S(2)}) collective-permute-start(bf16[384,512]{1,0:T(8,128)(2,1)S(1)} %get-tuple-element.49), channel_id=1, source_target_pairs={{0,2},{1,3},{2,0},{3,1},{4,6},{5,7},{6,4},{7,5},{8,10},{9,11},{10,... | collective-permute-start | bytes 1179656 | tf_op jit(solution)/shard_map/ppermute | solution.py:424
  86.2 11.5 %collective-permute-start.7 = (bf16[384,512]{1,0:T(8,128)(2,1)S(1)}, bf16[384,512]{1,0:T(8,128)(2,1)S(1)}, u32[]{:S(2)}, u32[]{:S(2)}) collective-permute-start(bf16[384,512]{1,0:T(8,128)(2,1)S(1)} %get-tuple-element.51), channel_id=1, source_target_pairs={{0,16},{1,17},{2,18},{3,19},{4,20},{5,21},{6,22},{7,23},{8,24},{9,... | collective-permute-start | bytes 1179656 | tf_op jit(solution)/shard_map/ppermute | solution.py:424
  97.8 12.0 %copy-start.7 = (bf16[32,32,128]{2,1,0:T(8,128)(2,1)S(1)}, bf16[32,32,128]{2,1,0:T(8,128)(2,1)}, u32[]{:S(2)}) copy-start(bf16[32,32,128]{2,1,0:T(8,128)(2,1)} %copy-done.6) | copy-start | bytes 786436
  97.8 12.0 %copy-start.8 = (f32[512,512]{1,0:T(8,128)S(1)}, f32[512,512]{1,0:T(8,128)}, u32[]{:S(2)}) copy-start(f32[512,512]{1,0:T(8,128)} %get-tuple-element.61.local_ref) | copy-start | bytes 3145732
  97.8 12.0 %copy-start.9 = (bf16[512,512]{1,0:T(8,128)(2,1)S(1)}, bf16[512,512]{1,0:T(8,128)(2,1)}, u32[]{:S(2)}) copy-start(bf16[512,512]{1,0:T(8,128)(2,1)} %get-tuple-element.62.weighted_ref) | copy-start | bytes 1572868
  97.9 7.3 %collective-permute-start.8 = (bf16[192,512]{1,0:T(8,128)(2,1)S(1)}, bf16[192,512]{1,0:T(8,128)(2,1)S(1)}, u32[]{:S(2)}, u32[]{:S(2)}) collective-permute-start(bf16[192,512]{1,0:T(8,128)(2,1)S(1)} %get-tuple-element.53), channel_id=1, source_target_pairs={{0,16},{1,17},{2,18},{3,19},{4,20},{5,21},{6,22},{7,23},{8,24},{9,... | collective-permute-start | bytes 589832 | tf_op jit(solution)/shard_map/ppermute | solution.py:424
  99.2 7.4 %collective-permute-start.9 = (bf16[192,512]{1,0:T(8,128)(2,1)S(1)}, bf16[192,512]{1,0:T(8,128)(2,1)S(1)}, u32[]{:S(2)}, u32[]{:S(2)}) collective-permute-start(bf16[192,512]{1,0:T(8,128)(2,1)S(1)} %get-tuple-element.55), channel_id=1, source_target_pairs={{0,2},{1,3},{2,0},{3,1},{4,6},{5,7},{6,4},{7,5},{8,10},{9,11},{10,... | collective-permute-start | bytes 589832 | tf_op jit(solution)/shard_map/ppermute | solution.py:424
  106.7 12.8 %collective-permute-start.10 = (bf16[96,1024]{1,0:T(8,128)(2,1)S(1)}, bf16[96,1024]{1,0:T(8,128)(2,1)S(1)}, u32[]{:S(2)}, u32[]{:S(2)}) collective-permute-start(bf16[96,1024]{1,0:T(8,128)(2,1)S(1)} %get-tuple-element.57), channel_id=1, source_target_pairs={{0,4},{1,5},{2,6},{3,7},{4,0},{5,1},{6,2},{7,3},{8,12},{9,13},{10,... | collective-permute-start | bytes 589832 | tf_op jit(solution)/shard_map/ppermute | solution.py:424

commit v3 on v2

--- a/solution.py
+++ b/solution.py
@@ -16,7 +16,7 @@
 RANKS = CORES * SEQ
 STEPS = 5
 AXES = ("core", "y", "z")
-MESSAGE = 48
+MESSAGE = 40
 BF16 = jnp.bfloat16
 F32 = jnp.float32
 VMEM = pltpu.CompilerParams(vmem_limit_bytes=20 * 2**20)
@@ -91,12 +91,17 @@
 
 
 def prefix_sums(decay):
-    tokens = decay.shape[1]
+    heads, tokens = decay.shape
     rows = lax.broadcasted_iota(jnp.int32, (tokens, tokens), 0)
     columns = lax.broadcasted_iota(jnp.int32, (tokens, tokens), 1)
     lower = jnp.where(rows >= columns, 1.0, 0.0).astype(BF16)
-    pieces = split3(decay)
-    return sum(dot(lower, piece, (1, 1)) for piece in pieces), sum(dot(piece, lower, (1, 1)) for piece in pieces)
+    parts = jnp.concatenate([piece.astype(F32) for piece in split3(decay)], axis=0).astype(BF16)
+    down = dot(lower, parts, (1, 1))
+    across = dot(parts, lower, (1, 1))
+    return (
+        down[:, :heads] + down[:, heads : 2 * heads] + down[:, 2 * heads :],
+        across[:heads] + across[heads : 2 * heads] + across[2 * heads :],
+    )
 
 
 def states_kernel(
@@ -118,10 +123,10 @@
     to_end = jnp.exp(total - cumulative)
     per = SEQ // (2 * heads)
     span = HEAD // per
-    line = lax.broadcasted_iota(jnp.int32, (16, HEAD), 0)
+    line = lax.broadcasted_iota(jnp.int32, (MESSAGE - span, HEAD), 0)
     tails = []
     for head in range(heads):
-        marks = split3(jnp.broadcast_to(total[:, head : head + 1], (16, HEAD)))
+        marks = split3(jnp.broadcast_to(total[:, head : head + 1], (MESSAGE - span, HEAD)))
         tail = jnp.where(
             line == 0, marks[0].astype(F32), jnp.where(line == 1, marks[1].astype(F32), marks[2].astype(F32))
         )
@@ -152,7 +157,7 @@
         emit(1, head, dot(weighted, grad_ref[:, part], (0, 0)))
 
 
-def scan_kernel(place_ref, in_ref, after_hbm, out_ref):
+def scan_kernel(place_ref, in_ref, out_ref):
     count = in_ref.shape[0]
     span = out_ref.shape[1]
     backward = place_ref[0] >= count // 2
@@ -250,15 +255,15 @@
 ):
     heads = wo_ref.shape[1] // HEAD
     copies = moves(
-        (states_hbm, wo_hbm, gq_hbm, sq_hbm, wv_hbm, gk_hbm, sk_hbm),
-        (states_ref, wo_ref, gq_ref, sq_ref, wv_ref, gk_ref, sk_ref),
+        (wo_hbm, states_hbm, gq_hbm, sq_hbm, wv_hbm, gk_hbm, sk_hbm),
+        (wo_ref, states_ref, gq_ref, sq_ref, wv_ref, gk_ref, sk_ref),
         semaphores,
     )
     start_all(copies)
     for stream, (weighted, local, slope, slopes) in enumerate(
         ((wo_ref, gq_ref, sq_ref, slopes_q_ref), (wv_ref, gk_ref, sk_ref, slopes_k_ref))
     ):
-        for copy in copies[1 + 3 * stream : 4 + 3 * stream] + copies[: 1 - stream]:
+        for copy in copies[4 * stream : 4 * stream + 4 - stream]:
             copy.wait()
         for head in range(heads):
             part = slice(head * HEAD, (head + 1) * HEAD)
@@ -267,16 +272,14 @@
             slopes[:, part] = (gradient * slope[:, part].astype(F32)).astype(BF16)
 
 
-def pair_kernel(
-    own0_ref, rows0_ref, slopes0_ref, own1_ref, rows1_ref, slopes1_ref, keep0_ref, send0_ref, keep1_ref, send1_ref
-):
-    half = keep0_ref.shape[0]
-    for own, rows, slopes, keep, send in (
-        (own0_ref, rows0_ref, slopes0_ref, keep0_ref, send0_ref),
-        (own1_ref, rows1_ref, slopes1_ref, keep1_ref, send1_ref),
+def pair_kernel(own0_ref, rows0_ref, slopes0_ref, own1_ref, rows1_ref, slopes1_ref, *refs, first):
+    out0_ref, out1_ref = refs[-2:]
+    part = slice(first, first + out0_ref.shape[0])
+    for own, rows, slopes, out in (
+        (own0_ref, rows0_ref, slopes0_ref, out0_ref),
+        (own1_ref, rows1_ref, slopes1_ref, out1_ref),
     ):
-        send[...] = (own[half:] + dot(rows[half:], slopes[...], (1, 0))).astype(BF16)
-        keep[...] = own[:half] + dot(rows[:half], slopes[...], (1, 0))
+        out[...] = (own[part] + dot(rows[...], slopes[...], (1, 0))).astype(out.dtype)
 
 
 def values_kernel(local_ref, weighted_ref, states_ref, out_ref):
@@ -287,8 +290,11 @@
         out_ref[:, part] = (local_ref[:, part] + dot(weighted_ref[:, part], states_ref[later, :], (1, 0))).astype(BF16)
 
 
-def arrange_kernel(place_ref, table_ref, input_hbm, *refs, first):
-    out0_hbm, out1_hbm, input_ref, turned_ref, out0_ref, out1_ref, semaphores = refs[-7:]
+def arrange_kernel(
+    place_ref, table_ref, input_hbm,
+    late0_hbm, late1_hbm, early0_hbm, early1_hbm, kept0_hbm, kept1_hbm,
+    input_ref, turned_ref, late0_ref, late1_ref, early0_ref, early1_ref, kept0_ref, kept1_ref, semaphores,
+):
     tokens, width = input_ref.shape
     block = width // SEQ
     chunk = 384
@@ -298,22 +304,33 @@
         semaphores,
     )
     start_all(reads)
-    writes = moves((out0_ref, out1_ref), (out0_hbm, out1_hbm), semaphores, len(reads))
+    outs = (late0_ref, late1_ref, early0_ref, early1_ref, kept0_ref, kept1_ref)
+    targets = (late0_hbm, late1_hbm, early0_hbm, early1_hbm, kept0_hbm, kept1_hbm)
+    writes = moves(outs, targets, semaphores, len(reads))
     for at, copy in enumerate(reads):
         copy.wait()
         turned_ref[at * chunk : (at + 1) * chunk, :] = input_ref[:, at * chunk : (at + 1) * chunk].T
-    for stream, target in enumerate((out0_ref, out1_ref)):
-        for at in range(SEQ // 2):
+    firsts = (3 * SEQ // 4, 3 * SEQ // 4, SEQ // 2, SEQ // 2, 0, 0)
+    for out, write, stream, first in zip(outs, writes, (0, 1) * 3, firsts):
+        for at in range(out.shape[0] // block):
             entry = (stream * RANKS + place_ref[0]) * SEQ + first + at
             start = pl.multiple_of(table_ref[entry] * block, block)
-            target[at * block : (at + 1) * block, :] = turned_ref[pl.ds(start, block), :]
-        writes[stream].start()
+            out[at * block : (at + 1) * block, :] = turned_ref[pl.ds(start, block), :]
+        write.start()
     for copy in writes:
         copy.wait()
 
 
-def projection_kernel(rows_ref, slope_ref, out_ref):
-    out_ref[...] = dot(rows_ref[...], slope_ref[...], (1, 0))
+def own_kernel(
+    rows0_hbm, rows1_hbm, slopes0_ref, slopes1_ref, out0_ref, out1_ref, rows0_ref, rows1_ref, semaphores
+):
+    copies = moves((rows0_hbm, rows1_hbm), (rows0_ref, rows1_ref), semaphores)
+    start_all(copies)
+    for copy, rows, slopes, out in zip(
+        copies, (rows0_ref, rows1_ref), (slopes0_ref, slopes1_ref), (out0_ref, out1_ref)
+    ):
+        copy.wait()
+        out[...] = dot(rows[...], slopes[...], (1, 0))
 
 
 def add_kernel(received0_ref, kept0_ref, received1_ref, kept1_ref, keep0_ref, send0_ref, keep1_ref, send1_ref):
@@ -391,39 +408,42 @@
         scratch_shapes=scratch(decay, *(small,) * 6, *local_shapes, shaped((tokens, heads), F32), decay)
         + semaphores(13),
         compiler_params=WIDE,
-        cost_estimate=cost(4 * 10**9, 10**7),
+        cost_estimate=cost(6 * 10**10, 10**7),
     )(*arguments)
     rank = (core * SEQ + place)[None].astype(jnp.int32)
     table = jnp.asarray(ORDERS.reshape(-1))
     chunks = width // 384
 
-    def arranged(first, *after):
-        return pl.pallas_call(
-            functools.partial(arrange_kernel, first=first),
-            in_specs=[pl.BlockSpec(memory_space=pltpu.SMEM)] * 2 + [IN_HBM] + [pl.BlockSpec(memory_space=pl.ANY)] * len(after),
-            out_specs=(IN_HBM,) * 2,
-            out_shape=(turned,) * 2,
-            scratch_shapes=scratch(shaped((tokens, width), BF16), shaped((width, tokens), BF16), turned, turned)
-            + semaphores(chunks + 2),
-            compiler_params=WIDE,
-            cost_estimate=cost(10**9, 10**7),
-        )(rank, table, layer_input, *after)
-
-    sent0, sent1 = arranged(SEQ // 2)
+    quarter = shaped((half // 2, tokens), BF16)
+    arranged = (quarter,) * 4 + (turned,) * 2
+    late0, late1, early0, early1, kept0, kept1 = pl.pallas_call(
+        arrange_kernel,
+        in_specs=[pl.BlockSpec(memory_space=pltpu.SMEM)] * 2 + [IN_HBM],
+        out_specs=(IN_HBM,) * 6,
+        out_shape=arranged,
+        scratch_shapes=scratch(shaped((tokens, width), BF16), shaped((width, tokens), BF16), *arranged)
+        + semaphores(chunks + 6),
+        compiler_params=WIDE,
+        cost_estimate=cost(10**9, 10**7),
+    )(rank, table, layer_input)
+    states, kept0 = lax.optimization_barrier((states, kept0))
     span = 2 * heads * HEAD // SEQ
     incoming = pl.pallas_call(
         scan_kernel,
-        in_specs=[pl.BlockSpec(memory_space=pltpu.SMEM), IN_VMEM, IN_HBM],
+        in_specs=[pl.BlockSpec(memory_space=pltpu.SMEM), IN_VMEM],
         out_shape=shaped((SEQ, span, HEAD), BF16),
         compiler_params=VMEM,
-    )(place[None].astype(jnp.int32), states, sent0)
+    )(place[None].astype(jnp.int32), states)
+    incoming, early0, early1 = lax.optimization_barrier((incoming, early0, early1))
     incoming = lax.all_to_all(incoming, ("y", "z"), 0, 0, tiled=True).reshape(2 * heads * HEAD, HEAD)
     flops = 2 * half * columns * tokens
 
     def exchange(stream, step, array):
         return lax.ppermute(array, AXES, sorted(PARTNERS[stream][step].items()))
 
-    other0, other1 = exchange(0, 0, sent0), exchange(1, 0, sent1)
+    late0, late1 = exchange(0, 0, late0), exchange(1, 0, late1)
+    early0, early1 = exchange(0, 0, early0), exchange(1, 0, early1)
+    early0, early1, kept0 = lax.optimization_barrier((early0, early1, kept0))
     slopes_q, slopes_k = pl.pallas_call(
         heads_kernel,
         in_specs=[pl.BlockSpec(memory_space=pl.ANY)] + [IN_HBM] * 6,
@@ -433,21 +453,27 @@
         cost_estimate=cost(10**9, 4 * 10**6),
     )(incoming, weighted_o, local_q, slope_q, weighted_v, local_k, slope_k)
     partner_q, partner_k = exchange(0, 0, slopes_q), exchange(1, 0, slopes_k)
-    kept0, kept1 = arranged(0, slopes_q)
-    keeps = [
-        pl.pallas_call(
-            projection_kernel,
-            out_shape=shaped((half, columns), F32),
+    own0, own1 = pl.pallas_call(
+        own_kernel,
+        in_specs=[IN_HBM, IN_HBM, IN_VMEM, IN_VMEM],
+        out_shape=(shaped((half, columns), F32),) * 2,
+        scratch_shapes=scratch(turned, turned) + semaphores(2),
+        compiler_params=VMEM,
+        cost_estimate=cost(2 * flops, 10**7),
+    )(kept0, kept1, slopes_q, slopes_k)
+    rows = half // 2
+
+    def paired(first, dtype, other0, other1, *after):
+        return pl.pallas_call(
+            functools.partial(pair_kernel, first=first),
+            in_specs=[IN_VMEM] * 6 + [IN_HBM] * len(after),
+            out_shape=(shaped((rows, columns), dtype),) * 2,
             compiler_params=VMEM,
-            cost_estimate=cost(flops, 5 * 10**6),
-        )(rows, slopes)
-        for rows, slopes in ((kept0, slopes_q), (kept1, slopes_k))
-    ]
-    rows = half // 2
-    pair = (shaped((rows, columns), F32), shaped((rows, columns), BF16))
-    keep0, send0, keep1, send1 = pl.pallas_call(
-        pair_kernel, out_shape=pair + pair, compiler_params=VMEM, cost_estimate=cost(2 * flops, 12 * 10**6)
-    )(keeps[0], other0, partner_q, keeps[1], other1, partner_k)
+            cost_estimate=cost(flops, 6 * 10**6),
+        )(own0, other0, partner_q, own1, other1, partner_k, *after)
+
+    send0, send1 = paired(rows, BF16, late0, late1)
+    keep0, keep1 = paired(0, F32, early0, early1, send1[:16, :128])
     for step in range(1, STEPS - 1):
         operands = (exchange(0, step, send0), keep0, exchange(1, step, send1), keep1)
         rows //= 2

time: 122 us -> 115 us (0.943)
  the two profiles are of different devices: /device:TPU:4 before, /device:TPU:39 now
where the time goes in v3:
time: 115 us; the launch traced here: 114 us
  waiting for transfers between devices  47.7 us (41%)
  starting transfers between devices  35.1 us (31%)
  Pallas kernels  27.8 us (24%)
  local copies, waits for them, and re-layouts  2.81 us (2%)
    ppermute x13, waiting for transfers between devices, exchange(): return lax.ppermute(array, AXES, sorted(PARTNERS[stream][step].items()))  45 us
    ppermute x13, starting transfers between devices, exchange(): return lax.ppermute(array, AXES, sorted(PARTNERS[stream][step].items()))  19.3 us
    all_to_all x1, starting transfers between devices, per_device(): states = lax.all_to_all(states, ('y', 'z'), 0, 0, tiled=True)  10.8 us
    pallas_call x1, Pallas kernels, per_device(): pl.pallas_call(local_kernel, in_specs=[IN_HBM] * 5, out_specs=(IN_HBM,) *...  7.57 us
    pallas_call x1, Pallas kernels, per_device(): pl.pallas_call(arrange_kernel, in_specs=[pl.BlockSpec(memory_space=pltpu....  5.94 us
    all_to_all x1, starting transfers between devices, per_device(): lax.all_to_all(incoming, ('y', 'z'), 0, 0, tiled=True)  5 us
    pallas_call x1, Pallas kernels, per_device(): pl.pallas_call(states_kernel, in_specs=[IN_HBM] * 5, out_shape=shaped((SE...  3.66 us
    pallas_call x1, Pallas kernels, per_device(): pl.pallas_call(heads_kernel, in_specs=[pl.BlockSpec(memory_space=pl.ANY)]...  3.3 us
  transfers between devices with their start and end apart: 15, of which 11 were waited for; matrix products, arithmetic and copies ran while one was open for 0% of the time, Pallas kernels for 19%

profile of v3, /device:TPU:39, one launch (start us, length us, event | category | flops | bytes accessed | tf_op | source)
XLA Modules:
  0.0 114.2 jit_solution(5798474385906937434)
XLA Ops:
  0.6 3.7 %shard_map.94 = bf16[32,40,128]{2,1,0:T(8,128)(2,1)} custom-call(f32[4,512]{1,0:T(4,128)} %bitcast.6, bf16[512,512]{1,0:T(8,128)(2,1)} %query_hbm.3, bf16[512,512]{1,0:T(8,128)(2,1)} %key_hbm.3, bf16[512,512]{1,0:T(8,128)(2,1)} %value_hbm.3, bf16[512,512]{1,0:T(8,128)(2,1)} %grad_hbm.3), custom_call_target="tpu_custom_call" | custom-call | flops 1000000000 | bytes 4000000 | tf_op jit(solution)/shard_map/pallas_call | solution.py:393
  4.3 10.8 %all-to-all-start = ((bf16[32,40,128]{2,1,0:T(8,128)(2,1)}), bf16[32,40,128]{2,1,0:T(8,128)(2,1)S(1)}, u32[]{:S(2)}, u32[]{:S(2)}) async-start(bf16[32,40,128]{2,1,0:T(8,128)(2,1)} %shard_map.94), calls=%async_computation | async-start | bytes 655360 | tf_op jit(solution)/shard_map/all_to_all | solution.py:401
  15.1 5.9 %shard_map.95 = (bf16[768,512]{1,0:T(8,128)(2,1)}, bf16[768,512]{1,0:T(8,128)(2,1)}, bf16[768,512]{1,0:T(8,128)(2,1)}, bf16[768,512]{1,0:T(8,128)(2,1)}, bf16[15...) custom-call(s32[1]{0:T(128)} %bitcast.2.place_ref, s32[4096]{0:T(1024)} %constant.20.clone.table_ref, ...), custom_call_target="tpu_custom_call" | custom-call | flops 1000000000 | bytes 10000000 | tf_op jit(solution)/shard_map/pallas_call | solution.py:419
  21.1 1.3 %collective-permute-start.2 = (bf16[768,512]{1,0:T(8,128)(2,1)}, bf16[768,512]{1,0:T(8,128)(2,1)S(1)}, u32[]{:S(2)}, u32[]{:S(2)}) collective-permute-start(bf16[768,512]{1,0:T(8,128)(2,1)} %get-tuple-element.64), channel_id=1, source_target_pairs={{0,1},{1,0},{2,3},{3,2},{4,5},{5,4},{6,7},{7,6},{8,9},{9,8},{10,11... | collective-permute-start | bytes 2359304 | tf_op jit(solution)/shard_map/ppermute | solution.py:442
  22.3 2.5 %collective-permute-start.4 = (bf16[768,512]{1,0:T(8,128)(2,1)}, bf16[768,512]{1,0:T(8,128)(2,1)S(1)}, u32[]{:S(2)}, u32[]{:S(2)}) collective-permute-start(bf16[768,512]{1,0:T(8,128)(2,1)} %get-tuple-element.66), channel_id=1, source_target_pairs={{0,8},{1,9},{2,10},{3,11},{4,12},{5,13},{6,14},{7,15},{8,0},{9,1},... | collective-permute-start | bytes 2359304 | tf_op jit(solution)/shard_map/ppermute | solution.py:442
  24.8 2.7 %all-to-all-done.in_ref = bf16[32,40,128]{2,1,0:T(8,128)(2,1)S(1)} async-done(((bf16[32,40,128]{2,1,0:T(8,128)(2,1)}), bf16[32,40,128]{2,1,0:T(8,128)(2,1)S(1)}, u32[]{:S(2)}, u32[]{:S(2)}) %all-to-all-start) | async-done | bytes 327712 | tf_op jit(solution)/shard_map/all_to_all | solution.py:401
  27.5 0.9 shard_map.96
  28.4 5.0 %all-to-all-start.1 = ((bf16[32,32,128]{2,1,0:T(8,128)(2,1)}), bf16[32,32,128]{2,1,0:T(8,128)(2,1)S(1)}, u32[]{:S(2)}, u32[]{:S(2)}) async-start(bf16[32,32,128]{2,1,0:T(8,128)(2,1)} %shard_map.96), calls=%async_computation.1 | async-start | bytes 524288 | tf_op jit(solution)/shard_map/all_to_all | solution.py:438
  33.4 1.3 %collective-permute-start = (bf16[768,512]{1,0:T(8,128)(2,1)}, bf16[768,512]{1,0:T(8,128)(2,1)S(1)}, u32[]{:S(2)}, u32[]{:S(2)}) collective-permute-start(bf16[768,512]{1,0:T(8,128)(2,1)} %get-tuple-element.49), channel_id=1, source_target_pairs={{0,1},{1,0},{2,3},{3,2},{4,5},{5,4},{6,7},{7,6},{8,9},{9,8},{10,11... | collective-permute-start | bytes 2359304 | tf_op jit(solution)/shard_map/ppermute | solution.py:442
  34.7 2.5 %collective-permute-start.1 = (bf16[768,512]{1,0:T(8,128)(2,1)}, bf16[768,512]{1,0:T(8,128)(2,1)S(1)}, u32[]{:S(2)}, u32[]{:S(2)}) collective-permute-start(bf16[768,512]{1,0:T(8,128)(2,1)} %get-tuple-element.50), channel_id=1, source_target_pairs={{0,8},{1,9},{2,10},{3,11},{4,12},{5,13},{6,14},{7,15},{8,0},{9,1},... | collective-permute-start | bytes 2359304 | tf_op jit(solution)/shard_map/ppermute | solution.py:442
  37.2 7.6 %shard_map.97 = (bf16[512,512]{1,0:T(8,128)(2,1)}, bf16[512,512]{1,0:T(8,128)(2,1)}, f32[512,512]{1,0:T(8,128)}, bf16[512,512]{1,0:T(8,128)(2,1)}, bf16[512,512]...) custom-call(f32[4,512]{1,0:T(4,128)} %bitcast.7, ...), custom_call_target="tpu_custom_call" | custom-call | flops 60000002048 | bytes 10000000 | tf_op jit(solution)/shard_map/pallas_call | solution.py:403
  45.5 3.3 %shard_map.98 = (bf16[512,512]{1,0:T(8,128)(2,1)}, bf16[512,512]{1,0:T(8,128)(2,1)}) custom-call(bf16[1024,128]{1,0:T(8,128)(2,1)} %bitcast.4, bf16[512,512]{1,0:T(8,128)(2,1)} %get-tuple-element.55.wo_hbm, bf16[512,512]{1,0:T(8,128)(2,1)} %get-tuple-element.56.gq_hbm, bf16[512,512]{1,0:T(8,128)(2,1)} %get-tuple-element.57.sq_hbm, ...), custom_call_target="tpu_custom_call" | custom-call | flops 1000000000 | bytes 4000000 | tf_op jit(solution)/shard_map/pallas_call | solution.py:447
  49.7 2.6 %collective-permute-start.5 = (bf16[512,512]{1,0:T(8,128)(2,1)}, bf16[512,512]{1,0:T(8,128)(2,1)S(1)}, u32[]{:S(2)}, u32[]{:S(2)}) collective-permute-start(bf16[512,512]{1,0:T(8,128)(2,1)} %get-tuple-element.62.slopes1_ref), channel_id=1, source_target_pairs={{0,8},{1,9},{2,10},{3,11},{4,12},{5,13},{6,14},{7,15},{8,0},{9,1},... | collective-permute-start | bytes 1572872 | tf_op jit(solution)/shard_map/ppermute | solution.py:442
  52.4 1.1 copy-done.2
  53.4 1.0 copy-done.3
  54.5 2.2 %shard_map.99 = (f32[1536,512]{1,0:T(8,128)S(1)}, f32[1536,512]{1,0:T(8,128)S(1)}) custom-call(bf16[1536,512]{1,0:T(8,128)(2,1)S(1)} %copy-done.4, bf16[1536,512]{1,0:T(8,128)(2,1)S(1)} %copy-done.5, bf16[512,512]{1,0:T(8,128)(2,1)S(1)} %copy-done.3, bf16[512,512]{1,0:T(8,128)(2,1)S(1)} %copy-done.2), custom_call_target="tpu_custom_call" | custom-call | flops 1610612736 | bytes 10000000 | tf_op jit(solution)/shard_map/pallas_call | solution.py:456
  56.7 0.7 collective-permute-done.3.slopes0_ref
  57.4 1.8 %collective-permute-done.5.slopes1_ref = bf16[512,512]{1,0:T(8,128)(2,1)S(1)} collective-permute-done((bf16[512,512]{1,0:T(8,128)(2,1)}, bf16[512,512]{1,0:T(8,128)(2,1)S(1)}, u32[]{:S(2)}, u32[]{:S(2)}) %collective-permute-start.5) | collective-permute-done | bytes 524320 | tf_op jit(solution)/shard_map/ppermute | solution.py:442
  59.2 1.0 shard_map.100
  60.1 2.7 %collective-permute-start.6 = (bf16[768,512]{1,0:T(8,128)(2,1)S(1)}, bf16[768,512]{1,0:T(8,128)(2,1)S(1)}, u32[]{:S(2)}, u32[]{:S(2)}) collective-permute-start(bf16[768,512]{1,0:T(8,128)(2,1)S(1)} %get-tuple-element.67), channel_id=1, source_target_pairs={{0,8},{1,9},{2,10},{3,11},{4,12},{5,13},{6,14},{7,15},{8,0},{9,1},... | collective-permute-start | bytes 2359304 | tf_op jit(solution)/shard_map/ppermute | solution.py:442
  63.2 1.0 shard_map.101
  64.2 8.1 %collective-permute-done.6.received0_ref = bf16[768,512]{1,0:T(8,128)(2,1)S(1)} collective-permute-done((bf16[768,512]{1,0:T(8,128)(2,1)S(1)}, bf16[768,512]{1,0:T(8,128)(2,1)S(1)}, u32[]{:S(2)}, u32[]{:S(2)}) %collective-permute-start.6) | collective-permute-done | bytes 786464 | tf_op jit(solution)/shard_map/ppermute | solution.py:442
  72.3 1.7 %collective-permute-done.7.received1_ref = bf16[768,512]{1,0:T(8,128)(2,1)S(1)} collective-permute-done((bf16[768,512]{1,0:T(8,128)(2,1)S(1)}, bf16[768,512]{1,0:T(8,128)(2,1)S(1)}, u32[]{:S(2)}, u32[]{:S(2)}) %collective-permute-start.7) | collective-permute-done | bytes 786464 | tf_op jit(solution)/shard_map/ppermute | solution.py:442
  74.2 2.7 %collective-permute-start.8 = (bf16[384,512]{1,0:T(8,128)(2,1)S(1)}, bf16[384,512]{1,0:T(8,128)(2,1)S(1)}, u32[]{:S(2)}, u32[]{:S(2)}) collective-permute-start(bf16[384,512]{1,0:T(8,128)(2,1)S(1)} %get-tuple-element.73), channel_id=1, source_target_pairs={{0,2},{1,3},{2,0},{3,1},{4,6},{5,7},{6,4},{7,5},{8,10},{9,11},{10,... | collective-permute-start | bytes 1179656 | tf_op jit(solution)/shard_map/ppermute | solution.py:442
  77.0 8.2 %collective-permute-done.8.received0_ref = bf16[384,512]{1,0:T(8,128)(2,1)S(1)} collective-permute-done((bf16[384,512]{1,0:T(8,128)(2,1)S(1)}, bf16[384,512]{1,0:T(8,128)(2,1)S(1)}, u32[]{:S(2)}, u32[]{:S(2)}) %collective-permute-start.8) | collective-permute-done | bytes 393248 | tf_op jit(solution)/shard_map/ppermute | solution.py:442
  85.2 4.2 %collective-permute-done.9.received1_ref = bf16[384,512]{1,0:T(8,128)(2,1)S(1)} collective-permute-done((bf16[384,512]{1,0:T(8,128)(2,1)S(1)}, bf16[384,512]{1,0:T(8,128)(2,1)S(1)}, u32[]{:S(2)}, u32[]{:S(2)}) %collective-permute-start.9) | collective-permute-done | bytes 393248 | tf_op jit(solution)/shard_map/ppermute | solution.py:442
  89.9 7.1 %collective-permute-done.10.received0_ref = bf16[192,512]{1,0:T(8,128)(2,1)S(1)} collective-permute-done((bf16[192,512]{1,0:T(8,128)(2,1)S(1)}, bf16[192,512]{1,0:T(8,128)(2,1)S(1)}, u32[]{:S(2)}, u32[]{:S(2)}) %collective-permute-start.10) | collective-permute-done | bytes 196640 | tf_op jit(solution)/shard_map/ppermute | solution.py:442
  97.0 1.5 %collective-permute-done.11.received1_ref = bf16[192,512]{1,0:T(8,128)(2,1)S(1)} collective-permute-done((bf16[192,512]{1,0:T(8,128)(2,1)S(1)}, bf16[192,512]{1,0:T(8,128)(2,1)S(1)}, u32[]{:S(2)}, u32[]{:S(2)}) %collective-permute-start.11) | collective-permute-done | bytes 196640 | tf_op jit(solution)/shard_map/ppermute | solution.py:442
  98.6 2.7 %collective-permute-start.12 = (bf16[96,1024]{1,0:T(8,128)(2,1)S(1)}, bf16[96,1024]{1,0:T(8,128)(2,1)S(1)}, u32[]{:S(2)}, u32[]{:S(2)}) collective-permute-start(bf16[96,1024]{1,0:T(8,128)(2,1)S(1)} %get-tuple-element.81), channel_id=1, source_target_pairs={{0,4},{1,5},{2,6},{3,7},{4,0},{5,1},{6,2},{7,3},{8,12},{9,13},{10,... | collective-permute-start | bytes 589832 | tf_op jit(solution)/shard_map/ppermute | solution.py:442
  101.3 1.1 shard_map.106
  102.4 11.1 %collective-permute-done.12.received_ref = bf16[96,1024]{1,0:T(8,128)(2,1)S(1)} collective-permute-done((bf16[96,1024]{1,0:T(8,128)(2,1)S(1)}, bf16[96,1024]{1,0:T(8,128)(2,1)S(1)}, u32[]{:S(2)}, u32[]{:S(2)}) %collective-permute-start.12) | collective-permute-done | bytes 196640 | tf_op jit(solution)/shard_map/ppermute | solution.py:442
  113.4 0.8 shard_map.105
  (28 shorter events, 2.8 us)
Async XLA Ops:
  4.3 23.2 %all-to-all-start = ((bf16[32,40,128]{2,1,0:T(8,128)(2,1)}), bf16[32,40,128]{2,1,0:T(8,128)(2,1)S(1)}, u32[]{:S(2)}, u32[]{:S(2)}) async-start(bf16[32,40,128]{2,1,0:T(8,128)(2,1)} %shard_map.94), calls=%async_computation | async-start | bytes 655360 | tf_op jit(solution)/shard_map/all_to_all | solution.py:401
  21.1 35.6 %collective-permute-start.2 = (bf16[768,512]{1,0:T(8,128)(2,1)}, bf16[768,512]{1,0:T(8,128)(2,1)S(1)}, u32[]{:S(2)}, u32[]{:S(2)}) collective-permute-start(bf16[768,512]{1,0:T(8,128)(2,1)} %get-tuple-element.64), channel_id=1, source_target_pairs={{0,1},{1,0},{2,3},{3,2},{4,5},{5,4},{6,7},{7,6},{8,9},{9,8},{10,11... | collective-permute-start | bytes 2359304 | tf_op jit(solution)/shard_map/ppermute | solution.py:442
  22.3 34.3 %collective-permute-start.4 = (bf16[768,512]{1,0:T(8,128)(2,1)}, bf16[768,512]{1,0:T(8,128)(2,1)S(1)}, u32[]{:S(2)}, u32[]{:S(2)}) collective-permute-start(bf16[768,512]{1,0:T(8,128)(2,1)} %get-tuple-element.66), channel_id=1, source_target_pairs={{0,8},{1,9},{2,10},{3,11},{4,12},{5,13},{6,14},{7,15},{8,0},{9,1},... | collective-permute-start | bytes 2359304 | tf_op jit(solution)/shard_map/ppermute | solution.py:442
  28.4 16.3 %all-to-all-start.1 = ((bf16[32,32,128]{2,1,0:T(8,128)(2,1)}), bf16[32,32,128]{2,1,0:T(8,128)(2,1)S(1)}, u32[]{:S(2)}, u32[]{:S(2)}) async-start(bf16[32,32,128]{2,1,0:T(8,128)(2,1)} %shard_map.96), calls=%async_computation.1 | async-start | bytes 524288 | tf_op jit(solution)/shard_map/all_to_all | solution.py:438
  33.4 16.3 %collective-permute-start = (bf16[768,512]{1,0:T(8,128)(2,1)}, bf16[768,512]{1,0:T(8,128)(2,1)S(1)}, u32[]{:S(2)}, u32[]{:S(2)}) collective-permute-start(bf16[768,512]{1,0:T(8,128)(2,1)} %get-tuple-element.49), channel_id=1, source_target_pairs={{0,1},{1,0},{2,3},{3,2},{4,5},{5,4},{6,7},{7,6},{8,9},{9,8},{10,11... | collective-permute-start | bytes 2359304 | tf_op jit(solution)/shard_map/ppermute | solution.py:442
  34.7 17.6 %collective-permute-start.1 = (bf16[768,512]{1,0:T(8,128)(2,1)}, bf16[768,512]{1,0:T(8,128)(2,1)S(1)}, u32[]{:S(2)}, u32[]{:S(2)}) collective-permute-start(bf16[768,512]{1,0:T(8,128)(2,1)} %get-tuple-element.50), channel_id=1, source_target_pairs={{0,8},{1,9},{2,10},{3,11},{4,12},{5,13},{6,14},{7,15},{8,0},{9,1},... | collective-permute-start | bytes 2359304 | tf_op jit(solution)/shard_map/ppermute | solution.py:442
  44.7 0.7 copy-start
  45.5 6.9 %copy-start.4 = (bf16[1536,512]{1,0:T(8,128)(2,1)S(1)}, bf16[1536,512]{1,0:T(8,128)(2,1)}, u32[]{:S(2)}) copy-start(bf16[1536,512]{1,0:T(8,128)(2,1)} %get-tuple-element.52.rows0_hbm) | copy-start | bytes 4718596
  45.5 6.9 %copy-start.5 = (bf16[1536,512]{1,0:T(8,128)(2,1)S(1)}, bf16[1536,512]{1,0:T(8,128)(2,1)}, u32[]{:S(2)}) copy-start(bf16[1536,512]{1,0:T(8,128)(2,1)} %get-tuple-element.53.rows1_hbm) | copy-start | bytes 4718596
  48.8 8.6 %collective-permute-start.3 = (bf16[512,512]{1,0:T(8,128)(2,1)}, bf16[512,512]{1,0:T(8,128)(2,1)S(1)}, u32[]{:S(2)}, u32[]{:S(2)}) collective-permute-start(bf16[512,512]{1,0:T(8,128)(2,1)} %get-tuple-element.61.slopes0_ref), channel_id=1, source_target_pairs={{0,1},{1,0},{2,3},{3,2},{4,5},{5,4},{6,7},{7,6},{8,9},{9,8},{10,11... | collective-permute-start | bytes 1572872 | tf_op jit(solution)/shard_map/ppermute | solution.py:442
  49.7 9.5 %collective-permute-start.5 = (bf16[512,512]{1,0:T(8,128)(2,1)}, bf16[512,512]{1,0:T(8,128)(2,1)S(1)}, u32[]{:S(2)}, u32[]{:S(2)}) collective-permute-start(bf16[512,512]{1,0:T(8,128)(2,1)} %get-tuple-element.62.slopes1_ref), channel_id=1, source_target_pairs={{0,8},{1,9},{2,10},{3,11},{4,12},{5,13},{6,14},{7,15},{8,0},{9,1},... | collective-permute-start | bytes 1572872 | tf_op jit(solution)/shard_map/ppermute | solution.py:442
  52.3 1.1 copy-start.2
  53.4 1.0 copy-start.3
  60.1 12.1 %collective-permute-start.6 = (bf16[768,512]{1,0:T(8,128)(2,1)S(1)}, bf16[768,512]{1,0:T(8,128)(2,1)S(1)}, u32[]{:S(2)}, u32[]{:S(2)}) collective-permute-start(bf16[768,512]{1,0:T(8,128)(2,1)S(1)} %get-tuple-element.67), channel_id=1, source_target_pairs={{0,8},{1,9},{2,10},{3,11},{4,12},{5,13},{6,14},{7,15},{8,0},{9,1},... | collective-permute-start | bytes 2359304 | tf_op jit(solution)/shard_map/ppermute | solution.py:442
  62.8 11.1 %collective-permute-start.7 = (bf16[768,512]{1,0:T(8,128)(2,1)S(1)}, bf16[768,512]{1,0:T(8,128)(2,1)S(1)}, u32[]{:S(2)}, u32[]{:S(2)}) collective-permute-start(bf16[768,512]{1,0:T(8,128)(2,1)S(1)} %get-tuple-element.70), channel_id=1, source_target_pairs={{0,1},{1,0},{2,3},{3,2},{4,5},{5,4},{6,7},{7,6},{8,9},{9,8},{10,11... | collective-permute-start | bytes 2359304 | tf_op jit(solution)/shard_map/ppermute | solution.py:442
  74.2 11.0 %collective-permute-start.8 = (bf16[384,512]{1,0:T(8,128)(2,1)S(1)}, bf16[384,512]{1,0:T(8,128)(2,1)S(1)}, u32[]{:S(2)}, u32[]{:S(2)}) collective-permute-start(bf16[384,512]{1,0:T(8,128)(2,1)S(1)} %get-tuple-element.73), channel_id=1, source_target_pairs={{0,2},{1,3},{2,0},{3,1},{4,6},{5,7},{6,4},{7,5},{8,10},{9,11},{10,... | collective-permute-start | bytes 1179656 | tf_op jit(solution)/shard_map/ppermute | solution.py:442
  77.0 12.4 %collective-permute-start.9 = (bf16[384,512]{1,0:T(8,128)(2,1)S(1)}, bf16[384,512]{1,0:T(8,128)(2,1)S(1)}, u32[]{:S(2)}, u32[]{:S(2)}) collective-permute-start(bf16[384,512]{1,0:T(8,128)(2,1)S(1)} %get-tuple-element.75), channel_id=1, source_target_pairs={{0,16},{1,17},{2,18},{3,19},{4,20},{5,21},{6,22},{7,23},{8,24},{9,... | collective-permute-start | bytes 1179656 | tf_op jit(solution)/shard_map/ppermute | solution.py:442
  89.4 11.8 %copy-start.1 = (bf16[32,32,128]{2,1,0:T(8,128)(2,1)S(1)}, bf16[32,32,128]{2,1,0:T(8,128)(2,1)}, u32[]{:S(2)}) copy-start(bf16[32,32,128]{2,1,0:T(8,128)(2,1)} %copy-done) | copy-start | bytes 786436
  89.4 11.8 %copy-start.6 = (f32[512,512]{1,0:T(8,128)S(1)}, f32[512,512]{1,0:T(8,128)}, u32[]{:S(2)}) copy-start(f32[512,512]{1,0:T(8,128)} %get-tuple-element.85.local_ref) | copy-start | bytes 3145732
  89.4 11.9 %copy-start.7 = (bf16[512,512]{1,0:T(8,128)(2,1)S(1)}, bf16[512,512]{1,0:T(8,128)(2,1)}, u32[]{:S(2)}) copy-start(bf16[512,512]{1,0:T(8,128)(2,1)} %get-tuple-element.86.weighted_ref) | copy-start | bytes 1572868
  89.6 7.5 %collective-permute-start.10 = (bf16[192,512]{1,0:T(8,128)(2,1)S(1)}, bf16[192,512]{1,0:T(8,128)(2,1)S(1)}, u32[]{:S(2)}, u32[]{:S(2)}) collective-permute-start(bf16[192,512]{1,0:T(8,128)(2,1)S(1)} %get-tuple-element.77), channel_id=1, source_target_pairs={{0,16},{1,17},{2,18},{3,19},{4,20},{5,21},{6,22},{7,23},{8,24},{9,... | collective-permute-start | bytes 589832 | tf_op jit(solution)/shard_map/ppermute | solution.py:442
  89.7 8.8 %collective-permute-start.11 = (bf16[192,512]{1,0:T(8,128)(2,1)S(1)}, bf16[192,512]{1,0:T(8,128)(2,1)S(1)}, u32[]{:S(2)}, u32[]{:S(2)}) collective-permute-start(bf16[192,512]{1,0:T(8,128)(2,1)S(1)} %get-tuple-element.79), channel_id=1, source_target_pairs={{0,2},{1,3},{2,0},{3,1},{4,6},{5,7},{6,4},{7,5},{8,10},{9,11},{10,... | collective-permute-start | bytes 589832 | tf_op jit(solution)/shard_map/ppermute | solution.py:442
  98.6 14.9 %collective-permute-start.12 = (bf16[96,1024]{1,0:T(8,128)(2,1)S(1)}, bf16[96,1024]{1,0:T(8,128)(2,1)S(1)}, u32[]{:S(2)}, u32[]{:S(2)}) collective-permute-start(bf16[96,1024]{1,0:T(8,128)(2,1)S(1)} %get-tuple-element.81), channel_id=1, source_target_pairs={{0,4},{1,5},{2,6},{3,7},{4,0},{5,1},{6,2},{7,3},{8,12},{9,13},{10,... | collective-permute-start | bytes 589832 | tf_op jit(solution)/shard_map/ppermute | solution.py:442

commit v4 on v3

--- a/solution.py
+++ b/solution.py
@@ -24,9 +24,10 @@
 
 
 def exchange_plan(stream, core):
+    way = 1 - 2 * core
     if stream == 0:
-        return [("z", 1, core), ("y", 1, core), ("z", 2, 2 * core), ("y", 2, 0), ("z", 4, 0)]
-    return [("y", 1, core), ("z", 1, core), ("y", 2, 0), ("z", 2, 2 * core), ("z", 4, 0)]
+        return [("z", way), ("y", way), ("z", -way), ("y", -way), ("z", 3 * way)]
+    return [("y", way), ("z", way), ("y", -way), ("z", -way), ("z", 3 * way)]
 
 
 def rank_of(core, y, z):
@@ -34,10 +35,10 @@
 
 
 def partner_of(kind, core, y, z):
-    axis, distance, offset = kind
+    axis, shift = kind
     if axis == "z":
-        return rank_of(core, y, (((z - offset) ^ distance) + offset) % N_Z)
-    return rank_of(core, (((y - offset) ^ distance) + offset) % N_Y, z)
+        return rank_of(core, y, (z + shift * (1 - 2 * (z % 2))) % N_Z)
+    return rank_of(core, (y + shift * (1 - 2 * (y % 2))) % N_Y, z)
 
 
 def exchange_partners(stream):
@@ -333,14 +334,10 @@
         out[...] = dot(rows[...], slopes[...], (1, 0))
 
 
-def add_kernel(received0_ref, kept0_ref, received1_ref, kept1_ref, keep0_ref, send0_ref, keep1_ref, send1_ref):
-    half = keep0_ref.shape[0]
-    for received, kept, keep, send in (
-        (received0_ref, kept0_ref, keep0_ref, send0_ref),
-        (received1_ref, kept1_ref, keep1_ref, send1_ref),
-    ):
-        keep[...] = kept[:half] + received[:half].astype(F32)
-        send[...] = (kept[half:] + received[half:].astype(F32)).astype(BF16)
+def add_kernel(received_ref, kept_ref, keep_ref, send_ref):
+    half = keep_ref.shape[0]
+    keep_ref[...] = kept_ref[:half] + received_ref[:half].astype(F32)
+    send_ref[...] = (kept_ref[half:] + received_ref[half:].astype(F32)).astype(BF16)
 
 
 def join_kernel(received0_ref, kept0_ref, received1_ref, kept1_ref, keep_ref, send_ref):
@@ -474,20 +471,26 @@
 
     send0, send1 = paired(rows, BF16, late0, late1)
     keep0, keep1 = paired(0, F32, early0, early1, send1[:16, :128])
+    keeps, sends = [keep0, keep1], [send0, send1]
     for step in range(1, STEPS - 1):
-        operands = (exchange(0, step, send0), keep0, exchange(1, step, send1), keep1)
+        received = [exchange(stream, step, sends[stream]) for stream in range(2)]
         rows //= 2
         if step < STEPS - 2:
-            pair = (shaped((rows, columns), F32), shaped((rows, columns), BF16))
-            keep0, send0, keep1, send1 = pl.pallas_call(
-                add_kernel, out_shape=pair + pair, compiler_params=VMEM
-            )(*operands)
+            pairs = [
+                pl.pallas_call(
+                    add_kernel,
+                    out_shape=(shaped((rows, columns), F32), shaped((rows, columns), BF16)),
+                    compiler_params=VMEM,
+                )(received[stream], keeps[stream])
+                for stream in range(2)
+            ]
+            keeps, sends = [one[0] for one in pairs], [one[1] for one in pairs]
         else:
             keep, send = pl.pallas_call(
                 join_kernel,
                 out_shape=(shaped((rows, 2 * columns), F32), shaped((rows, 2 * columns), BF16)),
                 compiler_params=VMEM,
-            )(*operands)
+            )(received[0], keeps[0], received[1], keeps[1])
     assert PARTNERS[0][STEPS - 1] == PARTNERS[1][STEPS - 1]
     received = exchange(0, STEPS - 1, send)
     qweight_grad, kweight_grad = pl.pallas_call(

time: 115 us -> 108 us (0.939)
  the two profiles are of different devices: /device:TPU:39 before, /device:TPU:42 now
where the time goes in v4:
time: 108 us; the launch traced here: 107 us
  waiting for transfers between devices  49.5 us (46%)
  Pallas kernels  27.8 us (26%)
  starting transfers between devices  26.1 us (24%)
  local copies, waits for them, and re-layouts  2.81 us (3%)
    ppermute x13, waiting for transfers between devices, exchange(): return lax.ppermute(array, AXES, sorted(PARTNERS[stream][step].items()))  40.3 us
    all_to_all x1, starting transfers between devices, per_device(): states = lax.all_to_all(states, ('y', 'z'), 0, 0, tiled=True)  11.3 us
    ppermute x13, starting transfers between devices, exchange(): return lax.ppermute(array, AXES, sorted(PARTNERS[stream][step].items()))  9.32 us
    pallas_call x1, Pallas kernels, per_device(): pl.pallas_call(local_kernel, in_specs=[IN_HBM] * 5, out_specs=(IN_HBM,) *...  7.57 us
    all_to_all x1, waiting for transfers between devices, per_device(): states = lax.all_to_all(states, ('y', 'z'), 0, 0, tiled=True)  6.01 us
    pallas_call x1, Pallas kernels, per_device(): pl.pallas_call(arrange_kernel, in_specs=[pl.BlockSpec(memory_space=pltpu....  5.94 us
    all_to_all x1, starting transfers between devices, per_device(): lax.all_to_all(incoming, ('y', 'z'), 0, 0, tiled=True)  5.51 us
    pallas_call x1, Pallas kernels, per_device(): pl.pallas_call(states_kernel, in_specs=[IN_HBM] * 5, out_shape=shaped((SE...  3.66 us
  transfers between devices with their start and end apart: 15, of which 11 were waited for; matrix products, arithmetic and copies ran while one was open for 0% of the time, Pallas kernels for 21%

profile of v4, /device:TPU:42, one launch (start us, length us, event | category | flops | bytes accessed | tf_op | source)
XLA Modules:
  0.0 107.1 jit_solution(17395675931827994879)
XLA Ops:
  0.6 3.7 %shard_map.94 = bf16[32,40,128]{2,1,0:T(8,128)(2,1)} custom-call(f32[4,512]{1,0:T(4,128)} %bitcast.6, bf16[512,512]{1,0:T(8,128)(2,1)} %query_hbm.3, bf16[512,512]{1,0:T(8,128)(2,1)} %key_hbm.3, bf16[512,512]{1,0:T(8,128)(2,1)} %value_hbm.3, bf16[512,512]{1,0:T(8,128)(2,1)} %grad_hbm.3), custom_call_target="tpu_custom_call" | custom-call | flops 1000000000 | bytes 4000000 | tf_op jit(solution)/shard_map/pallas_call | solution.py:390
  4.3 11.3 %all-to-all-start = ((bf16[32,40,128]{2,1,0:T(8,128)(2,1)}), bf16[32,40,128]{2,1,0:T(8,128)(2,1)S(1)}, u32[]{:S(2)}, u32[]{:S(2)}) async-start(bf16[32,40,128]{2,1,0:T(8,128)(2,1)} %shard_map.94), calls=%async_computation | async-start | bytes 655360 | tf_op jit(solution)/shard_map/all_to_all | solution.py:398
  15.6 5.9 %shard_map.95 = (bf16[768,512]{1,0:T(8,128)(2,1)}, bf16[768,512]{1,0:T(8,128)(2,1)}, bf16[768,512]{1,0:T(8,128)(2,1)}, bf16[768,512]{1,0:T(8,128)(2,1)}, bf16[15...) custom-call(s32[1]{0:T(128)} %bitcast.2.place_ref, s32[4096]{0:T(1024)} %constant.20.clone.table_ref, ...), custom_call_target="tpu_custom_call" | custom-call | flops 1000000000 | bytes 10000000 | tf_op jit(solution)/shard_map/pallas_call | solution.py:416
  21.5 0.7 collective-permute-start.2
  22.4 6.0 %all-to-all-done.in_ref = bf16[32,40,128]{2,1,0:T(8,128)(2,1)S(1)} async-done(((bf16[32,40,128]{2,1,0:T(8,128)(2,1)}), bf16[32,40,128]{2,1,0:T(8,128)(2,1)S(1)}, u32[]{:S(2)}, u32[]{:S(2)}) %all-to-all-start) | async-done | bytes 327712 | tf_op jit(solution)/shard_map/all_to_all | solution.py:398
  28.4 0.9 shard_map.96
  29.3 5.5 %all-to-all-start.1 = ((bf16[32,32,128]{2,1,0:T(8,128)(2,1)}), bf16[32,32,128]{2,1,0:T(8,128)(2,1)S(1)}, u32[]{:S(2)}, u32[]{:S(2)}) async-start(bf16[32,32,128]{2,1,0:T(8,128)(2,1)} %shard_map.96), calls=%async_computation.1 | async-start | bytes 524288 | tf_op jit(solution)/shard_map/all_to_all | solution.py:435
  34.8 0.7 collective-permute-start
  35.7 7.6 %shard_map.97 = (bf16[512,512]{1,0:T(8,128)(2,1)}, bf16[512,512]{1,0:T(8,128)(2,1)}, f32[512,512]{1,0:T(8,128)}, bf16[512,512]{1,0:T(8,128)(2,1)}, bf16[512,512]...) custom-call(f32[4,512]{1,0:T(4,128)} %bitcast.7, ...), custom_call_target="tpu_custom_call" | custom-call | flops 60000002048 | bytes 10000000 | tf_op jit(solution)/shard_map/pallas_call | solution.py:400
  43.3 3.3 %all-to-all-done.1 = bf16[32,32,128]{2,1,0:T(8,128)(2,1)S(1)} async-done(((bf16[32,32,128]{2,1,0:T(8,128)(2,1)}), bf16[32,32,128]{2,1,0:T(8,128)(2,1)S(1)}, u32[]{:S(2)}, u32[]{:S(2)}) %all-to-all-start.1) | async-done | bytes 262176 | tf_op jit(solution)/shard_map/all_to_all | solution.py:435
  46.6 0.7 copy-done
  47.3 3.3 %shard_map.98 = (bf16[512,512]{1,0:T(8,128)(2,1)}, bf16[512,512]{1,0:T(8,128)(2,1)}) custom-call(bf16[1024,128]{1,0:T(8,128)(2,1)} %bitcast.4, bf16[512,512]{1,0:T(8,128)(2,1)} %get-tuple-element.55.wo_hbm, bf16[512,512]{1,0:T(8,128)(2,1)} %get-tuple-element.56.gq_hbm, bf16[512,512]{1,0:T(8,128)(2,1)} %get-tuple-element.57.sq_hbm, ...), custom_call_target="tpu_custom_call" | custom-call | flops 1000000000 | bytes 4000000 | tf_op jit(solution)/shard_map/pallas_call | solution.py:444
  50.7 2.4 %collective-permute-start.5 = (bf16[512,512]{1,0:T(8,128)(2,1)}, bf16[512,512]{1,0:T(8,128)(2,1)S(1)}, u32[]{:S(2)}, u32[]{:S(2)}) collective-permute-start(bf16[512,512]{1,0:T(8,128)(2,1)} %get-tuple-element.62.slopes1_ref), channel_id=1, source_target_pairs={{0,8},{1,9},{2,10},{3,11},{4,12},{5,13},{6,14},{7,15},{8,0},{9,1},... | collective-permute-start | bytes 1572872 | tf_op jit(solution)/shard_map/ppermute | solution.py:439
  53.1 1.1 copy-done.2
  54.2 1.0 copy-done.3
  55.2 2.2 %shard_map.99 = (f32[1536,512]{1,0:T(8,128)S(1)}, f32[1536,512]{1,0:T(8,128)S(1)}) custom-call(bf16[1536,512]{1,0:T(8,128)(2,1)S(1)} %copy-done.4, bf16[1536,512]{1,0:T(8,128)(2,1)S(1)} %copy-done.5, bf16[512,512]{1,0:T(8,128)(2,1)S(1)} %copy-done.3, bf16[512,512]{1,0:T(8,128)(2,1)S(1)} %copy-done.2), custom_call_target="tpu_custom_call" | custom-call | flops 1610612736 | bytes 10000000 | tf_op jit(solution)/shard_map/pallas_call | solution.py:453
  57.4 2.6 %collective-permute-done.3.slopes0_ref = bf16[512,512]{1,0:T(8,128)(2,1)S(1)} collective-permute-done((bf16[512,512]{1,0:T(8,128)(2,1)}, bf16[512,512]{1,0:T(8,128)(2,1)S(1)}, u32[]{:S(2)}, u32[]{:S(2)}) %collective-permute-start.3) | collective-permute-done | bytes 524320 | tf_op jit(solution)/shard_map/ppermute | solution.py:439
  60.5 1.0 shard_map.100
  61.4 2.1 %collective-permute-start.6 = (bf16[768,512]{1,0:T(8,128)(2,1)S(1)}, bf16[768,512]{1,0:T(8,128)(2,1)S(1)}, u32[]{:S(2)}, u32[]{:S(2)}) collective-permute-start(bf16[768,512]{1,0:T(8,128)(2,1)S(1)} %get-tuple-element.67), channel_id=1, source_target_pairs={{0,8},{1,9},{2,10},{3,11},{4,12},{5,13},{6,14},{7,15},{8,0},{9,1},... | collective-permute-start | bytes 2359304 | tf_op jit(solution)/shard_map/ppermute | solution.py:439
  63.6 1.0 collective-permute-start.9
  64.5 1.0 shard_map.101
  65.5 8.0 %collective-permute-done.6.received_ref = bf16[768,512]{1,0:T(8,128)(2,1)S(1)} collective-permute-done((bf16[768,512]{1,0:T(8,128)(2,1)S(1)}, bf16[768,512]{1,0:T(8,128)(2,1)S(1)}, u32[]{:S(2)}, u32[]{:S(2)}) %collective-permute-start.6) | collective-permute-done | bytes 786464 | tf_op jit(solution)/shard_map/ppermute | solution.py:439
  73.7 0.9 collective-permute-start.7
  74.5 3.3 %collective-permute-done.9.received_ref = bf16[768,512]{1,0:T(8,128)(2,1)S(1)} collective-permute-done((bf16[768,512]{1,0:T(8,128)(2,1)S(1)}, bf16[768,512]{1,0:T(8,128)(2,1)S(1)}, u32[]{:S(2)}, u32[]{:S(2)}) %collective-permute-start.9) | collective-permute-done | bytes 786464 | tf_op jit(solution)/shard_map/ppermute | solution.py:439
  78.1 3.4 %collective-permute-done.7.received_ref = bf16[384,512]{1,0:T(8,128)(2,1)S(1)} collective-permute-done((bf16[384,512]{1,0:T(8,128)(2,1)S(1)}, bf16[384,512]{1,0:T(8,128)(2,1)S(1)}, u32[]{:S(2)}, u32[]{:S(2)}) %collective-permute-start.7) | collective-permute-done | bytes 393248 | tf_op jit(solution)/shard_map/ppermute | solution.py:439
  81.6 0.8 collective-permute-start.8
  82.4 3.4 %collective-permute-done.10.received_ref = bf16[384,512]{1,0:T(8,128)(2,1)S(1)} collective-permute-done((bf16[384,512]{1,0:T(8,128)(2,1)S(1)}, bf16[384,512]{1,0:T(8,128)(2,1)S(1)}, u32[]{:S(2)}, u32[]{:S(2)}) %collective-permute-start.10) | collective-permute-done | bytes 393248 | tf_op jit(solution)/shard_map/ppermute | solution.py:439
  86.0 1.9 %collective-permute-done.8.received0_ref = bf16[192,512]{1,0:T(8,128)(2,1)S(1)} collective-permute-done((bf16[192,512]{1,0:T(8,128)(2,1)S(1)}, bf16[192,512]{1,0:T(8,128)(2,1)S(1)}, u32[]{:S(2)}, u32[]{:S(2)}) %collective-permute-start.8) | collective-permute-done | bytes 196640 | tf_op jit(solution)/shard_map/ppermute | solution.py:439
  88.0 7.5 %collective-permute-done.11.received1_ref = bf16[192,512]{1,0:T(8,128)(2,1)S(1)} collective-permute-done((bf16[192,512]{1,0:T(8,128)(2,1)S(1)}, bf16[192,512]{1,0:T(8,128)(2,1)S(1)}, u32[]{:S(2)}, u32[]{:S(2)}) %collective-permute-start.11) | collective-permute-done | bytes 196640 | tf_op jit(solution)/shard_map/ppermute | solution.py:439
  95.7 1.1 %shard_map.108 = bf16[512,512]{1,0:T(8,128)(2,1)} custom-call(f32[512,512]{1,0:T(8,128)S(1)} %copy-done.6, bf16[512,512]{1,0:T(8,128)(2,1)S(1)} %copy-done.7, bf16[1024,128]{1,0:T(8,128)(2,1)S(1)} %bitcast.5), custom_call_target="tpu_custom_call" | custom-call | flops 1000000000 | bytes 5000000 | tf_op jit(solution)/shard_map/pallas_call | solution.py:499
  96.7 9.6 %collective-permute-done.12.received_ref = bf16[96,1024]{1,0:T(8,128)(2,1)S(1)} collective-permute-done((bf16[96,1024]{1,0:T(8,128)(2,1)S(1)}, bf16[96,1024]{1,0:T(8,128)(2,1)S(1)}, u32[]{:S(2)}, u32[]{:S(2)}) %collective-permute-start.12) | collective-permute-done | bytes 196640 | tf_op jit(solution)/shard_map/ppermute | solution.py:439
  106.3 0.8 shard_map.107
  (30 shorter events, 1.8 us)
Async XLA Ops:
  4.3 24.1 %all-to-all-start = ((bf16[32,40,128]{2,1,0:T(8,128)(2,1)}), bf16[32,40,128]{2,1,0:T(8,128)(2,1)S(1)}, u32[]{:S(2)}, u32[]{:S(2)}) async-start(bf16[32,40,128]{2,1,0:T(8,128)(2,1)} %shard_map.94), calls=%async_computation | async-start | bytes 655360 | tf_op jit(solution)/shard_map/all_to_all | solution.py:398
  21.5 35.9 %collective-permute-start.2 = (bf16[768,512]{1,0:T(8,128)(2,1)}, bf16[768,512]{1,0:T(8,128)(2,1)S(1)}, u32[]{:S(2)}, u32[]{:S(2)}) collective-permute-start(bf16[768,512]{1,0:T(8,128)(2,1)} %get-tuple-element.64), channel_id=1, source_target_pairs={{0,1},{1,0},{2,3},{3,2},{4,5},{5,4},{6,7},{7,6},{8,9},{9,8},{10,11... | collective-permute-start | bytes 2359304 | tf_op jit(solution)/shard_map/ppermute | solution.py:439
  22.2 35.3 %collective-permute-start.4 = (bf16[768,512]{1,0:T(8,128)(2,1)}, bf16[768,512]{1,0:T(8,128)(2,1)S(1)}, u32[]{:S(2)}, u32[]{:S(2)}) collective-permute-start(bf16[768,512]{1,0:T(8,128)(2,1)} %get-tuple-element.66), channel_id=1, source_target_pairs={{0,8},{1,9},{2,10},{3,11},{4,12},{5,13},{6,14},{7,15},{8,0},{9,1},... | collective-permute-start | bytes 2359304 | tf_op jit(solution)/shard_map/ppermute | solution.py:439
  29.3 17.2 %all-to-all-start.1 = ((bf16[32,32,128]{2,1,0:T(8,128)(2,1)}), bf16[32,32,128]{2,1,0:T(8,128)(2,1)S(1)}, u32[]{:S(2)}, u32[]{:S(2)}) async-start(bf16[32,32,128]{2,1,0:T(8,128)(2,1)} %shard_map.96), calls=%async_computation.1 | async-start | bytes 524288 | tf_op jit(solution)/shard_map/all_to_all | solution.py:435
  34.8 15.8 %collective-permute-start = (bf16[768,512]{1,0:T(8,128)(2,1)}, bf16[768,512]{1,0:T(8,128)(2,1)S(1)}, u32[]{:S(2)}, u32[]{:S(2)}) collective-permute-start(bf16[768,512]{1,0:T(8,128)(2,1)} %get-tuple-element.49), channel_id=1, source_target_pairs={{0,1},{1,0},{2,3},{3,2},{4,5},{5,4},{6,7},{7,6},{8,9},{9,8},{10,11... | collective-permute-start | bytes 2359304 | tf_op jit(solution)/shard_map/ppermute | solution.py:439
  35.5 17.6 %collective-permute-start.1 = (bf16[768,512]{1,0:T(8,128)(2,1)}, bf16[768,512]{1,0:T(8,128)(2,1)S(1)}, u32[]{:S(2)}, u32[]{:S(2)}) collective-permute-start(bf16[768,512]{1,0:T(8,128)(2,1)} %get-tuple-element.50), channel_id=1, source_target_pairs={{0,8},{1,9},{2,10},{3,11},{4,12},{5,13},{6,14},{7,15},{8,0},{9,1},... | collective-permute-start | bytes 2359304 | tf_op jit(solution)/shard_map/ppermute | solution.py:439
  46.6 0.7 copy-start
  47.3 5.8 %copy-start.4 = (bf16[1536,512]{1,0:T(8,128)(2,1)S(1)}, bf16[1536,512]{1,0:T(8,128)(2,1)}, u32[]{:S(2)}) copy-start(bf16[1536,512]{1,0:T(8,128)(2,1)} %get-tuple-element.52.rows0_hbm) | copy-start | bytes 4718596
  47.3 5.8 %copy-start.5 = (bf16[1536,512]{1,0:T(8,128)(2,1)S(1)}, bf16[1536,512]{1,0:T(8,128)(2,1)}, u32[]{:S(2)}) copy-start(bf16[1536,512]{1,0:T(8,128)(2,1)} %get-tuple-element.53.rows1_hbm) | copy-start | bytes 4718596
  50.6 9.5 %collective-permute-start.3 = (bf16[512,512]{1,0:T(8,128)(2,1)}, bf16[512,512]{1,0:T(8,128)(2,1)S(1)}, u32[]{:S(2)}, u32[]{:S(2)}) collective-permute-start(bf16[512,512]{1,0:T(8,128)(2,1)} %get-tuple-element.61.slopes0_ref), channel_id=1, source_target_pairs={{0,1},{1,0},{2,3},{3,2},{4,5},{5,4},{6,7},{7,6},{8,9},{9,8},{10,11... | collective-permute-start | bytes 1572872 | tf_op jit(solution)/shard_map/ppermute | solution.py:439
  50.7 9.8 %collective-permute-start.5 = (bf16[512,512]{1,0:T(8,128)(2,1)}, bf16[512,512]{1,0:T(8,128)(2,1)S(1)}, u32[]{:S(2)}, u32[]{:S(2)}) collective-permute-start(bf16[512,512]{1,0:T(8,128)(2,1)} %get-tuple-element.62.slopes1_ref), channel_id=1, source_target_pairs={{0,8},{1,9},{2,10},{3,11},{4,12},{5,13},{6,14},{7,15},{8,0},{9,1},... | collective-permute-start | bytes 1572872 | tf_op jit(solution)/shard_map/ppermute | solution.py:439
  53.1 1.1 copy-start.2
  54.2 1.0 copy-start.3
  61.4 12.1 %collective-permute-start.6 = (bf16[768,512]{1,0:T(8,128)(2,1)S(1)}, bf16[768,512]{1,0:T(8,128)(2,1)S(1)}, u32[]{:S(2)}, u32[]{:S(2)}) collective-permute-start(bf16[768,512]{1,0:T(8,128)(2,1)S(1)} %get-tuple-element.67), channel_id=1, source_target_pairs={{0,8},{1,9},{2,10},{3,11},{4,12},{5,13},{6,14},{7,15},{8,0},{9,1},... | collective-permute-start | bytes 2359304 | tf_op jit(solution)/shard_map/ppermute | solution.py:439
  63.6 14.3 %collective-permute-start.9 = (bf16[768,512]{1,0:T(8,128)(2,1)S(1)}, bf16[768,512]{1,0:T(8,128)(2,1)S(1)}, u32[]{:S(2)}, u32[]{:S(2)}) collective-permute-start(bf16[768,512]{1,0:T(8,128)(2,1)S(1)} %get-tuple-element.70), channel_id=1, source_target_pairs={{0,1},{1,0},{2,3},{3,2},{4,5},{5,4},{6,7},{7,6},{8,9},{9,8},{10,11... | collective-permute-start | bytes 2359304 | tf_op jit(solution)/shard_map/ppermute | solution.py:439
  73.7 7.9 %collective-permute-start.7 = (bf16[384,512]{1,0:T(8,128)(2,1)S(1)}, bf16[384,512]{1,0:T(8,128)(2,1)S(1)}, u32[]{:S(2)}, u32[]{:S(2)}) collective-permute-start(bf16[384,512]{1,0:T(8,128)(2,1)S(1)} %get-tuple-element.72), channel_id=1, source_target_pairs={{0,7},{1,2},{2,1},{3,4},{4,3},{5,6},{6,5},{7,0},{8,15},{9,10},{10,... | collective-permute-start | bytes 1179656 | tf_op jit(solution)/shard_map/ppermute | solution.py:439
  78.0 7.9 %collective-permute-start.10 = (bf16[384,512]{1,0:T(8,128)(2,1)S(1)}, bf16[384,512]{1,0:T(8,128)(2,1)S(1)}, u32[]{:S(2)}, u32[]{:S(2)}) collective-permute-start(bf16[384,512]{1,0:T(8,128)(2,1)S(1)} %get-tuple-element.77), channel_id=1, source_target_pairs={{0,24},{1,25},{2,26},{3,27},{4,28},{5,29},{6,30},{7,31},{8,16},{9,... | collective-permute-start | bytes 1179656 | tf_op jit(solution)/shard_map/ppermute | solution.py:439
  81.5 14.1 %copy-start.1 = (bf16[32,32,128]{2,1,0:T(8,128)(2,1)S(1)}, bf16[32,32,128]{2,1,0:T(8,128)(2,1)}, u32[]{:S(2)}) copy-start(bf16[32,32,128]{2,1,0:T(8,128)(2,1)} %copy-done) | copy-start | bytes 786436
  81.5 14.1 %copy-start.6 = (f32[512,512]{1,0:T(8,128)S(1)}, f32[512,512]{1,0:T(8,128)}, u32[]{:S(2)}) copy-start(f32[512,512]{1,0:T(8,128)} %get-tuple-element.85.local_ref) | copy-start | bytes 3145732
  81.5 14.1 %copy-start.7 = (bf16[512,512]{1,0:T(8,128)(2,1)S(1)}, bf16[512,512]{1,0:T(8,128)(2,1)}, u32[]{:S(2)}) copy-start(bf16[512,512]{1,0:T(8,128)(2,1)} %get-tuple-element.86.weighted_ref) | copy-start | bytes 1572868
  81.6 6.4 %collective-permute-start.8 = (bf16[192,512]{1,0:T(8,128)(2,1)S(1)}, bf16[192,512]{1,0:T(8,128)(2,1)S(1)}, u32[]{:S(2)}, u32[]{:S(2)}) collective-permute-start(bf16[192,512]{1,0:T(8,128)(2,1)S(1)} %get-tuple-element.74), channel_id=1, source_target_pairs={{0,24},{1,25},{2,26},{3,27},{4,28},{5,29},{6,30},{7,31},{8,16},{9,... | collective-permute-start | bytes 589832 | tf_op jit(solution)/shard_map/ppermute | solution.py:439
  85.9 9.5 %collective-permute-start.11 = (bf16[192,512]{1,0:T(8,128)(2,1)S(1)}, bf16[192,512]{1,0:T(8,128)(2,1)S(1)}, u32[]{:S(2)}, u32[]{:S(2)}) collective-permute-start(bf16[192,512]{1,0:T(8,128)(2,1)S(1)} %get-tuple-element.79), channel_id=1, source_target_pairs={{0,7},{1,2},{2,1},{3,4},{4,3},{5,6},{6,5},{7,0},{8,15},{9,10},{10,... | collective-permute-start | bytes 589832 | tf_op jit(solution)/shard_map/ppermute | solution.py:439
  95.5 10.8 %collective-permute-start.12 = (bf16[96,1024]{1,0:T(8,128)(2,1)S(1)}, bf16[96,1024]{1,0:T(8,128)(2,1)S(1)}, u32[]{:S(2)}, u32[]{:S(2)}) collective-permute-start(bf16[96,1024]{1,0:T(8,128)(2,1)S(1)} %get-tuple-element.81), channel_id=1, source_target_pairs={{0,3},{1,6},{2,5},{3,0},{4,7},{5,2},{6,1},{7,4},{8,11},{9,14},{10,... | collective-permute-start | bytes 589832 | tf_op jit(solution)/shard_map/ppermute | solution.py:439

commit v5 on v4

--- a/solution.py
+++ b/solution.py
@@ -273,14 +273,10 @@
             slopes[:, part] = (gradient * slope[:, part].astype(F32)).astype(BF16)
 
 
-def pair_kernel(own0_ref, rows0_ref, slopes0_ref, own1_ref, rows1_ref, slopes1_ref, *refs, first):
-    out0_ref, out1_ref = refs[-2:]
-    part = slice(first, first + out0_ref.shape[0])
-    for own, rows, slopes, out in (
-        (own0_ref, rows0_ref, slopes0_ref, out0_ref),
-        (own1_ref, rows1_ref, slopes1_ref, out1_ref),
-    ):
-        out[...] = (own[part] + dot(rows[...], slopes[...], (1, 0))).astype(out.dtype)
+def pair_kernel(own_ref, rows_ref, slopes_ref, *refs, first):
+    out_ref = refs[-1]
+    part = slice(first, first + out_ref.shape[0])
+    out_ref[...] = (own_ref[part] + dot(rows_ref[...], slopes_ref[...], (1, 0))).astype(out_ref.dtype)
 
 
 def values_kernel(local_ref, weighted_ref, states_ref, out_ref):
@@ -340,19 +336,8 @@
     send_ref[...] = (kept_ref[half:] + received_ref[half:].astype(F32)).astype(BF16)
 
 
-def join_kernel(received0_ref, kept0_ref, received1_ref, kept1_ref, keep_ref, send_ref):
-    half, columns = keep_ref.shape[0], kept0_ref.shape[1]
-    for stream, (received, kept) in enumerate(((received0_ref, kept0_ref), (received1_ref, kept1_ref))):
-        part = slice(stream * columns, (stream + 1) * columns)
-        keep_ref[:, part] = kept[:half] + received[:half].astype(F32)
-        send_ref[:, part] = (kept[half:] + received[half:].astype(F32)).astype(BF16)
-
-
-def last_kernel(received_ref, kept_ref, out0_ref, out1_ref):
-    columns = out0_ref.shape[1]
-    for stream, out in enumerate((out0_ref, out1_ref)):
-        part = slice(stream * columns, (stream + 1) * columns)
-        out[...] = kept_ref[:, part] + received_ref[:, part].astype(F32)
+def last_one_kernel(received_ref, kept_ref, mark_ref, out_ref):
+    out_ref[...] = kept_ref[...] + received_ref[...].astype(F32)
 
 
 def shaped(shape, dtype):
@@ -460,17 +445,20 @@
     )(kept0, kept1, slopes_q, slopes_k)
     rows = half // 2
 
-    def paired(first, dtype, other0, other1, *after):
+    def paired(first, dtype, *operands):
         return pl.pallas_call(
             functools.partial(pair_kernel, first=first),
-            in_specs=[IN_VMEM] * 6 + [IN_HBM] * len(after),
-            out_shape=(shaped((rows, columns), dtype),) * 2,
+            in_specs=[IN_VMEM] * 3 + [IN_HBM] * (len(operands) - 3),
+            out_shape=shaped((rows, columns), dtype),
             compiler_params=VMEM,
-            cost_estimate=cost(flops, 6 * 10**6),
-        )(own0, other0, partner_q, own1, other1, partner_k, *after)
-
-    send0, send1 = paired(rows, BF16, late0, late1)
-    keep0, keep1 = paired(0, F32, early0, early1, send1[:16, :128])
+            cost_estimate=cost(flops // 2, 3 * 10**6),
+        )(*operands)
+
+    send0 = paired(rows, BF16, own0, late0, partner_q)
+    send1 = paired(rows, BF16, own1, late1, partner_k)
+    after = send1[:16, :128]
+    keep0 = paired(0, F32, own0, early0, partner_q, after)
+    keep1 = paired(0, F32, own1, early1, partner_k, after)
     keeps, sends = [keep0, keep1], [send0, send1]
     for step in range(1, STEPS - 1):
         received = [exchange(stream, step, sends[stream]) for stream in range(2)]
@@ -486,16 +474,28 @@
             ]
             keeps, sends = [one[0] for one in pairs], [one[1] for one in pairs]
         else:
-            keep, send = pl.pallas_call(
-                join_kernel,
-                out_shape=(shaped((rows, 2 * columns), F32), shaped((rows, 2 * columns), BF16)),
-                compiler_params=VMEM,
-            )(received[0], keeps[0], received[1], keeps[1])
-    assert PARTNERS[0][STEPS - 1] == PARTNERS[1][STEPS - 1]
-    received = exchange(0, STEPS - 1, send)
-    qweight_grad, kweight_grad = pl.pallas_call(
-        last_kernel, out_shape=(shaped((rows, columns), F32),) * 2, compiler_params=VMEM
-    )(received, keep)
+            pairs = [
+                pl.pallas_call(
+                    add_kernel,
+                    out_shape=(shaped((rows, columns), F32), shaped((rows, columns), BF16)),
+                    compiler_params=VMEM,
+                )(received[stream], keeps[stream])
+                for stream in range(2)
+            ]
+            keeps, sends = [one[0] for one in pairs], [one[1] for one in pairs]
+    other_core = [(rank, (rank + SEQ) % RANKS) for rank in range(RANKS)]
+    mark = lax.ppermute(sends[1][:16, :128], AXES, other_core)
+    gated, mark = lax.optimization_barrier((sends[0], mark))
+    sends = (gated, sends[1], mark)
+    qweight_grad, kweight_grad = [
+        pl.pallas_call(
+            last_one_kernel,
+            in_specs=[IN_VMEM, IN_VMEM, pl.BlockSpec(memory_space=pl.ANY)],
+            out_shape=shaped((rows, columns), F32),
+            compiler_params=VMEM,
+        )(exchange(stream, STEPS - 1, sends[stream]), keeps[stream], sends[2])
+        for stream in range(2)
+    ]
     value_grad = pl.pallas_call(
         values_kernel,
         out_shape=small,

time: 108 us -> 104 us (0.963)
  the two profiles are of different devices: /device:TPU:42 before, /device:TPU:4 now
where the time goes in v5:
time: 104 us; the launch traced here: 103 us
  waiting for transfers between devices  36.9 us (35%)
  starting transfers between devices  33.3 us (32%)
  Pallas kernels  28.8 us (28%)
  local copies, waits for them, and re-layouts  2.81 us (3%)
    ppermute x14, waiting for transfers between devices, exchange(): return lax.ppermute(array, AXES, sorted(PARTNERS[stream][step].items()))  30.2 us
    ppermute x14, starting transfers between devices, exchange(): return lax.ppermute(array, AXES, sorted(PARTNERS[stream][step].items()))  16.9 us
    all_to_all x1, starting transfers between devices, per_device(): states = lax.all_to_all(states, ('y', 'z'), 0, 0, tiled=True)  11.5 us
    pallas_call x1, Pallas kernels, per_device(): pl.pallas_call(local_kernel, in_specs=[IN_HBM] * 5, out_specs=(IN_HBM,) *...  7.57 us
    pallas_call x1, Pallas kernels, per_device(): pl.pallas_call(arrange_kernel, in_specs=[pl.BlockSpec(memory_space=pltpu....  5.94 us
    all_to_all x1, starting transfers between devices, per_device(): lax.all_to_all(incoming, ('y', 'z'), 0, 0, tiled=True)  4.8 us
    all_to_all x1, waiting for transfers between devices, per_device(): states = lax.all_to_all(states, ('y', 'z'), 0, 0, tiled=True)  4.26 us
    pallas_call x1, Pallas kernels, per_device(): pl.pallas_call(states_kernel, in_specs=[IN_HBM] * 5, out_shape=shaped((SE...  3.66 us
  transfers between devices with their start and end apart: 17, of which 11 were waited for; matrix products, arithmetic and copies ran while one was open for 0% of the time, Pallas kernels for 24%

profile of v5, /device:TPU:4, one launch (start us, length us, event | category | flops | bytes accessed | tf_op | source)
XLA Modules:
  0.0 102.7 jit_solution(12231349996946287079)
XLA Ops:
  0.6 3.7 %shard_map.94 = bf16[32,40,128]{2,1,0:T(8,128)(2,1)} custom-call(f32[4,512]{1,0:T(4,128)} %bitcast.6, bf16[512,512]{1,0:T(8,128)(2,1)} %query_hbm.3, bf16[512,512]{1,0:T(8,128)(2,1)} %key_hbm.3, bf16[512,512]{1,0:T(8,128)(2,1)} %value_hbm.3, bf16[512,512]{1,0:T(8,128)(2,1)} %grad_hbm.3), custom_call_target="tpu_custom_call" | custom-call | flops 1000000000 | bytes 4000000 | tf_op jit(solution)/shard_map/pallas_call | solution.py:375
  4.3 11.5 %all-to-all-start = ((bf16[32,40,128]{2,1,0:T(8,128)(2,1)}), bf16[32,40,128]{2,1,0:T(8,128)(2,1)S(1)}, u32[]{:S(2)}, u32[]{:S(2)}) async-start(bf16[32,40,128]{2,1,0:T(8,128)(2,1)} %shard_map.94), calls=%async_computation | async-start | bytes 655360 | tf_op jit(solution)/shard_map/all_to_all | solution.py:383
  15.8 5.9 %shard_map.95 = (bf16[768,512]{1,0:T(8,128)(2,1)}, bf16[768,512]{1,0:T(8,128)(2,1)}, bf16[768,512]{1,0:T(8,128)(2,1)}, bf16[768,512]{1,0:T(8,128)(2,1)}, bf16[15...) custom-call(s32[1]{0:T(128)} %bitcast.2.place_ref, s32[4096]{0:T(1024)} %constant.20.clone.table_ref, ...), custom_call_target="tpu_custom_call" | custom-call | flops 1000000000 | bytes 10000000 | tf_op jit(solution)/shard_map/pallas_call | solution.py:401
  21.8 1.9 %collective-permute-start.2 = (bf16[768,512]{1,0:T(8,128)(2,1)}, bf16[768,512]{1,0:T(8,128)(2,1)S(1)}, u32[]{:S(2)}, u32[]{:S(2)}) collective-permute-start(bf16[768,512]{1,0:T(8,128)(2,1)} %get-tuple-element.62), channel_id=1, source_target_pairs={{0,1},{1,0},{2,3},{3,2},{4,5},{5,4},{6,7},{7,6},{8,9},{9,8},{10,11... | collective-permute-start | bytes 2359304 | tf_op jit(solution)/shard_map/ppermute | solution.py:424
  23.6 1.5 %collective-permute-start.5 = (bf16[768,512]{1,0:T(8,128)(2,1)}, bf16[768,512]{1,0:T(8,128)(2,1)S(1)}, u32[]{:S(2)}, u32[]{:S(2)}) collective-permute-start(bf16[768,512]{1,0:T(8,128)(2,1)} %get-tuple-element.65), channel_id=1, source_target_pairs={{0,8},{1,9},{2,10},{3,11},{4,12},{5,13},{6,14},{7,15},{8,0},{9,1},... | collective-permute-start | bytes 2359304 | tf_op jit(solution)/shard_map/ppermute | solution.py:424
  25.1 4.3 %all-to-all-done.in_ref = bf16[32,40,128]{2,1,0:T(8,128)(2,1)S(1)} async-done(((bf16[32,40,128]{2,1,0:T(8,128)(2,1)}), bf16[32,40,128]{2,1,0:T(8,128)(2,1)S(1)}, u32[]{:S(2)}, u32[]{:S(2)}) %all-to-all-start) | async-done | bytes 327712 | tf_op jit(solution)/shard_map/all_to_all | solution.py:383
  29.4 0.9 shard_map.96
  30.3 4.8 %all-to-all-start.1 = ((bf16[32,32,128]{2,1,0:T(8,128)(2,1)}), bf16[32,32,128]{2,1,0:T(8,128)(2,1)S(1)}, u32[]{:S(2)}, u32[]{:S(2)}) async-start(bf16[32,32,128]{2,1,0:T(8,128)(2,1)} %shard_map.96), calls=%async_computation.1 | async-start | bytes 524288 | tf_op jit(solution)/shard_map/all_to_all | solution.py:420
  35.1 1.9 %collective-permute-start = (bf16[768,512]{1,0:T(8,128)(2,1)}, bf16[768,512]{1,0:T(8,128)(2,1)S(1)}, u32[]{:S(2)}, u32[]{:S(2)}) collective-permute-start(bf16[768,512]{1,0:T(8,128)(2,1)} %get-tuple-element.47), channel_id=1, source_target_pairs={{0,1},{1,0},{2,3},{3,2},{4,5},{5,4},{6,7},{7,6},{8,9},{9,8},{10,11... | collective-permute-start | bytes 2359304 | tf_op jit(solution)/shard_map/ppermute | solution.py:424
  37.0 1.5 %collective-permute-start.1 = (bf16[768,512]{1,0:T(8,128)(2,1)}, bf16[768,512]{1,0:T(8,128)(2,1)S(1)}, u32[]{:S(2)}, u32[]{:S(2)}) collective-permute-start(bf16[768,512]{1,0:T(8,128)(2,1)} %get-tuple-element.48), channel_id=1, source_target_pairs={{0,8},{1,9},{2,10},{3,11},{4,12},{5,13},{6,14},{7,15},{8,0},{9,1},... | collective-permute-start | bytes 2359304 | tf_op jit(solution)/shard_map/ppermute | solution.py:424
  38.4 7.6 %shard_map.97 = (bf16[512,512]{1,0:T(8,128)(2,1)}, bf16[512,512]{1,0:T(8,128)(2,1)}, f32[512,512]{1,0:T(8,128)}, bf16[512,512]{1,0:T(8,128)(2,1)}, bf16[512,512]...) custom-call(f32[4,512]{1,0:T(4,128)} %bitcast.7, ...), custom_call_target="tpu_custom_call" | custom-call | flops 60000002048 | bytes 10000000 | tf_op jit(solution)/shard_map/pallas_call | solution.py:385
  46.0 2.5 %all-to-all-done.1 = bf16[32,32,128]{2,1,0:T(8,128)(2,1)S(1)} async-done(((bf16[32,32,128]{2,1,0:T(8,128)(2,1)}), bf16[32,32,128]{2,1,0:T(8,128)(2,1)S(1)}, u32[]{:S(2)}, u32[]{:S(2)}) %all-to-all-start.1) | async-done | bytes 262176 | tf_op jit(solution)/shard_map/all_to_all | solution.py:420
  49.1 3.3 %shard_map.98 = (bf16[512,512]{1,0:T(8,128)(2,1)}, bf16[512,512]{1,0:T(8,128)(2,1)}) custom-call(bf16[1024,128]{1,0:T(8,128)(2,1)} %bitcast.4, bf16[512,512]{1,0:T(8,128)(2,1)} %get-tuple-element.53.wo_hbm, bf16[512,512]{1,0:T(8,128)(2,1)} %get-tuple-element.54.gq_hbm, bf16[512,512]{1,0:T(8,128)(2,1)} %get-tuple-element.55.sq_hbm, ...), custom_call_target="tpu_custom_call" | custom-call | flops 1000000000 | bytes 4000000 | tf_op jit(solution)/shard_map/pallas_call | solution.py:429
  52.6 1.6 %collective-permute-start.3 = (bf16[512,512]{1,0:T(8,128)(2,1)}, bf16[512,512]{1,0:T(8,128)(2,1)S(1)}, u32[]{:S(2)}, u32[]{:S(2)}) collective-permute-start(bf16[512,512]{1,0:T(8,128)(2,1)} %get-tuple-element.59.slopes0_ref), channel_id=1, source_target_pairs={{0,1},{1,0},{2,3},{3,2},{4,5},{5,4},{6,7},{7,6},{8,9},{9,8},{10,11... | collective-permute-start | bytes 1572872 | tf_op jit(solution)/shard_map/ppermute | solution.py:424
  54.2 1.1 %copy-done.2 = bf16[512,512]{1,0:T(8,128)(2,1)S(1)} copy-done((bf16[512,512]{1,0:T(8,128)(2,1)S(1)}, bf16[512,512]{1,0:T(8,128)(2,1)}, u32[]{:S(2)}) %copy-start.2) | copy-done | bytes 524312
  55.2 1.0 %copy-done.3 = bf16[512,512]{1,0:T(8,128)(2,1)S(1)} copy-done((bf16[512,512]{1,0:T(8,128)(2,1)S(1)}, bf16[512,512]{1,0:T(8,128)(2,1)}, u32[]{:S(2)}) %copy-start.3) | copy-done | bytes 524312
  56.3 2.2 %shard_map.99 = (f32[1536,512]{1,0:T(8,128)S(1)}, f32[1536,512]{1,0:T(8,128)S(1)}) custom-call(bf16[1536,512]{1,0:T(8,128)(2,1)S(1)} %copy-done.4, bf16[1536,512]{1,0:T(8,128)(2,1)S(1)} %copy-done.5, bf16[512,512]{1,0:T(8,128)(2,1)S(1)} %copy-done.2, bf16[512,512]{1,0:T(8,128)(2,1)S(1)} %copy-done.3), custom_call_target="tpu_custom_call" | custom-call | flops 1610612736 | bytes 10000000 | tf_op jit(solution)/shard_map/pallas_call | solution.py:438
  58.5 3.5 %collective-permute-done.6.slopes_ref = bf16[512,512]{1,0:T(8,128)(2,1)S(1)} collective-permute-done((bf16[512,512]{1,0:T(8,128)(2,1)}, bf16[512,512]{1,0:T(8,128)(2,1)S(1)}, u32[]{:S(2)}, u32[]{:S(2)}) %collective-permute-start.6) | collective-permute-done | bytes 524320 | tf_op jit(solution)/shard_map/ppermute | solution.py:424
  62.5 1.1 %collective-permute-start.9 = (bf16[768,512]{1,0:T(8,128)(2,1)S(1)}, bf16[768,512]{1,0:T(8,128)(2,1)S(1)}, u32[]{:S(2)}, u32[]{:S(2)}) collective-permute-start(bf16[768,512]{1,0:T(8,128)(2,1)S(1)} %shard_map.101), channel_id=1, source_target_pairs={{0,1},{1,0},{2,3},{3,2},{4,5},{5,4},{6,7},{7,6},{8,9},{9,8},{10,11... | collective-permute-start | bytes 2359304 | tf_op jit(solution)/shard_map/ppermute | solution.py:424
  65.4 9.1 %collective-permute-done.9.received_ref = bf16[768,512]{1,0:T(8,128)(2,1)S(1)} collective-permute-done((bf16[768,512]{1,0:T(8,128)(2,1)S(1)}, bf16[768,512]{1,0:T(8,128)(2,1)S(1)}, u32[]{:S(2)}, u32[]{:S(2)}) %collective-permute-start.9) | collective-permute-done | bytes 786464 | tf_op jit(solution)/shard_map/ppermute | solution.py:424
  74.7 0.9 collective-permute-start.10
  77.1 0.9 collective-permute-start.7
  78.0 5.8 %collective-permute-done.10.received_ref = bf16[384,512]{1,0:T(8,128)(2,1)S(1)} collective-permute-done((bf16[384,512]{1,0:T(8,128)(2,1)S(1)}, bf16[384,512]{1,0:T(8,128)(2,1)S(1)}, u32[]{:S(2)}, u32[]{:S(2)}) %collective-permute-start.10) | collective-permute-done | bytes 393248 | tf_op jit(solution)/shard_map/ppermute | solution.py:424
  84.4 1.7 %collective-permute-done.7.received_ref = bf16[384,512]{1,0:T(8,128)(2,1)S(1)} collective-permute-done((bf16[384,512]{1,0:T(8,128)(2,1)S(1)}, bf16[384,512]{1,0:T(8,128)(2,1)S(1)}, u32[]{:S(2)}, u32[]{:S(2)}) %collective-permute-start.7) | collective-permute-done | bytes 393248 | tf_op jit(solution)/shard_map/ppermute | solution.py:424
  86.3 1.9 %collective-permute-start.8 = (bf16[192,512]{1,0:T(8,128)(2,1)S(1)}, bf16[192,512]{1,0:T(8,128)(2,1)S(1)}, u32[]{:S(2)}, u32[]{:S(2)}) collective-permute-start(bf16[192,512]{1,0:T(8,128)(2,1)S(1)} %get-tuple-element.68), channel_id=1, source_target_pairs={{0,24},{1,25},{2,26},{3,27},{4,28},{5,29},{6,30},{7,31},{8,16},{9,... | collective-permute-start | bytes 589832 | tf_op jit(solution)/shard_map/ppermute | solution.py:424
  88.2 2.7 %collective-permute-done.11.received_ref = bf16[192,512]{1,0:T(8,128)(2,1)S(1)} collective-permute-done((bf16[192,512]{1,0:T(8,128)(2,1)S(1)}, bf16[192,512]{1,0:T(8,128)(2,1)S(1)}, u32[]{:S(2)}, u32[]{:S(2)}) %collective-permute-start.11) | collective-permute-done | bytes 196640 | tf_op jit(solution)/shard_map/ppermute | solution.py:424
  91.0 0.8 collective-permute-start.14
  91.8 1.4 %collective-permute-done.8.received_ref = bf16[192,512]{1,0:T(8,128)(2,1)S(1)} collective-permute-done((bf16[192,512]{1,0:T(8,128)(2,1)S(1)}, bf16[192,512]{1,0:T(8,128)(2,1)S(1)}, u32[]{:S(2)}, u32[]{:S(2)}) %collective-permute-start.8) | collective-permute-done | bytes 196640 | tf_op jit(solution)/shard_map/ppermute | solution.py:424
  93.3 1.8 %collective-permute-start.13 = (bf16[96,512]{1,0:T(8,128)(2,1)S(1)}, bf16[96,512]{1,0:T(8,128)(2,1)S(1)}, u32[]{:S(2)}, u32[]{:S(2)}) collective-permute-start(bf16[96,512]{1,0:T(8,128)(2,1)S(1)} %get-tuple-element.77), channel_id=1, source_target_pairs={{0,3},{1,6},{2,5},{3,0},{4,7},{5,2},{6,1},{7,4},{8,11},{9,14},{10,... | collective-permute-start | bytes 294920 | tf_op jit(solution)/shard_map/ppermute | solution.py:424
  95.1 1.1 %shard_map.112 = bf16[512,512]{1,0:T(8,128)(2,1)} custom-call(f32[512,512]{1,0:T(8,128)S(1)} %copy-done.6, bf16[512,512]{1,0:T(8,128)(2,1)S(1)} %copy-done.7, bf16[1024,128]{1,0:T(8,128)(2,1)S(1)} %bitcast.5), custom_call_target="tpu_custom_call" | custom-call | flops 1000000000 | bytes 5000000 | tf_op jit(solution)/shard_map/pallas_call | solution.py:499
  96.2 2.7 %collective-permute-done.14.received_ref = bf16[96,512]{1,0:T(8,128)(2,1)S(1)} collective-permute-done((bf16[96,512]{1,0:T(8,128)(2,1)S(1)}, bf16[96,512]{1,0:T(8,128)(2,1)S(1)}, u32[]{:S(2)}, u32[]{:S(2)}) %collective-permute-start.14) | collective-permute-done | bytes 98336 | tf_op jit(solution)/shard_map/ppermute | solution.py:424
  99.6 2.4 %collective-permute-done.13.received_ref = bf16[96,512]{1,0:T(8,128)(2,1)S(1)} collective-permute-done((bf16[96,512]{1,0:T(8,128)(2,1)S(1)}, bf16[96,512]{1,0:T(8,128)(2,1)S(1)}, u32[]{:S(2)}, u32[]{:S(2)}) %collective-permute-start.13) | collective-permute-done | bytes 98336 | tf_op jit(solution)/shard_map/ppermute | solution.py:424
  (39 shorter events, 7.1 us)
Async XLA Ops:
  4.3 25.1 %all-to-all-start = ((bf16[32,40,128]{2,1,0:T(8,128)(2,1)}), bf16[32,40,128]{2,1,0:T(8,128)(2,1)S(1)}, u32[]{:S(2)}, u32[]{:S(2)}) async-start(bf16[32,40,128]{2,1,0:T(8,128)(2,1)} %shard_map.94), calls=%async_computation | async-start | bytes 655360 | tf_op jit(solution)/shard_map/all_to_all | solution.py:383
  21.8 41.8 %collective-permute-start.2 = (bf16[768,512]{1,0:T(8,128)(2,1)}, bf16[768,512]{1,0:T(8,128)(2,1)S(1)}, u32[]{:S(2)}, u32[]{:S(2)}) collective-permute-start(bf16[768,512]{1,0:T(8,128)(2,1)} %get-tuple-element.62), channel_id=1, source_target_pairs={{0,1},{1,0},{2,3},{3,2},{4,5},{5,4},{6,7},{7,6},{8,9},{9,8},{10,11... | collective-permute-start | bytes 2359304 | tf_op jit(solution)/shard_map/ppermute | solution.py:424
  23.6 34.8 %collective-permute-start.5 = (bf16[768,512]{1,0:T(8,128)(2,1)}, bf16[768,512]{1,0:T(8,128)(2,1)S(1)}, u32[]{:S(2)}, u32[]{:S(2)}) collective-permute-start(bf16[768,512]{1,0:T(8,128)(2,1)} %get-tuple-element.65), channel_id=1, source_target_pairs={{0,8},{1,9},{2,10},{3,11},{4,12},{5,13},{6,14},{7,15},{8,0},{9,1},... | collective-permute-start | bytes 2359304 | tf_op jit(solution)/shard_map/ppermute | solution.py:424
  30.3 18.2 %all-to-all-start.1 = ((bf16[32,32,128]{2,1,0:T(8,128)(2,1)}), bf16[32,32,128]{2,1,0:T(8,128)(2,1)S(1)}, u32[]{:S(2)}, u32[]{:S(2)}) async-start(bf16[32,32,128]{2,1,0:T(8,128)(2,1)} %shard_map.96), calls=%async_computation.1 | async-start | bytes 524288 | tf_op jit(solution)/shard_map/all_to_all | solution.py:420
  35.1 17.5 %collective-permute-start = (bf16[768,512]{1,0:T(8,128)(2,1)}, bf16[768,512]{1,0:T(8,128)(2,1)S(1)}, u32[]{:S(2)}, u32[]{:S(2)}) collective-permute-start(bf16[768,512]{1,0:T(8,128)(2,1)} %get-tuple-element.47), channel_id=1, source_target_pairs={{0,1},{1,0},{2,3},{3,2},{4,5},{5,4},{6,7},{7,6},{8,9},{9,8},{10,11... | collective-permute-start | bytes 2359304 | tf_op jit(solution)/shard_map/ppermute | solution.py:424
  37.0 17.2 %collective-permute-start.1 = (bf16[768,512]{1,0:T(8,128)(2,1)}, bf16[768,512]{1,0:T(8,128)(2,1)S(1)}, u32[]{:S(2)}, u32[]{:S(2)}) collective-permute-start(bf16[768,512]{1,0:T(8,128)(2,1)} %get-tuple-element.48), channel_id=1, source_target_pairs={{0,8},{1,9},{2,10},{3,11},{4,12},{5,13},{6,14},{7,15},{8,0},{9,1},... | collective-permute-start | bytes 2359304 | tf_op jit(solution)/shard_map/ppermute | solution.py:424
  48.4 0.7 copy-start
  49.1 5.0 %copy-start.4 = (bf16[1536,512]{1,0:T(8,128)(2,1)S(1)}, bf16[1536,512]{1,0:T(8,128)(2,1)}, u32[]{:S(2)}) copy-start(bf16[1536,512]{1,0:T(8,128)(2,1)} %get-tuple-element.50.rows0_hbm) | copy-start | bytes 4718596
  49.1 5.0 %copy-start.5 = (bf16[1536,512]{1,0:T(8,128)(2,1)S(1)}, bf16[1536,512]{1,0:T(8,128)(2,1)}, u32[]{:S(2)}) copy-start(bf16[1536,512]{1,0:T(8,128)(2,1)} %get-tuple-element.51.rows1_hbm) | copy-start | bytes 4718596
  52.4 9.5 %collective-permute-start.6 = (bf16[512,512]{1,0:T(8,128)(2,1)}, bf16[512,512]{1,0:T(8,128)(2,1)S(1)}, u32[]{:S(2)}, u32[]{:S(2)}) collective-permute-start(bf16[512,512]{1,0:T(8,128)(2,1)} %get-tuple-element.60.slopes1_ref), channel_id=1, source_target_pairs={{0,8},{1,9},{2,10},{3,11},{4,12},{5,13},{6,14},{7,15},{8,0},{9,1},... | collective-permute-start | bytes 1572872 | tf_op jit(solution)/shard_map/ppermute | solution.py:424
  52.6 11.0 %collective-permute-start.3 = (bf16[512,512]{1,0:T(8,128)(2,1)}, bf16[512,512]{1,0:T(8,128)(2,1)S(1)}, u32[]{:S(2)}, u32[]{:S(2)}) collective-permute-start(bf16[512,512]{1,0:T(8,128)(2,1)} %get-tuple-element.59.slopes0_ref), channel_id=1, source_target_pairs={{0,1},{1,0},{2,3},{3,2},{4,5},{5,4},{6,7},{7,6},{8,9},{9,8},{10,11... | collective-permute-start | bytes 1572872 | tf_op jit(solution)/shard_map/ppermute | solution.py:424
  54.2 1.1 %copy-start.2 = (bf16[512,512]{1,0:T(8,128)(2,1)S(1)}, bf16[512,512]{1,0:T(8,128)(2,1)}, u32[]{:S(2)}) copy-start(bf16[512,512]{1,0:T(8,128)(2,1)} %get-tuple-element.59.slopes0_ref) | copy-start | bytes 1572868
  55.2 1.0 %copy-start.3 = (bf16[512,512]{1,0:T(8,128)(2,1)S(1)}, bf16[512,512]{1,0:T(8,128)(2,1)}, u32[]{:S(2)}) copy-start(bf16[512,512]{1,0:T(8,128)(2,1)} %get-tuple-element.60.slopes1_ref) | copy-start | bytes 1572868
  62.5 12.1 %collective-permute-start.9 = (bf16[768,512]{1,0:T(8,128)(2,1)S(1)}, bf16[768,512]{1,0:T(8,128)(2,1)S(1)}, u32[]{:S(2)}, u32[]{:S(2)}) collective-permute-start(bf16[768,512]{1,0:T(8,128)(2,1)S(1)} %shard_map.101), channel_id=1, source_target_pairs={{0,1},{1,0},{2,3},{3,2},{4,5},{5,4},{6,7},{7,6},{8,9},{9,8},{10,11... | collective-permute-start | bytes 2359304 | tf_op jit(solution)/shard_map/ppermute | solution.py:424
  64.1 12.8 %collective-permute-start.4 = (bf16[768,512]{1,0:T(8,128)(2,1)S(1)}, bf16[768,512]{1,0:T(8,128)(2,1)S(1)}, u32[]{:S(2)}, u32[]{:S(2)}) collective-permute-start(bf16[768,512]{1,0:T(8,128)(2,1)S(1)} %shard_map.100), channel_id=1, source_target_pairs={{0,8},{1,9},{2,10},{3,11},{4,12},{5,13},{6,14},{7,15},{8,0},{9,1},... | collective-permute-start | bytes 2359304 | tf_op jit(solution)/shard_map/ppermute | solution.py:424
  74.7 9.1 %collective-permute-start.10 = (bf16[384,512]{1,0:T(8,128)(2,1)S(1)}, bf16[384,512]{1,0:T(8,128)(2,1)S(1)}, u32[]{:S(2)}, u32[]{:S(2)}) collective-permute-start(bf16[384,512]{1,0:T(8,128)(2,1)S(1)} %get-tuple-element.72), channel_id=1, source_target_pairs={{0,24},{1,25},{2,26},{3,27},{4,28},{5,29},{6,30},{7,31},{8,16},{9,... | collective-permute-start | bytes 1179656 | tf_op jit(solution)/shard_map/ppermute | solution.py:424
  77.1 9.1 %collective-permute-start.7 = (bf16[384,512]{1,0:T(8,128)(2,1)S(1)}, bf16[384,512]{1,0:T(8,128)(2,1)S(1)}, u32[]{:S(2)}, u32[]{:S(2)}) collective-permute-start(bf16[384,512]{1,0:T(8,128)(2,1)S(1)} %get-tuple-element.66), channel_id=1, source_target_pairs={{0,7},{1,2},{2,1},{3,4},{4,3},{5,6},{6,5},{7,0},{8,15},{9,10},{10,... | collective-permute-start | bytes 1179656 | tf_op jit(solution)/shard_map/ppermute | solution.py:424
  83.8 11.3 %copy-start.1 = (bf16[32,32,128]{2,1,0:T(8,128)(2,1)S(1)}, bf16[32,32,128]{2,1,0:T(8,128)(2,1)}, u32[]{:S(2)}) copy-start(bf16[32,32,128]{2,1,0:T(8,128)(2,1)} %copy-done) | copy-start | bytes 786436
  83.8 11.3 %copy-start.6 = (f32[512,512]{1,0:T(8,128)S(1)}, f32[512,512]{1,0:T(8,128)}, u32[]{:S(2)}) copy-start(f32[512,512]{1,0:T(8,128)} %get-tuple-element.81.local_ref) | copy-start | bytes 3145732
  83.8 11.3 %copy-start.7 = (bf16[512,512]{1,0:T(8,128)(2,1)S(1)}, bf16[512,512]{1,0:T(8,128)(2,1)}, u32[]{:S(2)}) copy-start(bf16[512,512]{1,0:T(8,128)(2,1)} %get-tuple-element.82.weighted_ref) | copy-start | bytes 1572868
  83.9 7.0 %collective-permute-start.11 = (bf16[192,512]{1,0:T(8,128)(2,1)S(1)}, bf16[192,512]{1,0:T(8,128)(2,1)S(1)}, u32[]{:S(2)}, u32[]{:S(2)}) collective-permute-start(bf16[192,512]{1,0:T(8,128)(2,1)S(1)} %get-tuple-element.74), channel_id=1, source_target_pairs={{0,7},{1,2},{2,1},{3,4},{4,3},{5,6},{6,5},{7,0},{8,15},{9,10},{10,... | collective-permute-start | bytes 589832 | tf_op jit(solution)/shard_map/ppermute | solution.py:424
  86.3 7.0 %collective-permute-start.8 = (bf16[192,512]{1,0:T(8,128)(2,1)S(1)}, bf16[192,512]{1,0:T(8,128)(2,1)S(1)}, u32[]{:S(2)}, u32[]{:S(2)}) collective-permute-start(bf16[192,512]{1,0:T(8,128)(2,1)S(1)} %get-tuple-element.68), channel_id=1, source_target_pairs={{0,24},{1,25},{2,26},{3,27},{4,28},{5,29},{6,30},{7,31},{8,16},{9,... | collective-permute-start | bytes 589832 | tf_op jit(solution)/shard_map/ppermute | solution.py:424
  90.9 2.4 %collective-permute-start.12 = (bf16[16,128]{1,0:T(8,128)(2,1)S(1)}, bf16[16,128]{1,0:T(8,128)(2,1)S(1)}, u32[]{:S(2)}, u32[]{:S(2)}) collective-permute-start(bf16[16,128]{1,0:T(8,128)(2,1)S(1)} %slice.7), channel_id=1, source_target_pairs={{0,32},{1,33},{2,34},{3,35},{4,36},{5,37},{6,38},{7,39},{8,40},{9,... | collective-permute-start | bytes 12296 | tf_op jit(solution)/shard_map/ppermute | solution.py:487
  91.0 7.9 %collective-permute-start.14 = (bf16[96,512]{1,0:T(8,128)(2,1)S(1)}, bf16[96,512]{1,0:T(8,128)(2,1)S(1)}, u32[]{:S(2)}, u32[]{:S(2)}) collective-permute-start(bf16[96,512]{1,0:T(8,128)(2,1)S(1)} %get-tuple-element.76), channel_id=1, source_target_pairs={{0,3},{1,6},{2,5},{3,0},{4,7},{5,2},{6,1},{7,4},{8,11},{9,14},{10,... | collective-permute-start | bytes 294920 | tf_op jit(solution)/shard_map/ppermute | solution.py:424
  93.3 8.7 %collective-permute-start.13 = (bf16[96,512]{1,0:T(8,128)(2,1)S(1)}, bf16[96,512]{1,0:T(8,128)(2,1)S(1)}, u32[]{:S(2)}, u32[]{:S(2)}) collective-permute-start(bf16[96,512]{1,0:T(8,128)(2,1)S(1)} %get-tuple-element.77), channel_id=1, source_target_pairs={{0,3},{1,6},{2,5},{3,0},{4,7},{5,2},{6,1},{7,4},{8,11},{9,14},{10,... | collective-permute-start | bytes 294920 | tf_op jit(solution)/shard_map/ppermute | solution.py:424

commit v6 on v5

--- a/solution.py
+++ b/solution.py
@@ -145,16 +145,14 @@
     for head in range(heads):
         part = slice(head * HEAD, (head + 1) * HEAD)
         x = key_ref[:, part].astype(F32)
-        keys = (x * jax.nn.sigmoid(x)).astype(BF16)
-        weighted = (keys.astype(F32) * to_end[:, head : head + 1]).astype(BF16)
+        weighted = (x * jax.nn.sigmoid(x) * to_end[:, head : head + 1]).astype(BF16)
         emit(0, head, dot(weighted, value_ref[:, part], (0, 0)))
     copies[3].wait()
     copies[4].wait()
     for head in range(heads):
         part = slice(head * HEAD, (head + 1) * HEAD)
         x = query_ref[:, part].astype(F32)
-        queries = (x * jax.nn.sigmoid(x) * scaling).astype(BF16)
-        weighted = (queries.astype(F32) * from_start[:, head : head + 1]).astype(BF16)
+        weighted = (x * jax.nn.sigmoid(x) * (scaling * from_start[:, head : head + 1])).astype(BF16)
         emit(1, head, dot(weighted, grad_ref[:, part], (0, 0)))
 
 
@@ -487,15 +485,13 @@
     mark = lax.ppermute(sends[1][:16, :128], AXES, other_core)
     gated, mark = lax.optimization_barrier((sends[0], mark))
     sends = (gated, sends[1], mark)
-    qweight_grad, kweight_grad = [
-        pl.pallas_call(
-            last_one_kernel,
-            in_specs=[IN_VMEM, IN_VMEM, pl.BlockSpec(memory_space=pl.ANY)],
-            out_shape=shaped((rows, columns), F32),
-            compiler_params=VMEM,
-        )(exchange(stream, STEPS - 1, sends[stream]), keeps[stream], sends[2])
-        for stream in range(2)
-    ]
+    kweight_grad = pl.pallas_call(
+        last_one_kernel,
+        in_specs=[IN_VMEM, IN_VMEM, pl.BlockSpec(memory_space=pl.ANY)],
+        out_shape=shaped((rows, columns), F32),
+        compiler_params=VMEM,
+    )(exchange(1, STEPS - 1, sends[1]), keeps[1], sends[2])
+    qweight_grad = keeps[0] + exchange(0, STEPS - 1, sends[0]).astype(F32)
     value_grad = pl.pallas_call(
         values_kernel,
         out_shape=small,

time: 104 us -> 104 us (level)
  no operation moved by 1% of the time
where the time goes in v6:
time: 104 us; the launch traced here: 103 us
  waiting for transfers between devices  36.9 us (35%)
  starting transfers between devices  33.3 us (32%)
  Pallas kernels  28.1 us (27%)
  local copies, waits for them, and re-layouts  2.81 us (3%)
    ppermute x14, waiting for transfers between devices, exchange(): return lax.ppermute(array, AXES, sorted(PARTNERS[stream][step].items()))  30.2 us
    ppermute x14, starting transfers between devices, exchange(): return lax.ppermute(array, AXES, sorted(PARTNERS[stream][step].items()))  16.9 us
    all_to_all x1, starting transfers between devices, per_device(): states = lax.all_to_all(states, ('y', 'z'), 0, 0, tiled=True)  11.5 us
    pallas_call x1, Pallas kernels, per_device(): pl.pallas_call(local_kernel, in_specs=[IN_HBM] * 5, out_specs=(IN_HBM,) *...  7.57 us
    pallas_call x1, Pallas kernels, per_device(): pl.pallas_call(arrange_kernel, in_specs=[pl.BlockSpec(memory_space=pltpu....  5.94 us
    all_to_all x1, starting transfers between devices, per_device(): lax.all_to_all(incoming, ('y', 'z'), 0, 0, tiled=True)  4.8 us
    all_to_all x1, waiting for transfers between devices, per_device(): states = lax.all_to_all(states, ('y', 'z'), 0, 0, tiled=True)  4.26 us
    pallas_call x1, Pallas kernels, per_device(): pl.pallas_call(states_kernel, in_specs=[IN_HBM] * 5, out_shape=shaped((SE...  3.66 us
  transfers between devices with their start and end apart: 17, of which 11 were waited for; matrix products, arithmetic and copies ran while one was open for 0% of the time, Pallas kernels for 24%

profile of v6, /device:TPU:4, one launch (start us, length us, event | category | flops | bytes accessed | tf_op | source)
XLA Modules:
  0.0 102.7 jit_solution(11149398291885226181)
XLA Ops:
  0.6 3.7 %shard_map.94 = bf16[32,40,128]{2,1,0:T(8,128)(2,1)} custom-call(f32[4,512]{1,0:T(4,128)} %bitcast.6, bf16[512,512]{1,0:T(8,128)(2,1)} %query_hbm.3, bf16[512,512]{1,0:T(8,128)(2,1)} %key_hbm.3, bf16[512,512]{1,0:T(8,128)(2,1)} %value_hbm.3, bf16[512,512]{1,0:T(8,128)(2,1)} %grad_hbm.3), custom_call_target="tpu_custom_call" | custom-call | flops 1000000000 | bytes 4000000 | tf_op jit(solution)/shard_map/pallas_call | solution.py:373
  4.3 11.5 %all-to-all-start = ((bf16[32,40,128]{2,1,0:T(8,128)(2,1)}), bf16[32,40,128]{2,1,0:T(8,128)(2,1)S(1)}, u32[]{:S(2)}, u32[]{:S(2)}) async-start(bf16[32,40,128]{2,1,0:T(8,128)(2,1)} %shard_map.94), calls=%async_computation | async-start | bytes 655360 | tf_op jit(solution)/shard_map/all_to_all | solution.py:381
  15.8 5.9 %shard_map.95 = (bf16[768,512]{1,0:T(8,128)(2,1)}, bf16[768,512]{1,0:T(8,128)(2,1)}, bf16[768,512]{1,0:T(8,128)(2,1)}, bf16[768,512]{1,0:T(8,128)(2,1)}, bf16[15...) custom-call(s32[1]{0:T(128)} %bitcast.2.place_ref, s32[4096]{0:T(1024)} %constant.20.clone.table_ref, ...), custom_call_target="tpu_custom_call" | custom-call | flops 1000000000 | bytes 10000000 | tf_op jit(solution)/shard_map/pallas_call | solution.py:399
  21.8 1.9 %collective-permute-start.2 = (bf16[768,512]{1,0:T(8,128)(2,1)}, bf16[768,512]{1,0:T(8,128)(2,1)S(1)}, u32[]{:S(2)}, u32[]{:S(2)}) collective-permute-start(bf16[768,512]{1,0:T(8,128)(2,1)} %get-tuple-element.62), channel_id=1, source_target_pairs={{0,1},{1,0},{2,3},{3,2},{4,5},{5,4},{6,7},{7,6},{8,9},{9,8},{10,11... | collective-permute-start | bytes 2359304 | tf_op jit(solution)/shard_map/ppermute | solution.py:422
  23.6 1.5 %collective-permute-start.5 = (bf16[768,512]{1,0:T(8,128)(2,1)}, bf16[768,512]{1,0:T(8,128)(2,1)S(1)}, u32[]{:S(2)}, u32[]{:S(2)}) collective-permute-start(bf16[768,512]{1,0:T(8,128)(2,1)} %get-tuple-element.65), channel_id=1, source_target_pairs={{0,8},{1,9},{2,10},{3,11},{4,12},{5,13},{6,14},{7,15},{8,0},{9,1},... | collective-permute-start | bytes 2359304 | tf_op jit(solution)/shard_map/ppermute | solution.py:422
  25.1 4.3 %all-to-all-done.in_ref = bf16[32,40,128]{2,1,0:T(8,128)(2,1)S(1)} async-done(((bf16[32,40,128]{2,1,0:T(8,128)(2,1)}), bf16[32,40,128]{2,1,0:T(8,128)(2,1)S(1)}, u32[]{:S(2)}, u32[]{:S(2)}) %all-to-all-start) | async-done | bytes 327712 | tf_op jit(solution)/shard_map/all_to_all | solution.py:381
  29.4 0.9 shard_map.96
  30.3 4.8 %all-to-all-start.1 = ((bf16[32,32,128]{2,1,0:T(8,128)(2,1)}), bf16[32,32,128]{2,1,0:T(8,128)(2,1)S(1)}, u32[]{:S(2)}, u32[]{:S(2)}) async-start(bf16[32,32,128]{2,1,0:T(8,128)(2,1)} %shard_map.96), calls=%async_computation.1 | async-start | bytes 524288 | tf_op jit(solution)/shard_map/all_to_all | solution.py:418
  35.1 1.9 %collective-permute-start = (bf16[768,512]{1,0:T(8,128)(2,1)}, bf16[768,512]{1,0:T(8,128)(2,1)S(1)}, u32[]{:S(2)}, u32[]{:S(2)}) collective-permute-start(bf16[768,512]{1,0:T(8,128)(2,1)} %get-tuple-element.47), channel_id=1, source_target_pairs={{0,1},{1,0},{2,3},{3,2},{4,5},{5,4},{6,7},{7,6},{8,9},{9,8},{10,11... | collective-permute-start | bytes 2359304 | tf_op jit(solution)/shard_map/ppermute | solution.py:422
  37.0 1.5 %collective-permute-start.1 = (bf16[768,512]{1,0:T(8,128)(2,1)}, bf16[768,512]{1,0:T(8,128)(2,1)S(1)}, u32[]{:S(2)}, u32[]{:S(2)}) collective-permute-start(bf16[768,512]{1,0:T(8,128)(2,1)} %get-tuple-element.48), channel_id=1, source_target_pairs={{0,8},{1,9},{2,10},{3,11},{4,12},{5,13},{6,14},{7,15},{8,0},{9,1},... | collective-permute-start | bytes 2359304 | tf_op jit(solution)/shard_map/ppermute | solution.py:422
  38.4 7.6 %shard_map.97 = (bf16[512,512]{1,0:T(8,128)(2,1)}, bf16[512,512]{1,0:T(8,128)(2,1)}, f32[512,512]{1,0:T(8,128)}, bf16[512,512]{1,0:T(8,128)(2,1)}, bf16[512,512]...) custom-call(f32[4,512]{1,0:T(4,128)} %bitcast.7, ...), custom_call_target="tpu_custom_call" | custom-call | flops 60000002048 | bytes 10000000 | tf_op jit(solution)/shard_map/pallas_call | solution.py:383
  46.0 2.5 %all-to-all-done.1 = bf16[32,32,128]{2,1,0:T(8,128)(2,1)S(1)} async-done(((bf16[32,32,128]{2,1,0:T(8,128)(2,1)}), bf16[32,32,128]{2,1,0:T(8,128)(2,1)S(1)}, u32[]{:S(2)}, u32[]{:S(2)}) %all-to-all-start.1) | async-done | bytes 262176 | tf_op jit(solution)/shard_map/all_to_all | solution.py:418
  49.2 3.3 %shard_map.98 = (bf16[512,512]{1,0:T(8,128)(2,1)}, bf16[512,512]{1,0:T(8,128)(2,1)}) custom-call(bf16[1024,128]{1,0:T(8,128)(2,1)} %bitcast.4, bf16[512,512]{1,0:T(8,128)(2,1)} %get-tuple-element.53.wo_hbm, bf16[512,512]{1,0:T(8,128)(2,1)} %get-tuple-element.54.gq_hbm, bf16[512,512]{1,0:T(8,128)(2,1)} %get-tuple-element.55.sq_hbm, ...), custom_call_target="tpu_custom_call" | custom-call | flops 1000000000 | bytes 4000000 | tf_op jit(solution)/shard_map/pallas_call | solution.py:427
  52.6 1.6 %collective-permute-start.3 = (bf16[512,512]{1,0:T(8,128)(2,1)}, bf16[512,512]{1,0:T(8,128)(2,1)S(1)}, u32[]{:S(2)}, u32[]{:S(2)}) collective-permute-start(bf16[512,512]{1,0:T(8,128)(2,1)} %get-tuple-element.59.slopes0_ref), channel_id=1, source_target_pairs={{0,1},{1,0},{2,3},{3,2},{4,5},{5,4},{6,7},{7,6},{8,9},{9,8},{10,11... | collective-permute-start | bytes 1572872 | tf_op jit(solution)/shard_map/ppermute | solution.py:422
  54.2 1.1 %copy-done.2 = bf16[512,512]{1,0:T(8,128)(2,1)S(1)} copy-done((bf16[512,512]{1,0:T(8,128)(2,1)S(1)}, bf16[512,512]{1,0:T(8,128)(2,1)}, u32[]{:S(2)}) %copy-start.2) | copy-done | bytes 524312
  55.2 1.0 %copy-done.3 = bf16[512,512]{1,0:T(8,128)(2,1)S(1)} copy-done((bf16[512,512]{1,0:T(8,128)(2,1)S(1)}, bf16[512,512]{1,0:T(8,128)(2,1)}, u32[]{:S(2)}) %copy-start.3) | copy-done | bytes 524312
  56.3 2.2 %shard_map.99 = (f32[1536,512]{1,0:T(8,128)S(1)}, f32[1536,512]{1,0:T(8,128)S(1)}) custom-call(bf16[1536,512]{1,0:T(8,128)(2,1)S(1)} %copy-done.4, bf16[1536,512]{1,0:T(8,128)(2,1)S(1)} %copy-done.5, bf16[512,512]{1,0:T(8,128)(2,1)S(1)} %copy-done.2, bf16[512,512]{1,0:T(8,128)(2,1)S(1)} %copy-done.3), custom_call_target="tpu_custom_call" | custom-call | flops 1610612736 | bytes 10000000 | tf_op jit(solution)/shard_map/pallas_call | solution.py:436
  58.5 3.5 %collective-permute-done.6.slopes_ref = bf16[512,512]{1,0:T(8,128)(2,1)S(1)} collective-permute-done((bf16[512,512]{1,0:T(8,128)(2,1)}, bf16[512,512]{1,0:T(8,128)(2,1)S(1)}, u32[]{:S(2)}, u32[]{:S(2)}) %collective-permute-start.6) | collective-permute-done | bytes 524320 | tf_op jit(solution)/shard_map/ppermute | solution.py:422
  62.5 1.1 %collective-permute-start.9 = (bf16[768,512]{1,0:T(8,128)(2,1)S(1)}, bf16[768,512]{1,0:T(8,128)(2,1)S(1)}, u32[]{:S(2)}, u32[]{:S(2)}) collective-permute-start(bf16[768,512]{1,0:T(8,128)(2,1)S(1)} %shard_map.101), channel_id=1, source_target_pairs={{0,1},{1,0},{2,3},{3,2},{4,5},{5,4},{6,7},{7,6},{8,9},{9,8},{10,11... | collective-permute-start | bytes 2359304 | tf_op jit(solution)/shard_map/ppermute | solution.py:422
  65.4 9.1 %collective-permute-done.9.received_ref = bf16[768,512]{1,0:T(8,128)(2,1)S(1)} collective-permute-done((bf16[768,512]{1,0:T(8,128)(2,1)S(1)}, bf16[768,512]{1,0:T(8,128)(2,1)S(1)}, u32[]{:S(2)}, u32[]{:S(2)}) %collective-permute-start.9) | collective-permute-done | bytes 786464 | tf_op jit(solution)/shard_map/ppermute | solution.py:422
  74.8 0.9 collective-permute-start.10
  77.1 0.9 collective-permute-start.7
  78.0 5.9 %collective-permute-done.10.received_ref = bf16[384,512]{1,0:T(8,128)(2,1)S(1)} collective-permute-done((bf16[384,512]{1,0:T(8,128)(2,1)S(1)}, bf16[384,512]{1,0:T(8,128)(2,1)S(1)}, u32[]{:S(2)}, u32[]{:S(2)}) %collective-permute-start.10) | collective-permute-done | bytes 393248 | tf_op jit(solution)/shard_map/ppermute | solution.py:422
  84.4 1.8 %collective-permute-done.7.received_ref = bf16[384,512]{1,0:T(8,128)(2,1)S(1)} collective-permute-done((bf16[384,512]{1,0:T(8,128)(2,1)S(1)}, bf16[384,512]{1,0:T(8,128)(2,1)S(1)}, u32[]{:S(2)}, u32[]{:S(2)}) %collective-permute-start.7) | collective-permute-done | bytes 393248 | tf_op jit(solution)/shard_map/ppermute | solution.py:422
  86.3 1.9 %collective-permute-start.8 = (bf16[192,512]{1,0:T(8,128)(2,1)S(1)}, bf16[192,512]{1,0:T(8,128)(2,1)S(1)}, u32[]{:S(2)}, u32[]{:S(2)}) collective-permute-start(bf16[192,512]{1,0:T(8,128)(2,1)S(1)} %get-tuple-element.68), channel_id=1, source_target_pairs={{0,24},{1,25},{2,26},{3,27},{4,28},{5,29},{6,30},{7,31},{8,16},{9,... | collective-permute-start | bytes 589832 | tf_op jit(solution)/shard_map/ppermute | solution.py:422
  88.2 2.6 %collective-permute-done.11.received_ref = bf16[192,512]{1,0:T(8,128)(2,1)S(1)} collective-permute-done((bf16[192,512]{1,0:T(8,128)(2,1)S(1)}, bf16[192,512]{1,0:T(8,128)(2,1)S(1)}, u32[]{:S(2)}, u32[]{:S(2)}) %collective-permute-start.11) | collective-permute-done | bytes 196640 | tf_op jit(solution)/shard_map/ppermute | solution.py:422
  91.0 0.8 collective-permute-start.14
  91.8 1.4 %collective-permute-done.8.received_ref = bf16[192,512]{1,0:T(8,128)(2,1)S(1)} collective-permute-done((bf16[192,512]{1,0:T(8,128)(2,1)S(1)}, bf16[192,512]{1,0:T(8,128)(2,1)S(1)}, u32[]{:S(2)}, u32[]{:S(2)}) %collective-permute-start.8) | collective-permute-done | bytes 196640 | tf_op jit(solution)/shard_map/ppermute | solution.py:422
  93.3 1.8 %collective-permute-start.13 = (bf16[96,512]{1,0:T(8,128)(2,1)S(1)}, bf16[96,512]{1,0:T(8,128)(2,1)S(1)}, u32[]{:S(2)}, u32[]{:S(2)}) collective-permute-start(bf16[96,512]{1,0:T(8,128)(2,1)S(1)} %get-tuple-element.78), channel_id=1, source_target_pairs={{0,3},{1,6},{2,5},{3,0},{4,7},{5,2},{6,1},{7,4},{8,11},{9,14},{10,... | collective-permute-start | bytes 294920 | tf_op jit(solution)/shard_map/ppermute | solution.py:422
  95.1 1.1 %shard_map.111 = bf16[512,512]{1,0:T(8,128)(2,1)} custom-call(f32[512,512]{1,0:T(8,128)S(1)} %copy-done.6, bf16[512,512]{1,0:T(8,128)(2,1)S(1)} %copy-done.7, bf16[1024,128]{1,0:T(8,128)(2,1)S(1)} %bitcast.5), custom_call_target="tpu_custom_call" | custom-call | flops 1000000000 | bytes 5000000 | tf_op jit(solution)/shard_map/pallas_call | solution.py:495
  96.2 2.7 %collective-permute-done.14.received_ref = bf16[96,512]{1,0:T(8,128)(2,1)S(1)} collective-permute-done((bf16[96,512]{1,0:T(8,128)(2,1)S(1)}, bf16[96,512]{1,0:T(8,128)(2,1)S(1)}, u32[]{:S(2)}, u32[]{:S(2)}) %collective-permute-start.14) | collective-permute-done | bytes 98336 | tf_op jit(solution)/shard_map/ppermute | solution.py:422
  99.6 2.4 %collective-permute-done.13 = bf16[96,512]{1,0:T(8,128)(2,1)S(1)} collective-permute-done((bf16[96,512]{1,0:T(8,128)(2,1)S(1)}, bf16[96,512]{1,0:T(8,128)(2,1)S(1)}, u32[]{:S(2)}, u32[]{:S(2)}) %collective-permute-start.13) | collective-permute-done | bytes 98336 | tf_op jit(solution)/shard_map/ppermute | solution.py:422
  (39 shorter events, 7.2 us)
Async XLA Ops:
  4.3 25.1 %all-to-all-start = ((bf16[32,40,128]{2,1,0:T(8,128)(2,1)}), bf16[32,40,128]{2,1,0:T(8,128)(2,1)S(1)}, u32[]{:S(2)}, u32[]{:S(2)}) async-start(bf16[32,40,128]{2,1,0:T(8,128)(2,1)} %shard_map.94), calls=%async_computation | async-start | bytes 655360 | tf_op jit(solution)/shard_map/all_to_all | solution.py:381
  21.8 41.8 %collective-permute-start.2 = (bf16[768,512]{1,0:T(8,128)(2,1)}, bf16[768,512]{1,0:T(8,128)(2,1)S(1)}, u32[]{:S(2)}, u32[]{:S(2)}) collective-permute-start(bf16[768,512]{1,0:T(8,128)(2,1)} %get-tuple-element.62), channel_id=1, source_target_pairs={{0,1},{1,0},{2,3},{3,2},{4,5},{5,4},{6,7},{7,6},{8,9},{9,8},{10,11... | collective-permute-start | bytes 2359304 | tf_op jit(solution)/shard_map/ppermute | solution.py:422
  23.6 34.8 %collective-permute-start.5 = (bf16[768,512]{1,0:T(8,128)(2,1)}, bf16[768,512]{1,0:T(8,128)(2,1)S(1)}, u32[]{:S(2)}, u32[]{:S(2)}) collective-permute-start(bf16[768,512]{1,0:T(8,128)(2,1)} %get-tuple-element.65), channel_id=1, source_target_pairs={{0,8},{1,9},{2,10},{3,11},{4,12},{5,13},{6,14},{7,15},{8,0},{9,1},... | collective-permute-start | bytes 2359304 | tf_op jit(solution)/shard_map/ppermute | solution.py:422
  30.3 18.2 %all-to-all-start.1 = ((bf16[32,32,128]{2,1,0:T(8,128)(2,1)}), bf16[32,32,128]{2,1,0:T(8,128)(2,1)S(1)}, u32[]{:S(2)}, u32[]{:S(2)}) async-start(bf16[32,32,128]{2,1,0:T(8,128)(2,1)} %shard_map.96), calls=%async_computation.1 | async-start | bytes 524288 | tf_op jit(solution)/shard_map/all_to_all | solution.py:418
  35.1 17.5 %collective-permute-start = (bf16[768,512]{1,0:T(8,128)(2,1)}, bf16[768,512]{1,0:T(8,128)(2,1)S(1)}, u32[]{:S(2)}, u32[]{:S(2)}) collective-permute-start(bf16[768,512]{1,0:T(8,128)(2,1)} %get-tuple-element.47), channel_id=1, source_target_pairs={{0,1},{1,0},{2,3},{3,2},{4,5},{5,4},{6,7},{7,6},{8,9},{9,8},{10,11... | collective-permute-start | bytes 2359304 | tf_op jit(solution)/shard_map/ppermute | solution.py:422
  37.0 17.2 %collective-permute-start.1 = (bf16[768,512]{1,0:T(8,128)(2,1)}, bf16[768,512]{1,0:T(8,128)(2,1)S(1)}, u32[]{:S(2)}, u32[]{:S(2)}) collective-permute-start(bf16[768,512]{1,0:T(8,128)(2,1)} %get-tuple-element.48), channel_id=1, source_target_pairs={{0,8},{1,9},{2,10},{3,11},{4,12},{5,13},{6,14},{7,15},{8,0},{9,1},... | collective-permute-start | bytes 2359304 | tf_op jit(solution)/shard_map/ppermute | solution.py:422
  48.5 0.7 copy-start
  49.1 5.0 %copy-start.4 = (bf16[1536,512]{1,0:T(8,128)(2,1)S(1)}, bf16[1536,512]{1,0:T(8,128)(2,1)}, u32[]{:S(2)}) copy-start(bf16[1536,512]{1,0:T(8,128)(2,1)} %get-tuple-element.50.rows0_hbm) | copy-start | bytes 4718596
  49.1 5.0 %copy-start.5 = (bf16[1536,512]{1,0:T(8,128)(2,1)S(1)}, bf16[1536,512]{1,0:T(8,128)(2,1)}, u32[]{:S(2)}) copy-start(bf16[1536,512]{1,0:T(8,128)(2,1)} %get-tuple-element.51.rows1_hbm) | copy-start | bytes 4718596
  52.4 9.5 %collective-permute-start.6 = (bf16[512,512]{1,0:T(8,128)(2,1)}, bf16[512,512]{1,0:T(8,128)(2,1)S(1)}, u32[]{:S(2)}, u32[]{:S(2)}) collective-permute-start(bf16[512,512]{1,0:T(8,128)(2,1)} %get-tuple-element.60.slopes1_ref), channel_id=1, source_target_pairs={{0,8},{1,9},{2,10},{3,11},{4,12},{5,13},{6,14},{7,15},{8,0},{9,1},... | collective-permute-start | bytes 1572872 | tf_op jit(solution)/shard_map/ppermute | solution.py:422
  52.6 11.0 %collective-permute-start.3 = (bf16[512,512]{1,0:T(8,128)(2,1)}, bf16[512,512]{1,0:T(8,128)(2,1)S(1)}, u32[]{:S(2)}, u32[]{:S(2)}) collective-permute-start(bf16[512,512]{1,0:T(8,128)(2,1)} %get-tuple-element.59.slopes0_ref), channel_id=1, source_target_pairs={{0,1},{1,0},{2,3},{3,2},{4,5},{5,4},{6,7},{7,6},{8,9},{9,8},{10,11... | collective-permute-start | bytes 1572872 | tf_op jit(solution)/shard_map/ppermute | solution.py:422
  54.2 1.1 %copy-start.2 = (bf16[512,512]{1,0:T(8,128)(2,1)S(1)}, bf16[512,512]{1,0:T(8,128)(2,1)}, u32[]{:S(2)}) copy-start(bf16[512,512]{1,0:T(8,128)(2,1)} %get-tuple-element.59.slopes0_ref) | copy-start | bytes 1572868
  55.2 1.0 %copy-start.3 = (bf16[512,512]{1,0:T(8,128)(2,1)S(1)}, bf16[512,512]{1,0:T(8,128)(2,1)}, u32[]{:S(2)}) copy-start(bf16[512,512]{1,0:T(8,128)(2,1)} %get-tuple-element.60.slopes1_ref) | copy-start | bytes 1572868
  62.5 12.1 %collective-permute-start.9 = (bf16[768,512]{1,0:T(8,128)(2,1)S(1)}, bf16[768,512]{1,0:T(8,128)(2,1)S(1)}, u32[]{:S(2)}, u32[]{:S(2)}) collective-permute-start(bf16[768,512]{1,0:T(8,128)(2,1)S(1)} %shard_map.101), channel_id=1, source_target_pairs={{0,1},{1,0},{2,3},{3,2},{4,5},{5,4},{6,7},{7,6},{8,9},{9,8},{10,11... | collective-permute-start | bytes 2359304 | tf_op jit(solution)/shard_map/ppermute | solution.py:422
  64.1 12.8 %collective-permute-start.4 = (bf16[768,512]{1,0:T(8,128)(2,1)S(1)}, bf16[768,512]{1,0:T(8,128)(2,1)S(1)}, u32[]{:S(2)}, u32[]{:S(2)}) collective-permute-start(bf16[768,512]{1,0:T(8,128)(2,1)S(1)} %shard_map.100), channel_id=1, source_target_pairs={{0,8},{1,9},{2,10},{3,11},{4,12},{5,13},{6,14},{7,15},{8,0},{9,1},... | collective-permute-start | bytes 2359304 | tf_op jit(solution)/shard_map/ppermute | solution.py:422
  74.8 9.1 %collective-permute-start.10 = (bf16[384,512]{1,0:T(8,128)(2,1)S(1)}, bf16[384,512]{1,0:T(8,128)(2,1)S(1)}, u32[]{:S(2)}, u32[]{:S(2)}) collective-permute-start(bf16[384,512]{1,0:T(8,128)(2,1)S(1)} %get-tuple-element.73), channel_id=1, source_target_pairs={{0,24},{1,25},{2,26},{3,27},{4,28},{5,29},{6,30},{7,31},{8,16},{9,... | collective-permute-start | bytes 1179656 | tf_op jit(solution)/shard_map/ppermute | solution.py:422
  77.1 9.1 %collective-permute-start.7 = (bf16[384,512]{1,0:T(8,128)(2,1)S(1)}, bf16[384,512]{1,0:T(8,128)(2,1)S(1)}, u32[]{:S(2)}, u32[]{:S(2)}) collective-permute-start(bf16[384,512]{1,0:T(8,128)(2,1)S(1)} %get-tuple-element.66), channel_id=1, source_target_pairs={{0,7},{1,2},{2,1},{3,4},{4,3},{5,6},{6,5},{7,0},{8,15},{9,10},{10,... | collective-permute-start | bytes 1179656 | tf_op jit(solution)/shard_map/ppermute | solution.py:422
  83.8 11.3 %copy-start.1 = (bf16[32,32,128]{2,1,0:T(8,128)(2,1)S(1)}, bf16[32,32,128]{2,1,0:T(8,128)(2,1)}, u32[]{:S(2)}) copy-start(bf16[32,32,128]{2,1,0:T(8,128)(2,1)} %copy-done) | copy-start | bytes 786436
  83.8 11.3 %copy-start.6 = (f32[512,512]{1,0:T(8,128)S(1)}, f32[512,512]{1,0:T(8,128)}, u32[]{:S(2)}) copy-start(f32[512,512]{1,0:T(8,128)} %get-tuple-element.81.local_ref) | copy-start | bytes 3145732
  83.8 11.3 %copy-start.7 = (bf16[512,512]{1,0:T(8,128)(2,1)S(1)}, bf16[512,512]{1,0:T(8,128)(2,1)}, u32[]{:S(2)}) copy-start(bf16[512,512]{1,0:T(8,128)(2,1)} %get-tuple-element.82.weighted_ref) | copy-start | bytes 1572868
  83.9 7.0 %collective-permute-start.11 = (bf16[192,512]{1,0:T(8,128)(2,1)S(1)}, bf16[192,512]{1,0:T(8,128)(2,1)S(1)}, u32[]{:S(2)}, u32[]{:S(2)}) collective-permute-start(bf16[192,512]{1,0:T(8,128)(2,1)S(1)} %get-tuple-element.75), channel_id=1, source_target_pairs={{0,7},{1,2},{2,1},{3,4},{4,3},{5,6},{6,5},{7,0},{8,15},{9,10},{10,... | collective-permute-start | bytes 589832 | tf_op jit(solution)/shard_map/ppermute | solution.py:422
  86.3 7.0 %collective-permute-start.8 = (bf16[192,512]{1,0:T(8,128)(2,1)S(1)}, bf16[192,512]{1,0:T(8,128)(2,1)S(1)}, u32[]{:S(2)}, u32[]{:S(2)}) collective-permute-start(bf16[192,512]{1,0:T(8,128)(2,1)S(1)} %get-tuple-element.68), channel_id=1, source_target_pairs={{0,24},{1,25},{2,26},{3,27},{4,28},{5,29},{6,30},{7,31},{8,16},{9,... | collective-permute-start | bytes 589832 | tf_op jit(solution)/shard_map/ppermute | solution.py:422
  90.9 2.4 %collective-permute-start.12 = (bf16[16,128]{1,0:T(8,128)(2,1)S(1)}, bf16[16,128]{1,0:T(8,128)(2,1)S(1)}, u32[]{:S(2)}, u32[]{:S(2)}) collective-permute-start(bf16[16,128]{1,0:T(8,128)(2,1)S(1)} %slice.7), channel_id=1, source_target_pairs={{0,32},{1,33},{2,34},{3,35},{4,36},{5,37},{6,38},{7,39},{8,40},{9,... | collective-permute-start | bytes 12296 | tf_op jit(solution)/shard_map/ppermute | solution.py:485
  91.0 7.9 %collective-permute-start.14 = (bf16[96,512]{1,0:T(8,128)(2,1)S(1)}, bf16[96,512]{1,0:T(8,128)(2,1)S(1)}, u32[]{:S(2)}, u32[]{:S(2)}) collective-permute-start(bf16[96,512]{1,0:T(8,128)(2,1)S(1)} %get-tuple-element.77), channel_id=1, source_target_pairs={{0,3},{1,6},{2,5},{3,0},{4,7},{5,2},{6,1},{7,4},{8,11},{9,14},{10,... | collective-permute-start | bytes 294920 | tf_op jit(solution)/shard_map/ppermute | solution.py:422
  93.3 8.7 %collective-permute-start.13 = (bf16[96,512]{1,0:T(8,128)(2,1)S(1)}, bf16[96,512]{1,0:T(8,128)(2,1)S(1)}, u32[]{:S(2)}, u32[]{:S(2)}) collective-permute-start(bf16[96,512]{1,0:T(8,128)(2,1)S(1)} %get-tuple-element.78), channel_id=1, source_target_pairs={{0,3},{1,6},{2,5},{3,0},{4,7},{5,2},{6,1},{7,4},{8,11},{9,14},{10,... | collective-permute-start | bytes 294920 | tf_op jit(solution)/shard_map/ppermute | solution.py:422

commit v7 on v6

--- a/solution.py
+++ b/solution.py
@@ -26,8 +26,8 @@
 def exchange_plan(stream, core):
     way = 1 - 2 * core
     if stream == 0:
-        return [("z", way), ("y", way), ("z", -way), ("y", -way), ("z", 3 * way)]
-    return [("y", way), ("z", way), ("y", -way), ("z", -way), ("z", 3 * way)]
+        return [("z", way), ("y", way), ("y", -way), ("z", -way), ("z", 3 * way)]
+    return [("y", way), ("z", way), ("z", -way), ("y", -way), ("z", 3 * way)]
 
 
 def rank_of(core, y, z):

time: 104 us -> 104 us (level)
  starting transfers between devices: 33.3 us -> 35.4 us
  waiting for transfers between devices: 36.9 us -> 35.4 us
    ppermute x14, starting transfers between devices: 16.9 us -> 19 us  [exchange(): return lax.ppermute(array, AXES, sorted(PARTNERS[stream][step].items()))]
    ppermute x14, waiting for transfers between devices: 30.2 us -> 28.7 us  [exchange(): return lax.ppermute(array, AXES, sorted(PARTNERS[stream][step].items()))]
where the time goes in v7:
time: 104 us; the launch traced here: 103 us
  starting transfers between devices  35.4 us (34%)
  waiting for transfers between devices  35.4 us (34%)
  Pallas kernels  28.1 us (27%)
  local copies, waits for them, and re-layouts  2.81 us (3%)
    ppermute x14, waiting for transfers between devices, exchange(): return lax.ppermute(array, AXES, sorted(PARTNERS[stream][step].items()))  28.7 us
    ppermute x14, starting transfers between devices, exchange(): return lax.ppermute(array, AXES, sorted(PARTNERS[stream][step].items()))  19 us
    all_to_all x1, starting transfers between devices, per_device(): states = lax.all_to_all(states, ('y', 'z'), 0, 0, tiled=True)  11.5 us
    pallas_call x1, Pallas kernels, per_device(): pl.pallas_call(local_kernel, in_specs=[IN_HBM] * 5, out_specs=(IN_HBM,) *...  7.57 us
    pallas_call x1, Pallas kernels, per_device(): pl.pallas_call(arrange_kernel, in_specs=[pl.BlockSpec(memory_space=pltpu....  5.94 us
    all_to_all x1, starting transfers between devices, per_device(): lax.all_to_all(incoming, ('y', 'z'), 0, 0, tiled=True)  4.8 us
    all_to_all x1, waiting for transfers between devices, per_device(): states = lax.all_to_all(states, ('y', 'z'), 0, 0, tiled=True)  4.26 us
    pallas_call x1, Pallas kernels, per_device(): pl.pallas_call(states_kernel, in_specs=[IN_HBM] * 5, out_shape=shaped((SE...  3.66 us
  transfers between devices with their start and end apart: 17, of which 11 were waited for; matrix products, arithmetic and copies ran while one was open for 0% of the time, Pallas kernels for 24%

profile of v7, /device:TPU:4, one launch (start us, length us, event | category | flops | bytes accessed | tf_op | source)
XLA Modules:
  0.0 103.3 jit_solution(10941070847481385365)
XLA Ops:
  0.6 3.7 %shard_map.94 = bf16[32,40,128]{2,1,0:T(8,128)(2,1)} custom-call(f32[4,512]{1,0:T(4,128)} %bitcast.6, bf16[512,512]{1,0:T(8,128)(2,1)} %query_hbm.3, bf16[512,512]{1,0:T(8,128)(2,1)} %key_hbm.3, bf16[512,512]{1,0:T(8,128)(2,1)} %value_hbm.3, bf16[512,512]{1,0:T(8,128)(2,1)} %grad_hbm.3), custom_call_target="tpu_custom_call" | custom-call | flops 1000000000 | bytes 4000000 | tf_op jit(solution)/shard_map/pallas_call | solution.py:373
  4.3 11.5 %all-to-all-start = ((bf16[32,40,128]{2,1,0:T(8,128)(2,1)}), bf16[32,40,128]{2,1,0:T(8,128)(2,1)S(1)}, u32[]{:S(2)}, u32[]{:S(2)}) async-start(bf16[32,40,128]{2,1,0:T(8,128)(2,1)} %shard_map.94), calls=%async_computation | async-start | bytes 655360 | tf_op jit(solution)/shard_map/all_to_all | solution.py:381
  15.8 5.9 %shard_map.95 = (bf16[768,512]{1,0:T(8,128)(2,1)}, bf16[768,512]{1,0:T(8,128)(2,1)}, bf16[768,512]{1,0:T(8,128)(2,1)}, bf16[768,512]{1,0:T(8,128)(2,1)}, bf16[15...) custom-call(s32[1]{0:T(128)} %bitcast.2.place_ref, s32[4096]{0:T(1024)} %constant.20.clone.table_ref, ...), custom_call_target="tpu_custom_call" | custom-call | flops 1000000000 | bytes 10000000 | tf_op jit(solution)/shard_map/pallas_call | solution.py:399
  21.8 1.9 %collective-permute-start.2 = (bf16[768,512]{1,0:T(8,128)(2,1)}, bf16[768,512]{1,0:T(8,128)(2,1)S(1)}, u32[]{:S(2)}, u32[]{:S(2)}) collective-permute-start(bf16[768,512]{1,0:T(8,128)(2,1)} %get-tuple-element.62), channel_id=1, source_target_pairs={{0,1},{1,0},{2,3},{3,2},{4,5},{5,4},{6,7},{7,6},{8,9},{9,8},{10,11... | collective-permute-start | bytes 2359304 | tf_op jit(solution)/shard_map/ppermute | solution.py:422
  23.6 1.5 %collective-permute-start.5 = (bf16[768,512]{1,0:T(8,128)(2,1)}, bf16[768,512]{1,0:T(8,128)(2,1)S(1)}, u32[]{:S(2)}, u32[]{:S(2)}) collective-permute-start(bf16[768,512]{1,0:T(8,128)(2,1)} %get-tuple-element.65), channel_id=1, source_target_pairs={{0,8},{1,9},{2,10},{3,11},{4,12},{5,13},{6,14},{7,15},{8,0},{9,1},... | collective-permute-start | bytes 2359304 | tf_op jit(solution)/shard_map/ppermute | solution.py:422
  25.1 4.3 %all-to-all-done.in_ref = bf16[32,40,128]{2,1,0:T(8,128)(2,1)S(1)} async-done(((bf16[32,40,128]{2,1,0:T(8,128)(2,1)}), bf16[32,40,128]{2,1,0:T(8,128)(2,1)S(1)}, u32[]{:S(2)}, u32[]{:S(2)}) %all-to-all-start) | async-done | bytes 327712 | tf_op jit(solution)/shard_map/all_to_all | solution.py:381
  29.4 0.9 shard_map.96
  30.3 4.8 %all-to-all-start.1 = ((bf16[32,32,128]{2,1,0:T(8,128)(2,1)}), bf16[32,32,128]{2,1,0:T(8,128)(2,1)S(1)}, u32[]{:S(2)}, u32[]{:S(2)}) async-start(bf16[32,32,128]{2,1,0:T(8,128)(2,1)} %shard_map.96), calls=%async_computation.1 | async-start | bytes 524288 | tf_op jit(solution)/shard_map/all_to_all | solution.py:418
  35.1 1.9 %collective-permute-start = (bf16[768,512]{1,0:T(8,128)(2,1)}, bf16[768,512]{1,0:T(8,128)(2,1)S(1)}, u32[]{:S(2)}, u32[]{:S(2)}) collective-permute-start(bf16[768,512]{1,0:T(8,128)(2,1)} %get-tuple-element.47), channel_id=1, source_target_pairs={{0,1},{1,0},{2,3},{3,2},{4,5},{5,4},{6,7},{7,6},{8,9},{9,8},{10,11... | collective-permute-start | bytes 2359304 | tf_op jit(solution)/shard_map/ppermute | solution.py:422
  37.0 1.5 %collective-permute-start.1 = (bf16[768,512]{1,0:T(8,128)(2,1)}, bf16[768,512]{1,0:T(8,128)(2,1)S(1)}, u32[]{:S(2)}, u32[]{:S(2)}) collective-permute-start(bf16[768,512]{1,0:T(8,128)(2,1)} %get-tuple-element.48), channel_id=1, source_target_pairs={{0,8},{1,9},{2,10},{3,11},{4,12},{5,13},{6,14},{7,15},{8,0},{9,1},... | collective-permute-start | bytes 2359304 | tf_op jit(solution)/shard_map/ppermute | solution.py:422
  38.4 7.6 %shard_map.97 = (bf16[512,512]{1,0:T(8,128)(2,1)}, bf16[512,512]{1,0:T(8,128)(2,1)}, f32[512,512]{1,0:T(8,128)}, bf16[512,512]{1,0:T(8,128)(2,1)}, bf16[512,512]...) custom-call(f32[4,512]{1,0:T(4,128)} %bitcast.7, ...), custom_call_target="tpu_custom_call" | custom-call | flops 60000002048 | bytes 10000000 | tf_op jit(solution)/shard_map/pallas_call | solution.py:383
  46.0 2.5 %all-to-all-done.1 = bf16[32,32,128]{2,1,0:T(8,128)(2,1)S(1)} async-done(((bf16[32,32,128]{2,1,0:T(8,128)(2,1)}), bf16[32,32,128]{2,1,0:T(8,128)(2,1)S(1)}, u32[]{:S(2)}, u32[]{:S(2)}) %all-to-all-start.1) | async-done | bytes 262176 | tf_op jit(solution)/shard_map/all_to_all | solution.py:418
  49.2 3.3 %shard_map.98 = (bf16[512,512]{1,0:T(8,128)(2,1)}, bf16[512,512]{1,0:T(8,128)(2,1)}) custom-call(bf16[1024,128]{1,0:T(8,128)(2,1)} %bitcast.4, bf16[512,512]{1,0:T(8,128)(2,1)} %get-tuple-element.53.wo_hbm, bf16[512,512]{1,0:T(8,128)(2,1)} %get-tuple-element.54.gq_hbm, bf16[512,512]{1,0:T(8,128)(2,1)} %get-tuple-element.55.sq_hbm, ...), custom_call_target="tpu_custom_call" | custom-call | flops 1000000000 | bytes 4000000 | tf_op jit(solution)/shard_map/pallas_call | solution.py:427
  52.6 1.6 %collective-permute-start.3 = (bf16[512,512]{1,0:T(8,128)(2,1)}, bf16[512,512]{1,0:T(8,128)(2,1)S(1)}, u32[]{:S(2)}, u32[]{:S(2)}) collective-permute-start(bf16[512,512]{1,0:T(8,128)(2,1)} %get-tuple-element.59.slopes0_ref), channel_id=1, source_target_pairs={{0,1},{1,0},{2,3},{3,2},{4,5},{5,4},{6,7},{7,6},{8,9},{9,8},{10,11... | collective-permute-start | bytes 1572872 | tf_op jit(solution)/shard_map/ppermute | solution.py:422
  54.2 1.1 %copy-done.2 = bf16[512,512]{1,0:T(8,128)(2,1)S(1)} copy-done((bf16[512,512]{1,0:T(8,128)(2,1)S(1)}, bf16[512,512]{1,0:T(8,128)(2,1)}, u32[]{:S(2)}) %copy-start.2) | copy-done | bytes 524312
  55.2 1.0 %copy-done.3 = bf16[512,512]{1,0:T(8,128)(2,1)S(1)} copy-done((bf16[512,512]{1,0:T(8,128)(2,1)S(1)}, bf16[512,512]{1,0:T(8,128)(2,1)}, u32[]{:S(2)}) %copy-start.3) | copy-done | bytes 524312
  56.3 2.2 %shard_map.99 = (f32[1536,512]{1,0:T(8,128)S(1)}, f32[1536,512]{1,0:T(8,128)S(1)}) custom-call(bf16[1536,512]{1,0:T(8,128)(2,1)S(1)} %copy-done.4, bf16[1536,512]{1,0:T(8,128)(2,1)S(1)} %copy-done.5, bf16[512,512]{1,0:T(8,128)(2,1)S(1)} %copy-done.2, bf16[512,512]{1,0:T(8,128)(2,1)S(1)} %copy-done.3), custom_call_target="tpu_custom_call" | custom-call | flops 1610612736 | bytes 10000000 | tf_op jit(solution)/shard_map/pallas_call | solution.py:436
  58.5 3.5 %collective-permute-done.6.slopes_ref = bf16[512,512]{1,0:T(8,128)(2,1)S(1)} collective-permute-done((bf16[512,512]{1,0:T(8,128)(2,1)}, bf16[512,512]{1,0:T(8,128)(2,1)S(1)}, u32[]{:S(2)}, u32[]{:S(2)}) %collective-permute-start.6) | collective-permute-done | bytes 524320 | tf_op jit(solution)/shard_map/ppermute | solution.py:422
  62.5 1.1 %collective-permute-start.9 = (bf16[768,512]{1,0:T(8,128)(2,1)S(1)}, bf16[768,512]{1,0:T(8,128)(2,1)S(1)}, u32[]{:S(2)}, u32[]{:S(2)}) collective-permute-start(bf16[768,512]{1,0:T(8,128)(2,1)S(1)} %shard_map.101), channel_id=1, source_target_pairs={{0,1},{1,0},{2,3},{3,2},{4,5},{5,4},{6,7},{7,6},{8,9},{9,8},{10,11... | collective-permute-start | bytes 2359304 | tf_op jit(solution)/shard_map/ppermute | solution.py:422
  64.1 0.7 collective-permute-start.4
  65.4 9.1 %collective-permute-done.9.received_ref = bf16[768,512]{1,0:T(8,128)(2,1)S(1)} collective-permute-done((bf16[768,512]{1,0:T(8,128)(2,1)S(1)}, bf16[768,512]{1,0:T(8,128)(2,1)S(1)}, u32[]{:S(2)}, u32[]{:S(2)}) %collective-permute-start.9) | collective-permute-done | bytes 786464 | tf_op jit(solution)/shard_map/ppermute | solution.py:422
  76.3 1.6 %collective-permute-start.7 = (bf16[384,512]{1,0:T(8,128)(2,1)S(1)}, bf16[384,512]{1,0:T(8,128)(2,1)S(1)}, u32[]{:S(2)}, u32[]{:S(2)}) collective-permute-start(bf16[384,512]{1,0:T(8,128)(2,1)S(1)} %get-tuple-element.66), channel_id=1, source_target_pairs={{0,24},{1,25},{2,26},{3,27},{4,28},{5,29},{6,30},{7,31},{8,16},{9,... | collective-permute-start | bytes 1179656 | tf_op jit(solution)/shard_map/ppermute | solution.py:422
  78.0 5.9 %collective-permute-done.10.received_ref = bf16[384,512]{1,0:T(8,128)(2,1)S(1)} collective-permute-done((bf16[384,512]{1,0:T(8,128)(2,1)S(1)}, bf16[384,512]{1,0:T(8,128)(2,1)S(1)}, u32[]{:S(2)}, u32[]{:S(2)}) %collective-permute-start.10) | collective-permute-done | bytes 393248 | tf_op jit(solution)/shard_map/ppermute | solution.py:422
  83.9 0.9 collective-permute-start.11
  85.5 2.5 %collective-permute-start.8 = (bf16[192,512]{1,0:T(8,128)(2,1)S(1)}, bf16[192,512]{1,0:T(8,128)(2,1)S(1)}, u32[]{:S(2)}, u32[]{:S(2)}) collective-permute-start(bf16[192,512]{1,0:T(8,128)(2,1)S(1)} %get-tuple-element.68), channel_id=1, source_target_pairs={{0,7},{1,2},{2,1},{3,4},{4,3},{5,6},{6,5},{7,0},{8,15},{9,10},{10,... | collective-permute-start | bytes 589832 | tf_op jit(solution)/shard_map/ppermute | solution.py:422
  88.1 2.8 %collective-permute-done.11.received_ref = bf16[192,512]{1,0:T(8,128)(2,1)S(1)} collective-permute-done((bf16[192,512]{1,0:T(8,128)(2,1)S(1)}, bf16[192,512]{1,0:T(8,128)(2,1)S(1)}, u32[]{:S(2)}, u32[]{:S(2)}) %collective-permute-start.11) | collective-permute-done | bytes 196640 | tf_op jit(solution)/shard_map/ppermute | solution.py:422
  91.0 0.8 collective-permute-start.14
  92.5 2.5 %collective-permute-start.13 = (bf16[96,512]{1,0:T(8,128)(2,1)S(1)}, bf16[96,512]{1,0:T(8,128)(2,1)S(1)}, u32[]{:S(2)}, u32[]{:S(2)}) collective-permute-start(bf16[96,512]{1,0:T(8,128)(2,1)S(1)} %get-tuple-element.78), channel_id=1, source_target_pairs={{0,3},{1,6},{2,5},{3,0},{4,7},{5,2},{6,1},{7,4},{8,11},{9,14},{10,... | collective-permute-start | bytes 294920 | tf_op jit(solution)/shard_map/ppermute | solution.py:422
  95.1 1.1 %shard_map.111 = bf16[512,512]{1,0:T(8,128)(2,1)} custom-call(f32[512,512]{1,0:T(8,128)S(1)} %copy-done.6, bf16[512,512]{1,0:T(8,128)(2,1)S(1)} %copy-done.7, bf16[1024,128]{1,0:T(8,128)(2,1)S(1)} %bitcast.5), custom_call_target="tpu_custom_call" | custom-call | flops 1000000000 | bytes 5000000 | tf_op jit(solution)/shard_map/pallas_call | solution.py:495
  96.2 2.7 %collective-permute-done.14.received_ref = bf16[96,512]{1,0:T(8,128)(2,1)S(1)} collective-permute-done((bf16[96,512]{1,0:T(8,128)(2,1)S(1)}, bf16[96,512]{1,0:T(8,128)(2,1)S(1)}, u32[]{:S(2)}, u32[]{:S(2)}) %collective-permute-start.14) | collective-permute-done | bytes 98336 | tf_op jit(solution)/shard_map/ppermute | solution.py:422
  99.6 3.0 %collective-permute-done.13 = bf16[96,512]{1,0:T(8,128)(2,1)S(1)} collective-permute-done((bf16[96,512]{1,0:T(8,128)(2,1)S(1)}, bf16[96,512]{1,0:T(8,128)(2,1)S(1)}, u32[]{:S(2)}, u32[]{:S(2)}) %collective-permute-start.13) | collective-permute-done | bytes 98336 | tf_op jit(solution)/shard_map/ppermute | solution.py:422
  102.6 0.7 convert_add_fusion
  (39 shorter events, 6.6 us)
Async XLA Ops:
  4.3 25.1 %all-to-all-start = ((bf16[32,40,128]{2,1,0:T(8,128)(2,1)}), bf16[32,40,128]{2,1,0:T(8,128)(2,1)S(1)}, u32[]{:S(2)}, u32[]{:S(2)}) async-start(bf16[32,40,128]{2,1,0:T(8,128)(2,1)} %shard_map.94), calls=%async_computation | async-start | bytes 655360 | tf_op jit(solution)/shard_map/all_to_all | solution.py:381
  21.8 41.8 %collective-permute-start.2 = (bf16[768,512]{1,0:T(8,128)(2,1)}, bf16[768,512]{1,0:T(8,128)(2,1)S(1)}, u32[]{:S(2)}, u32[]{:S(2)}) collective-permute-start(bf16[768,512]{1,0:T(8,128)(2,1)} %get-tuple-element.62), channel_id=1, source_target_pairs={{0,1},{1,0},{2,3},{3,2},{4,5},{5,4},{6,7},{7,6},{8,9},{9,8},{10,11... | collective-permute-start | bytes 2359304 | tf_op jit(solution)/shard_map/ppermute | solution.py:422
  23.6 34.8 %collective-permute-start.5 = (bf16[768,512]{1,0:T(8,128)(2,1)}, bf16[768,512]{1,0:T(8,128)(2,1)S(1)}, u32[]{:S(2)}, u32[]{:S(2)}) collective-permute-start(bf16[768,512]{1,0:T(8,128)(2,1)} %get-tuple-element.65), channel_id=1, source_target_pairs={{0,8},{1,9},{2,10},{3,11},{4,12},{5,13},{6,14},{7,15},{8,0},{9,1},... | collective-permute-start | bytes 2359304 | tf_op jit(solution)/shard_map/ppermute | solution.py:422
  30.3 18.2 %all-to-all-start.1 = ((bf16[32,32,128]{2,1,0:T(8,128)(2,1)}), bf16[32,32,128]{2,1,0:T(8,128)(2,1)S(1)}, u32[]{:S(2)}, u32[]{:S(2)}) async-start(bf16[32,32,128]{2,1,0:T(8,128)(2,1)} %shard_map.96), calls=%async_computation.1 | async-start | bytes 524288 | tf_op jit(solution)/shard_map/all_to_all | solution.py:418
  35.1 17.5 %collective-permute-start = (bf16[768,512]{1,0:T(8,128)(2,1)}, bf16[768,512]{1,0:T(8,128)(2,1)S(1)}, u32[]{:S(2)}, u32[]{:S(2)}) collective-permute-start(bf16[768,512]{1,0:T(8,128)(2,1)} %get-tuple-element.47), channel_id=1, source_target_pairs={{0,1},{1,0},{2,3},{3,2},{4,5},{5,4},{6,7},{7,6},{8,9},{9,8},{10,11... | collective-permute-start | bytes 2359304 | tf_op jit(solution)/shard_map/ppermute | solution.py:422
  37.0 17.2 %collective-permute-start.1 = (bf16[768,512]{1,0:T(8,128)(2,1)}, bf16[768,512]{1,0:T(8,128)(2,1)S(1)}, u32[]{:S(2)}, u32[]{:S(2)}) collective-permute-start(bf16[768,512]{1,0:T(8,128)(2,1)} %get-tuple-element.48), channel_id=1, source_target_pairs={{0,8},{1,9},{2,10},{3,11},{4,12},{5,13},{6,14},{7,15},{8,0},{9,1},... | collective-permute-start | bytes 2359304 | tf_op jit(solution)/shard_map/ppermute | solution.py:422
  48.5 0.7 copy-start
  49.1 5.0 %copy-start.4 = (bf16[1536,512]{1,0:T(8,128)(2,1)S(1)}, bf16[1536,512]{1,0:T(8,128)(2,1)}, u32[]{:S(2)}) copy-start(bf16[1536,512]{1,0:T(8,128)(2,1)} %get-tuple-element.50.rows0_hbm) | copy-start | bytes 4718596
  49.1 5.0 %copy-start.5 = (bf16[1536,512]{1,0:T(8,128)(2,1)S(1)}, bf16[1536,512]{1,0:T(8,128)(2,1)}, u32[]{:S(2)}) copy-start(bf16[1536,512]{1,0:T(8,128)(2,1)} %get-tuple-element.51.rows1_hbm) | copy-start | bytes 4718596
  52.4 9.5 %collective-permute-start.6 = (bf16[512,512]{1,0:T(8,128)(2,1)}, bf16[512,512]{1,0:T(8,128)(2,1)S(1)}, u32[]{:S(2)}, u32[]{:S(2)}) collective-permute-start(bf16[512,512]{1,0:T(8,128)(2,1)} %get-tuple-element.60.slopes1_ref), channel_id=1, source_target_pairs={{0,8},{1,9},{2,10},{3,11},{4,12},{5,13},{6,14},{7,15},{8,0},{9,1},... | collective-permute-start | bytes 1572872 | tf_op jit(solution)/shard_map/ppermute | solution.py:422
  52.6 11.0 %collective-permute-start.3 = (bf16[512,512]{1,0:T(8,128)(2,1)}, bf16[512,512]{1,0:T(8,128)(2,1)S(1)}, u32[]{:S(2)}, u32[]{:S(2)}) collective-permute-start(bf16[512,512]{1,0:T(8,128)(2,1)} %get-tuple-element.59.slopes0_ref), channel_id=1, source_target_pairs={{0,1},{1,0},{2,3},{3,2},{4,5},{5,4},{6,7},{7,6},{8,9},{9,8},{10,11... | collective-permute-start | bytes 1572872 | tf_op jit(solution)/shard_map/ppermute | solution.py:422
  54.2 1.1 %copy-start.2 = (bf16[512,512]{1,0:T(8,128)(2,1)S(1)}, bf16[512,512]{1,0:T(8,128)(2,1)}, u32[]{:S(2)}) copy-start(bf16[512,512]{1,0:T(8,128)(2,1)} %get-tuple-element.59.slopes0_ref) | copy-start | bytes 1572868
  55.2 1.0 %copy-start.3 = (bf16[512,512]{1,0:T(8,128)(2,1)S(1)}, bf16[512,512]{1,0:T(8,128)(2,1)}, u32[]{:S(2)}) copy-start(bf16[512,512]{1,0:T(8,128)(2,1)} %get-tuple-element.60.slopes1_ref) | copy-start | bytes 1572868
  62.5 12.1 %collective-permute-start.9 = (bf16[768,512]{1,0:T(8,128)(2,1)S(1)}, bf16[768,512]{1,0:T(8,128)(2,1)S(1)}, u32[]{:S(2)}, u32[]{:S(2)}) collective-permute-start(bf16[768,512]{1,0:T(8,128)(2,1)S(1)} %shard_map.101), channel_id=1, source_target_pairs={{0,1},{1,0},{2,3},{3,2},{4,5},{5,4},{6,7},{7,6},{8,9},{9,8},{10,11... | collective-permute-start | bytes 2359304 | tf_op jit(solution)/shard_map/ppermute | solution.py:422
  64.1 12.1 %collective-permute-start.4 = (bf16[768,512]{1,0:T(8,128)(2,1)S(1)}, bf16[768,512]{1,0:T(8,128)(2,1)S(1)}, u32[]{:S(2)}, u32[]{:S(2)}) collective-permute-start(bf16[768,512]{1,0:T(8,128)(2,1)S(1)} %shard_map.100), channel_id=1, source_target_pairs={{0,8},{1,9},{2,10},{3,11},{4,12},{5,13},{6,14},{7,15},{8,0},{9,1},... | collective-permute-start | bytes 2359304 | tf_op jit(solution)/shard_map/ppermute | solution.py:422
  74.8 9.1 %collective-permute-start.10 = (bf16[384,512]{1,0:T(8,128)(2,1)S(1)}, bf16[384,512]{1,0:T(8,128)(2,1)S(1)}, u32[]{:S(2)}, u32[]{:S(2)}) collective-permute-start(bf16[384,512]{1,0:T(8,128)(2,1)S(1)} %get-tuple-element.73), channel_id=1, source_target_pairs={{0,7},{1,2},{2,1},{3,4},{4,3},{5,6},{6,5},{7,0},{8,15},{9,10},{10,... | collective-permute-start | bytes 1179656 | tf_op jit(solution)/shard_map/ppermute | solution.py:422
  76.3 9.1 %collective-permute-start.7 = (bf16[384,512]{1,0:T(8,128)(2,1)S(1)}, bf16[384,512]{1,0:T(8,128)(2,1)S(1)}, u32[]{:S(2)}, u32[]{:S(2)}) collective-permute-start(bf16[384,512]{1,0:T(8,128)(2,1)S(1)} %get-tuple-element.66), channel_id=1, source_target_pairs={{0,24},{1,25},{2,26},{3,27},{4,28},{5,29},{6,30},{7,31},{8,16},{9,... | collective-permute-start | bytes 1179656 | tf_op jit(solution)/shard_map/ppermute | solution.py:422
  83.8 11.2 %copy-start.1 = (bf16[32,32,128]{2,1,0:T(8,128)(2,1)S(1)}, bf16[32,32,128]{2,1,0:T(8,128)(2,1)}, u32[]{:S(2)}) copy-start(bf16[32,32,128]{2,1,0:T(8,128)(2,1)} %copy-done) | copy-start | bytes 786436
  83.8 11.3 %copy-start.6 = (f32[512,512]{1,0:T(8,128)S(1)}, f32[512,512]{1,0:T(8,128)}, u32[]{:S(2)}) copy-start(f32[512,512]{1,0:T(8,128)} %get-tuple-element.81.local_ref) | copy-start | bytes 3145732
  83.8 11.3 %copy-start.7 = (bf16[512,512]{1,0:T(8,128)(2,1)S(1)}, bf16[512,512]{1,0:T(8,128)(2,1)}, u32[]{:S(2)}) copy-start(bf16[512,512]{1,0:T(8,128)(2,1)} %get-tuple-element.82.weighted_ref) | copy-start | bytes 1572868
  83.9 7.0 %collective-permute-start.11 = (bf16[192,512]{1,0:T(8,128)(2,1)S(1)}, bf16[192,512]{1,0:T(8,128)(2,1)S(1)}, u32[]{:S(2)}, u32[]{:S(2)}) collective-permute-start(bf16[192,512]{1,0:T(8,128)(2,1)S(1)} %get-tuple-element.75), channel_id=1, source_target_pairs={{0,24},{1,25},{2,26},{3,27},{4,28},{5,29},{6,30},{7,31},{8,16},{9,... | collective-permute-start | bytes 589832 | tf_op jit(solution)/shard_map/ppermute | solution.py:422
  85.5 7.0 %collective-permute-start.8 = (bf16[192,512]{1,0:T(8,128)(2,1)S(1)}, bf16[192,512]{1,0:T(8,128)(2,1)S(1)}, u32[]{:S(2)}, u32[]{:S(2)}) collective-permute-start(bf16[192,512]{1,0:T(8,128)(2,1)S(1)} %get-tuple-element.68), channel_id=1, source_target_pairs={{0,7},{1,2},{2,1},{3,4},{4,3},{5,6},{6,5},{7,0},{8,15},{9,10},{10,... | collective-permute-start | bytes 589832 | tf_op jit(solution)/shard_map/ppermute | solution.py:422
  90.9 1.6 %collective-permute-start.12 = (bf16[16,128]{1,0:T(8,128)(2,1)S(1)}, bf16[16,128]{1,0:T(8,128)(2,1)S(1)}, u32[]{:S(2)}, u32[]{:S(2)}) collective-permute-start(bf16[16,128]{1,0:T(8,128)(2,1)S(1)} %slice.7), channel_id=1, source_target_pairs={{0,32},{1,33},{2,34},{3,35},{4,36},{5,37},{6,38},{7,39},{8,40},{9,... | collective-permute-start | bytes 12296 | tf_op jit(solution)/shard_map/ppermute | solution.py:485
  91.0 7.9 %collective-permute-start.14 = (bf16[96,512]{1,0:T(8,128)(2,1)S(1)}, bf16[96,512]{1,0:T(8,128)(2,1)S(1)}, u32[]{:S(2)}, u32[]{:S(2)}) collective-permute-start(bf16[96,512]{1,0:T(8,128)(2,1)S(1)} %get-tuple-element.77), channel_id=1, source_target_pairs={{0,3},{1,6},{2,5},{3,0},{4,7},{5,2},{6,1},{7,4},{8,11},{9,14},{10,... | collective-permute-start | bytes 294920 | tf_op jit(solution)/shard_map/ppermute | solution.py:422
  92.5 10.1 %collective-permute-start.13 = (bf16[96,512]{1,0:T(8,128)(2,1)S(1)}, bf16[96,512]{1,0:T(8,128)(2,1)S(1)}, u32[]{:S(2)}, u32[]{:S(2)}) collective-permute-start(bf16[96,512]{1,0:T(8,128)(2,1)S(1)} %get-tuple-element.78), channel_id=1, source_target_pairs={{0,3},{1,6},{2,5},{3,0},{4,7},{5,2},{6,1},{7,4},{8,11},{9,14},{10,... | collective-permute-start | bytes 294920 | tf_op jit(solution)/shard_map/ppermute | solution.py:422
